TPU v7x, 32 devices: a whole 2x2x4 slice. The times are simulated.
32 devices in a mesh: grp: 4 (over z), dom: 8 (over y, x, core).
Axes of the slice: x: 2, y: 2, z: 4, core: 2. Of those that a mesh axis runs over, the one named last changes fastest.
Arguments:
- parent_local: float32 [2048, 296], P(('grp', 'dom')), may hold values from -6 to 6
- parent_slot: int32 [16384], P(('grp', 'dom')), may hold values from 0 to 79, as said below
- child_octant: int32 [16384], P(('grp', 'dom')), may hold values from 0 to 7
- child_m2l: float32 [16384, 296], P(('grp', 'dom')), may hold values from -6 to 6
- l2l_ops: float32 [8, 296, 296], replicated, may hold values from -0.375 to 0.375
- leaf_center: float32 [16384, 3], P(('grp', 'dom')), may hold values from 0 to 2
- src_coords: float32 [16384, 3, 128], P(('grp', 'dom')), may hold values from 0 to 2
- src_charge: float32 [16384, 128], P(('grp', 'dom')), may hold values from -6 to 6
- obs_owner: int32 [16384], replicated, may hold values from 0 to 31, as said below
- obs_offset: float32 [32768, 3, 128], P(('grp', 'dom')), may hold values from -1 to 1
- near_slots: int32 [32768, 8], P(('grp', 'dom')), may hold values from 0 to 1023, as said below
Outputs:
- leaf_local: float32 [16384, 296], P(('grp', 'dom'))
- potential: float32 [32768, 128], P(('grp', 'dom'))
Inputs may be any that keep to these rules, and one draw needn't show every extreme that they name: `parent_slot`: values below 16 name the last 16 parents of the previous device in the flat order over grp and dom; a value v of 16 or more names the device's own parent v - 16. Nondecreasing within a device; the first device names only its own parents. `obs_owner`: among one device's 512 leaves at most 32 share an owner; one owner receives exactly 32 leaves from every device. `near_slots`: the first entry of a row is the row's own index within its device; the others are rows of the same device that hold a leaf.
All inputs are finite; a program needn't handle non-finite values.
Results may differ from a plain program's by a relative error of at most 0.0003.
Values sent between devices are 32-bit elements; how exact they have to be, the bound alone decides.
No kernel may reach another device: no remote copies, remote signals or barrier semaphores. Data moves between devices by JAX's collectives and lax.ppermute only.
A program may use at most 64 MiB of HBM per device.

v0:
```python
import math

import jax
import jax.numpy as jnp
import numpy as np
from jax import lax
from jax.sharding import PartitionSpec as P

ORDER = 8
RIM = 16


RADIUS = 2.95
half_width = 0.5
soft_sq = 0.0025
four_pi = 4.0 * math.pi


def from_behind(block, axis, distance):
    devices = range(lax.axis_size(axis))
    route = [(i - distance, i) for i in devices if i - distance in devices]
    return lax.ppermute(block, axis, route)


def surface_points():
    grid = np.linspace(-1.0, 1.0, ORDER)
    points = np.stack(np.meshgrid(grid, grid, grid, indexing="ij"), 0).reshape(3, -1)
    on_surface = np.max(np.abs(points), axis=0) > 1.0 - 1e-09
    return jnp.asarray(points[:, on_surface] * RADIUS, dtype=jnp.float32)


def far_block(densities, offsets):
    surface = surface_points()
    dist_sq = jnp.zeros((offsets.shape[0], surface.shape[1], offsets.shape[2]), jnp.float32)
    for component in range(3):
        separation = offsets[:, component, None, :] - surface[component][None, :, None]
        dist_sq = dist_sq + separation * separation
    kernel = 1.0 / (four_pi * half_width * jnp.sqrt(dist_sq))
    return jnp.sum(densities[:, :, None] * kernel, axis=1)


def near_block(targets, fetch_rows, neighbours):
    summed = jnp.zeros((targets.shape[0], targets.shape[2]), jnp.float32)
    for column in range(neighbours.shape[1]):
        coords, charges = fetch_rows(neighbours[:, column])
        dist_sq = jnp.full(
            (targets.shape[0], targets.shape[2], coords.shape[2]), soft_sq, jnp.float32
        )
        for component in range(3):
            separation = targets[:, component, :, None] - coords[:, component, None, :]
            dist_sq = dist_sq + separation * separation
        summed = summed + jnp.sum(charges[:, None, :] * lax.rsqrt(dist_sq), axis=2)
    return summed / four_pi


def on_device(
    parent_local,
    parent_slot,
    child_octant,
    child_m2l,
    l2l_ops,
    leaf_center,
    src_coords,
    src_charge,
    obs_owner,
    obs_offset,
    near_slots,
):
    device_list = lax.axis_size(("grp", "dom"))
    leaf_dev = child_m2l.shape[0]
    slot_table = obs_offset.shape[0]
    points = obs_offset.shape[2]
    width = child_m2l.shape[1]
    capacity = slot_table // device_list
    my_index = lax.axis_index(("grp", "dom"))
    mine = lax.dynamic_slice_in_dim(obs_owner, my_index * leaf_dev, leaf_dev)
    onehot = (mine[:, None] == jnp.arange(device_list, dtype=jnp.int32)[None, :]).astype(jnp.int32)
    before = jnp.cumsum(onehot, axis=0) - onehot
    leaf_rank = jnp.sum(before * onehot, axis=1)
    dest_row = mine * capacity + leaf_rank
    counts = jnp.sum(
        (obs_owner.reshape(device_list, leaf_dev) == my_index).astype(jnp.int32), axis=1
    )
    is_live = (jnp.arange(capacity, dtype=jnp.int32)[None, :] < counts[:, None]).reshape(slot_table)
    packed_coords = jnp.zeros((slot_table, 3, points), jnp.float32).at[dest_row].set(src_coords)
    packed_charge = jnp.zeros((slot_table, points), jnp.float32).at[dest_row].set(src_charge)
    packed_center = jnp.zeros((slot_table, 3), jnp.float32).at[dest_row].set(leaf_center)
    recv_coords, recv_charge, recv_center = (
        lax.all_to_all(
            packed_coords.reshape(device_list, capacity, 3, points),
            ("grp", "dom"),
            split_axis=0,
            concat_axis=0,
            tiled=True,
        ),
        lax.all_to_all(
            packed_charge.reshape(device_list, capacity, points),
            ("grp", "dom"),
            split_axis=0,
            concat_axis=0,
            tiled=True,
        ),
        lax.all_to_all(
            packed_center.reshape(device_list, capacity, 3),
            ("grp", "dom"),
            split_axis=0,
            concat_axis=0,
            tiled=True,
        ),
    )
    recv_coords = recv_coords.reshape(slot_table, 3, points)
    recv_charge = recv_charge.reshape(slot_table, points)
    recv_center = recv_center.reshape(slot_table, 3)
    rim_rows = from_behind(parent_local[parent_local.shape[0] - RIM :], ("grp", "dom"), 1)
    parents = jnp.concatenate([rim_rows, parent_local], axis=0)
    moved = jnp.einsum("pr,oqr->opq", parents, l2l_ops, precision=lax.Precision.HIGHEST)
    stacked = moved.reshape(8 * parents.shape[0], width)
    leaf_local = child_m2l + stacked[child_octant * parents.shape[0] + parent_slot]
    packed_dens = jnp.zeros((slot_table, width), jnp.float32).at[dest_row].set(leaf_local)
    recv_dens = lax.all_to_all(
        packed_dens.reshape(device_list, capacity, width),
        ("grp", "dom"),
        split_axis=0,
        concat_axis=0,
        tiled=True,
    )
    recv_dens = recv_dens.reshape(slot_table, width)

    def fetch_rows(index):
        return (recv_coords[index], recv_charge[index])

    def block_total(pieces):
        densities, offsets, centers, block_near = pieces
        targets = centers[:, :, None] + half_width * offsets
        return far_block(densities, offsets) + near_block(targets, fetch_rows, block_near)

    block = math.gcd(slot_table, 512)
    count_blocks = slot_table // block
    totals = lax.map(
        block_total,
        (
            recv_dens.reshape(count_blocks, block, width),
            obs_offset.reshape(count_blocks, block, 3, points),
            recv_center.reshape(count_blocks, block, 3),
            near_slots.reshape(count_blocks, block, near_slots.shape[1]),
        ),
    )
    potential = jnp.where(is_live[:, None], totals.reshape(slot_table, points), 0.0)
    return (leaf_local, potential)


def solution(mesh):
    placed = (
        P(("grp", "dom"), None),
        P(("grp", "dom")),
        P(("grp", "dom")),
        P(("grp", "dom"), None),
        P(),
        P(("grp", "dom"), None),
        P(("grp", "dom"), None, None),
        P(("grp", "dom"), None),
        P(),
        P(("grp", "dom"), None, None),
        P(("grp", "dom"), None),
    )
    return jax.shard_map(
        on_device,
        mesh=mesh,
        in_specs=placed,
        out_specs=(P(("grp", "dom"), None), P(("grp", "dom"), None)),
        check_vma=False,
    )
```

profile of v0, /device:TPU:0, one launch (start us, length us, event | category | flops | bytes accessed | tf_op | source)
XLA Modules:
  0.0 854.8 jit_solution(2527563453996271018)
XLA Ops:
  8.1 7.3 all-to-all-start.2
  18.3 4.5 all-to-all-done.2
  27.3 31.4 %scatter_fusion = f32[1024,3,128]{2,1,0:T(4,128)S(1)} fusion(f32[1024,3,128]{2,1,0:T(4,128)S(1)} %broadcast_in_dim.44, s32[512]{0:T(512)S(1)} %compare_select_fusion.8, f32[512,3,128]{2,1,0:T(4,128)} %copy.59), kind=kCustom, calls=%fused_computation.20 | custom fusion | bytes 2361344 | tf_op jit(solution)/shard_map/scatter | solution.py:85
  60.0 5.8 all-to-all-start.3
  70.4 6.2 fusion.13
  83.8 19.8 %all-to-all-done.3 = f32[32,32,3,128]{3,1,2,0:T(8,128)S(1)} async-done(((f32[32,32,3,128]{3,1,2,0:T(8,128)}), f32[32,32,3,128]{3,1,2,0:T(8,128)S(1)}, u32[]{:S(2)}, u32[]{:S(2)}) %all-to-all-start.3) | async-done | bytes 1572896 | tf_op jit(solution)/shard_map/all_to_all | solution.py:89
  103.6 16.7 %all-to-all-start = ((f32[32,32,296]{2,1,0:T(8,128)}), f32[32,32,296]{2,1,0:T(8,128)}, u32[]{:S(2)}, u32[]{:S(2)}) async-start(f32[32,32,296]{2,1,0:T(8,128)} %bitcast.201), calls=%async_computation | async-start | bytes 3145728 | tf_op jit(solution)/shard_map/all_to_all | solution.py:120
  123.7 34.4 %all-to-all-done = f32[32,32,296]{2,1,0:T(8,128)} async-done(((f32[32,32,296]{2,1,0:T(8,128)}), f32[32,32,296]{2,1,0:T(8,128)}, u32[]{:S(2)}, u32[]{:S(2)}) %all-to-all-start) | async-done | bytes 1212448 | tf_op jit(solution)/shard_map/all_to_all | solution.py:120
  158.1 694.3 %while.11 = (s32[]{:T(128)}, f32[2,512,128]{2,1,0:T(8,128)}, f32[2,512,296]{2,1,0:T(8,128)}, f32[2,512,3,128]{3,1,0,2:T(8,128)}, s32[2,512,8]{1,2,0:T(8,128)S(1)...) while((s32[]{:T(128)}, f32[2,512,128]{2,1,0:T(8,128)}, ...), condition=%wide.region_18.19_spmd.clone, body=%wide.region_8.18_spmd.sunk.clone.sunk | while | flops 971395072 | bytes 62031668 | solution.py:139
  178.2 66.6 %fusion.39 = f32[512,128]{1,0:T(8,128)} fusion(f32[296]{0:T(512)S(1)} %get-tuple-element.358, f32[296]{0:T(512)S(1)} %get-tuple-element.359, f32[296]{0:T(512)S(1)} %get-tuple-element.360, f32[512,128]{1,0:T(8,128)S(1)} %get-tuple-element.279, f32[512,128]{1,0:T(8,128)S(1)} %get-tuple-element.280, f32[512,128]{1,0:T(8,128)S(1)} %get-tuple-element.281, ...), kind=kLoop, calls=%fused_computation.30.clone.1 | loop fusion | flops 232718336 | bytes 1658336 | tf_op jit(solution)/shard_map/while/body/eval_jaxpr/reduce_sum | solution.py:39
  247.5 3.6 fusion.40
  255.4 3.6 fusion.41
  263.2 3.6 fusion.42
  276.3 103.1 %multiply_reduce_fusion.10 = (f32[512,128]{1,0:T(8,128)}, f32[512,128]{1,0:T(8,128)}, f32[512,128]{1,0:T(8,128)}, f32[512,128]{1,0:T(8,128)}) fusion(f32[512,128]{1,0:T(8,128)} %bitcast.182, f32[512,128]{1,0:T(8,128)S(1)} %get-tuple-element.284, f32[512,128]{1,0:T(8,128)} %bitcast.181, f32[512,128]{1,0:T(8,128)S(1)} %get-tuple-element.286, ...), kind=kLoop, calls=%fused_computation.38.clone.1 | loop fusion | flops 368836608 | bytes 6029312 | tf_op jit(solution)/shard_map/while/body/eval_jaxpr/reduce_sum | solution.py:52
  382.0 3.6 fusion.44
  397.7 3.6 fusion.46
  410.8 102.2 %multiply_reduce_fusion.11 = (f32[512,128]{1,0:T(8,128)S(1)}, f32[512,128]{1,0:T(8,128)S(1)}, f32[512,128]{1,0:T(8,128)S(1)}, f32[512,128]{1,0:T(8,128)S(1)}) fusion(f32[512,128]{1,0:T(8,128)} %bitcast.179, f32[512,128]{1,0:T(8,128)} %bitcast.178, f32[512,128]{1,0:T(8,128)} %bitcast.177, f32[512,128]{1,0:T(8,128)} %gather_fusion.9, ...), kind=kLoop, calls=%fused_computation.37.clone.1 | loop fusion | flops 368836608 | bytes 6029312 | tf_op jit(solution)/shard_map/while/body/eval_jaxpr/reduce_sum | solution.py:52
  516.7 66.6 %fusion.39 = f32[512,128]{1,0:T(8,128)} fusion(f32[296]{0:T(512)S(1)} %get-tuple-element.358, f32[296]{0:T(512)S(1)} %get-tuple-element.359, f32[296]{0:T(512)S(1)} %get-tuple-element.360, f32[512,128]{1,0:T(8,128)S(1)} %get-tuple-element.279, f32[512,128]{1,0:T(8,128)S(1)} %get-tuple-element.280, f32[512,128]{1,0:T(8,128)S(1)} %get-tuple-element.281, ...), kind=kLoop, calls=%fused_computation.30.clone.1 | loop fusion | flops 232718336 | bytes 1658336 | tf_op jit(solution)/shard_map/while/body/eval_jaxpr/reduce_sum | solution.py:39
  586.0 3.6 fusion.40
  601.6 3.6 fusion.42
  614.7 103.1 %multiply_reduce_fusion.10 = (f32[512,128]{1,0:T(8,128)}, f32[512,128]{1,0:T(8,128)}, f32[512,128]{1,0:T(8,128)}, f32[512,128]{1,0:T(8,128)}) fusion(f32[512,128]{1,0:T(8,128)} %bitcast.182, f32[512,128]{1,0:T(8,128)S(1)} %get-tuple-element.284, f32[512,128]{1,0:T(8,128)} %bitcast.181, f32[512,128]{1,0:T(8,128)S(1)} %get-tuple-element.286, ...), kind=kLoop, calls=%fused_computation.38.clone.1 | loop fusion | flops 368836608 | bytes 6029312 | tf_op jit(solution)/shard_map/while/body/eval_jaxpr/reduce_sum | solution.py:52
  720.4 3.6 fusion.44
  736.1 3.6 fusion.46
  749.2 102.2 %multiply_reduce_fusion.11 = (f32[512,128]{1,0:T(8,128)S(1)}, f32[512,128]{1,0:T(8,128)S(1)}, f32[512,128]{1,0:T(8,128)S(1)}, f32[512,128]{1,0:T(8,128)S(1)}) fusion(f32[512,128]{1,0:T(8,128)} %bitcast.179, f32[512,128]{1,0:T(8,128)} %bitcast.178, f32[512,128]{1,0:T(8,128)} %bitcast.177, f32[512,128]{1,0:T(8,128)} %gather_fusion.9, ...), kind=kLoop, calls=%fused_computation.37.clone.1 | loop fusion | flops 368836608 | bytes 6029312 | tf_op jit(solution)/shard_map/while/body/eval_jaxpr/reduce_sum | solution.py:52
  (158 shorter events, 133.7 us)
Async XLA Ops:
  0.6 24.8 %copy-start.5 = (f32[512,3,128]{2,0,1:T(8,128)S(1)}, f32[512,3,128]{2,0,1:T(8,128)}, u32[]{:S(2)}) copy-start(f32[512,3,128]{2,0,1:T(8,128)} %param.20) | copy-start | bytes 2359300
  8.1 14.7 %all-to-all-start.2 = ((f32[32,32,3]{1,2,0:T(4,128)}), f32[32,32,3]{1,2,0:T(4,128)S(1)}, u32[]{:S(2)}, u32[]{:S(2)}) async-start(f32[32,32,3]{1,2,0:T(4,128)} %copy.57), calls=%async_computation.2 | async-start | bytes 131072 | tf_op jit(solution)/shard_map/all_to_all | solution.py:103
  22.9 37.2 %all-to-all-start.1 = ((f32[32,32,128]{2,1,0:T(8,128)}), f32[32,32,128]{2,1,0:T(8,128)S(1)}, u32[]{:S(2)}, u32[]{:S(2)}) async-start(f32[32,32,128]{2,1,0:T(8,128)} %bitcast.9), calls=%async_computation.1 | async-start | bytes 1048576 | tf_op jit(solution)/shard_map/all_to_all | solution.py:96
  60.0 43.6 %all-to-all-start.3 = ((f32[32,32,3,128]{3,1,2,0:T(8,128)}), f32[32,32,3,128]{3,1,2,0:T(8,128)S(1)}, u32[]{:S(2)}, u32[]{:S(2)}) async-start(f32[32,32,3,128]{3,1,2,0:T(8,128)} %copy.60), calls=%async_computation.3 | async-start | bytes 3145728 | tf_op jit(solution)/shard_map/all_to_all | solution.py:89
  65.9 4.4 collective-permute-start
  78.9 41.5 %copy-start.10 = (s32[16384]{0:T(1024)S(1)}, s32[16384]{0:T(1024)}, u32[]{:S(2)}) copy-start(s32[16384]{0:T(1024)} %param.22) | copy-start | bytes 196612
  103.6 54.4 %all-to-all-start = ((f32[32,32,296]{2,1,0:T(8,128)}), f32[32,32,296]{2,1,0:T(8,128)}, u32[]{:S(2)}, u32[]{:S(2)}) async-start(f32[32,32,296]{2,1,0:T(8,128)} %bitcast.201), calls=%async_computation | async-start | bytes 3145728 | tf_op jit(solution)/shard_map/all_to_all | solution.py:120
  122.3 35.8 %copy-start.8 = (s32[1024,8]{0,1:T(8,128)S(1)}, s32[1024,8]{0,1:T(8,128)}, u32[]{:S(2)}) copy-start(s32[1024,8]{0,1:T(8,128)} %param.24) | copy-start | bytes 98308
  122.3 35.8 %copy-start.14 = (f32[296]{0:T(512)S(1)}, f32[296]{0:T(512)}, u32[]{:S(2)}) copy-start(f32[296]{0:T(512)} %constant.180) | copy-start | bytes 3556
  122.3 35.8 %copy-start.15 = (f32[296]{0:T(512)S(1)}, f32[296]{0:T(512)}, u32[]{:S(2)}) copy-start(f32[296]{0:T(512)} %constant.181) | copy-start | bytes 3556
  122.3 35.8 %copy-start.16 = (f32[296]{0:T(512)S(1)}, f32[296]{0:T(512)}, u32[]{:S(2)}) copy-start(f32[296]{0:T(512)} %constant.182) | copy-start | bytes 3556
  158.1 694.3 %copy-start.11 = (pred[1024]{0:T(1024)(128)(4,1)S(1)}, pred[1024]{0:T(1024)(128)(4,1)}, u32[]{:S(2)}) copy-start(pred[1024]{0:T(1024)(128)(4,1)} %lt.79) | copy-start | bytes 3076
  410.7 102.2 %copy-start = (f32[512,128]{1,0:T(8,128)S(1)}, f32[512,128]{1,0:T(8,128)}, u32[]{:S(2)}) copy-start(f32[512,128]{1,0:T(8,128)} %fusion.39) | copy-start | bytes 786436 | tf_op jit(solution)/shard_map/while
  410.7 102.2 %copy-start.1 = (f32[512,128]{1,0:T(8,128)S(1)}, f32[512,128]{1,0:T(8,128)}, u32[]{:S(2)}) copy-start(f32[512,128]{1,0:T(8,128)} %get-tuple-element.323) | copy-start | bytes 786436 | tf_op jit(solution)/shard_map/while
  410.7 102.2 %copy-start.2 = (f32[512,128]{1,0:T(8,128)S(1)}, f32[512,128]{1,0:T(8,128)}, u32[]{:S(2)}) copy-start(f32[512,128]{1,0:T(8,128)} %get-tuple-element.303) | copy-start | bytes 786436 | tf_op jit(solution)/shard_map/while
  410.7 102.2 %copy-start.3 = (f32[512,128]{1,0:T(8,128)S(1)}, f32[512,128]{1,0:T(8,128)}, u32[]{:S(2)}) copy-start(f32[512,128]{1,0:T(8,128)} %get-tuple-element.302) | copy-start | bytes 786436 | tf_op jit(solution)/shard_map/while
  410.8 102.2 %copy-start.4 = (f32[512,128]{1,0:T(8,128)S(1)}, f32[512,128]{1,0:T(8,128)}, u32[]{:S(2)}) copy-start(f32[512,128]{1,0:T(8,128)} %get-tuple-element.301) | copy-start | bytes 786436 | tf_op jit(solution)/shard_map/while
  410.8 102.2 %copy-start.6 = (f32[2,512,128]{2,1,0:T(8,128)S(1)}, f32[2,512,128]{2,1,0:T(8,128)}, u32[]{:S(2)}) copy-start(f32[2,512,128]{2,1,0:T(8,128)} %get-tuple-element.338) | copy-start | bytes 1572868 | tf_op jit(solution)/shard_map/while
  749.2 102.2 %copy-start = (f32[512,128]{1,0:T(8,128)S(1)}, f32[512,128]{1,0:T(8,128)}, u32[]{:S(2)}) copy-start(f32[512,128]{1,0:T(8,128)} %fusion.39) | copy-start | bytes 786436 | tf_op jit(solution)/shard_map/while
  749.2 102.2 %copy-start.1 = (f32[512,128]{1,0:T(8,128)S(1)}, f32[512,128]{1,0:T(8,128)}, u32[]{:S(2)}) copy-start(f32[512,128]{1,0:T(8,128)} %get-tuple-element.323) | copy-start | bytes 786436 | tf_op jit(solution)/shard_map/while
  749.2 102.2 %copy-start.2 = (f32[512,128]{1,0:T(8,128)S(1)}, f32[512,128]{1,0:T(8,128)}, u32[]{:S(2)}) copy-start(f32[512,128]{1,0:T(8,128)} %get-tuple-element.303) | copy-start | bytes 786436 | tf_op jit(solution)/shard_map/while
  749.2 102.2 %copy-start.3 = (f32[512,128]{1,0:T(8,128)S(1)}, f32[512,128]{1,0:T(8,128)}, u32[]{:S(2)}) copy-start(f32[512,128]{1,0:T(8,128)} %get-tuple-element.302) | copy-start | bytes 786436 | tf_op jit(solution)/shard_map/while
  749.2 102.2 %copy-start.4 = (f32[512,128]{1,0:T(8,128)S(1)}, f32[512,128]{1,0:T(8,128)}, u32[]{:S(2)}) copy-start(f32[512,128]{1,0:T(8,128)} %get-tuple-element.301) | copy-start | bytes 786436 | tf_op jit(solution)/shard_map/while
  749.2 102.2 %copy-start.6 = (f32[2,512,128]{2,1,0:T(8,128)S(1)}, f32[2,512,128]{2,1,0:T(8,128)}, u32[]{:S(2)}) copy-start(f32[2,512,128]{2,1,0:T(8,128)} %get-tuple-element.338) | copy-start | bytes 1572868 | tf_op jit(solution)/shard_map/while
  (5 other events, 27.7 us)
where the time goes:
time: 867 us; the launch traced here: 855 us
  other arithmetic  553 us (64%)
  local copies, waits for them, and re-layouts  183 us (21%)
  waiting for transfers between devices  58.8 us (7%)
  starting transfers between devices  34.6 us (4%)
  loops' own time  17.7 us (2%)
    reduce_sum x4, other arithmetic, near_block(): summed = summed + jnp.sum(charges[:, None, :] * lax.rsqrt(dist_sq), axis=2)  411 us
    reduce_sum x2, other arithmetic, far_block(): return jnp.sum(densities[:, :, None] * kernel, axis=1)  133 us
    gather x32, local copies, waits for them, and re-layouts, fetch_rows(): return (recv_coords[index], recv_charge[index])  68.3 us
    slice x16, local copies, waits for them, and re-layouts, near_block(): separation = targets[:, component, :, None] - coords[:, component, None, :]  57.1 us
    all_to_all x1, waiting for transfers between devices, on_device(): lax.all_to_all(packed_dens.reshape(device_list, capacity, width), ('grp',...  34.4 us
    scatter x1, local copies, waits for them, and re-layouts, on_device(): jnp.zeros((slot_table, 3, points), jnp.float32).at[dest_row].set(src_coords)  31.4 us
    all_to_all x1, waiting for transfers between devices, on_device(): lax.all_to_all(packed_coords.reshape(device_list, capacity, 3, points), (...  19.8 us
    another operation x1, loops' own time, on_device(): lax.map(block_total, (recv_dens.reshape(count_blocks, block, width), obs_...  17.7 us
  transfers between devices with their start and end apart: 5, of which 3 were waited for; matrix products, arithmetic and copies ran while one was open for 7% of the time, Pallas kernels for 0%

commit v1 on v0

v1 whole, which is shorter than its diff:
```python
import functools
import math

import jax
import jax.numpy as jnp
import numpy as np
from jax import lax
from jax.experimental import pallas as pl
from jax.experimental.pallas import tpu as pltpu
from jax.sharding import PartitionSpec as P

ORDER = 8
RIM = 16
RADIUS = 2.95
HALF_WIDTH = 0.5
SOFT_SQ = 0.0025
FOUR_PI = 4.0 * math.pi
AXES = ("grp", "dom")
FEATS = 32
GROUP = 8
UNROLL = 2
VMEM_LIMIT = 50 * 1024 * 1024

F32 = jnp.float32
BF16 = jnp.bfloat16


def from_behind(block, axis, distance):
    devices = range(lax.axis_size(axis))
    route = [(i - distance, i) for i in devices if i - distance in devices]
    return lax.ppermute(block, axis, route)


def surface_points():
    grid = np.linspace(-1.0, 1.0, ORDER)
    points = np.stack(np.meshgrid(grid, grid, grid, indexing="ij"), 0).reshape(3, -1)
    on_surface = np.max(np.abs(points), axis=0) > 1.0 - 1e-09
    return (points[:, on_surface] * RADIUS).astype(np.float32)


def surface_feats(lanes):
    points = surface_points()
    short = jnp.bfloat16

    def pieces(value):
        high = value.astype(short)
        rest = value - high.astype(np.float32)
        mid = rest.astype(short)
        low = (rest - mid.astype(np.float32)).astype(short)
        return high, mid, low

    table = np.zeros((FEATS, lanes), short)
    width = points.shape[1]
    for c in range(3):
        high, mid, low = pieces(points[c])
        for i, piece in enumerate((high, high, high, mid, mid, low)):
            table[6 * c + i, :width] = piece
    norm = np.ones((lanes,), np.float32)
    norm[:width] = np.sum(points.astype(np.float64) ** 2, axis=0).astype(np.float32)
    table[18:21] = 1.0
    for i, piece in enumerate(pieces(norm)):
        table[21 + i] = piece
    return table


def split(value):
    high = value.astype(BF16).astype(F32)
    rest = value - high
    mid = rest.astype(BF16).astype(F32)
    return high, mid, rest - mid


def put_feats(stage_ref, rows, is_target):
    for f, row in enumerate(rows):
        stage_ref[pl.ds(f, GROUP, stride=FEATS), :] = row


def point_rows(coords, extra, is_target):
    norm = coords[0] * coords[0] + coords[1] * coords[1] + coords[2] * coords[2] + extra
    ones = jnp.ones_like(norm)
    rows = []
    for value in coords:
        high, mid, low = split(-2.0 * value if is_target else value)
        rows += [high, mid, low, high, mid, high] if is_target else [high, high, high, mid, mid, low]
    norms = list(split(norm))
    rows += norms + [ones] * 3 if is_target else [ones] * 3 + norms
    return rows


def store_feats(stage_ref, out_ref, base, rows):
    for f, row in enumerate(rows):
        stage_ref[pl.ds(f, GROUP, stride=FEATS), :] = row
    out_ref[pl.ds(base, GROUP)] = stage_ref[...].reshape(GROUP, FEATS, row.shape[1]).astype(BF16)


def clear_stage(stage_ref):
    stage_ref[...] = jnp.zeros_like(stage_ref)


def lane_sums(block):
    high = block.astype(BF16)
    low = (block - high.astype(F32)).astype(BF16)
    ones = jnp.ones((8, block.shape[1]), BF16)
    dims = (((1,), (1,)), ((), ()))
    total = lax.dot_general(ones, high, dims, preferred_element_type=F32)
    total = total + lax.dot_general(ones, low, dims, preferred_element_type=F32)
    return total[0:1]


def pair_sq(left, right):
    return lax.dot_general(left, right, (((0,), (0,)), ((), ())), preferred_element_type=F32)


def pack_sources(capacity, n_dev, owner_ref, center_ref, coords_ref, charge_ref, out_ref, dest_ref, count_ref):
    rows = 4 * capacity + 8
    leaves = charge_ref.shape[0]
    lane = lax.broadcasted_iota(jnp.int32, (8, 128), 1)
    sub = lax.broadcasted_iota(jnp.int32, (8, 128), 0)

    def clear(i, carry):
        count_ref[i] = 0
        return carry

    lax.fori_loop(0, n_dev, clear, 0)

    def step(j, carry):
        owner = owner_ref[j]
        rank = count_ref[owner]
        count_ref[owner] = rank + 1
        dest_ref[j] = owner * capacity + rank
        base = owner * rows
        for c in range(3):
            out_ref[pl.ds(base + c * capacity + rank, 1), :] = coords_ref[c, pl.ds(j, 1), :]
        out_ref[pl.ds(base + 3 * capacity + rank, 1), :] = charge_ref[pl.ds(j, 1), :]
        place = pl.ds(pl.multiple_of(base + 4 * capacity, 8), 8)
        value = jnp.where(
            sub == 0,
            center_ref[j],
            jnp.where(sub == 1, center_ref[leaves + j], center_ref[2 * leaves + j]),
        )
        out_ref[place, :] = jnp.where(lane == rank, value, out_ref[place, :])
        return carry

    lax.fori_loop(0, leaves, step, 0, unroll=2)


def route_leaves(parents, index_ref, dest_ref, m2l_ref, moved_ref, leaf_ref, out_ref):
    def step(j, carry):
        row = m2l_ref[pl.ds(j, 1), :] + moved_ref[pl.ds(index_ref[j], 1), :]
        leaf_ref[pl.ds(j, 1), :] = row
        out_ref[pl.ds(dest_ref[j], 1), :] = row
        return carry

    lax.fori_loop(0, m2l_ref.shape[0], step, 0, unroll=4)


def near_kernel(capacity, n_dev, slots_ref, recv_ref, obs_ref, out_ref, source_ref, target_ref, stage_a, stage_b):
    rows = 4 * capacity + 8
    clear_stage(stage_a)
    clear_stage(stage_b)

    def prepare(s, carry):
        base = pl.multiple_of(s * rows, 8)
        centers = recv_ref[pl.ds(base + 4 * capacity, 8), :].T
        for g in range(capacity // GROUP):
            slot = pl.multiple_of(s * capacity + g * GROUP, GROUP)
            coords = [
                recv_ref[pl.ds(base + c * capacity + g * GROUP, GROUP), :] - 1.0 for c in range(3)
            ]
            store_feats(stage_a, source_ref, slot, point_rows(coords, 0.0, False))
            targets = [
                (centers[g * GROUP : (g + 1) * GROUP, c : c + 1] - 1.0)
                + HALF_WIDTH * obs_ref[c, pl.ds(slot, GROUP), :]
                for c in range(3)
            ]
            store_feats(stage_b, target_ref, slot, point_rows(targets, SOFT_SQ, True))
        return carry

    lax.fori_loop(0, n_dev, prepare, 0)

    def charge_row(slot):
        dev = slot // capacity
        return recv_ref[pl.ds(dev * rows + 3 * capacity + slot - dev * capacity, 1), :]

    def one_row(r):
        left = target_ref[r]
        total = None
        for p in range(4):
            first, second = slots_ref[8 * r + 2 * p], slots_ref[8 * r + 2 * p + 1]
            right = jnp.concatenate([source_ref[first], source_ref[second]], axis=1)
            inverse = lax.rsqrt(pair_sq(left, right))
            part = inverse[:, :128] * charge_row(first) + inverse[:, 128:] * charge_row(second)
            total = part if total is None else total + part
        out_ref[pl.ds(r, 1), :] = lane_sums(total)

    def step(i, carry):
        for u in range(UNROLL):
            one_row(i * UNROLL + u)
        return carry

    lax.fori_loop(0, out_ref.shape[0] // UNROLL, step, 0)


def far_kernel(dens_ref, obs_ref, near_ref, live_ref, surface_ref, out_ref, target_ref, stage_a):
    width = dens_ref.shape[1]
    clear_stage(stage_a)

    def prepare(g, carry):
        slot = pl.multiple_of(g * GROUP, GROUP)
        targets = [obs_ref[c, pl.ds(slot, GROUP), :] for c in range(3)]
        store_feats(stage_a, target_ref, slot, point_rows(targets, 0.0, True))
        return carry

    lax.fori_loop(0, out_ref.shape[0] // GROUP, prepare, 0)

    def one_row(r):
        inverse = lax.rsqrt(pair_sq(target_ref[r], surface_ref[...]))
        row = dens_ref[pl.ds(r, 1), :]
        total = None
        for first in range(0, width, 128):
            last = min(first + 128, width)
            part = inverse[:, first:last] * row[:, first:last]
            if last - first < 128:
                part = jnp.concatenate([part, jnp.zeros((128, 128 - last + first), F32)], axis=1)
            total = part if total is None else total + part
        return lane_sums(total)

    def step(i, carry):
        for u in range(UNROLL):
            r = i * UNROLL + u
            far = one_row(r) * (1.0 / (FOUR_PI * HALF_WIDTH))
            near = near_ref[pl.ds(r, 1), :] * (1.0 / FOUR_PI)
            out_ref[pl.ds(r, 1), :] = jnp.where(live_ref[r] > 0, far + near, 0.0)
        return carry

    lax.fori_loop(0, out_ref.shape[0] // UNROLL, step, 0)


def on_device(
    parent_local,
    parent_slot,
    child_octant,
    child_m2l,
    l2l_ops,
    leaf_center,
    src_coords,
    src_charge,
    obs_owner,
    obs_offset,
    near_slots,
):
    n_dev = lax.axis_size(AXES)
    leaf_dev, width = child_m2l.shape
    slot_table = obs_offset.shape[0]
    points = obs_offset.shape[2]
    capacity = slot_table // n_dev
    block_rows = 4 * capacity + 8
    my_index = lax.axis_index(AXES)
    vmem, smem = pl.BlockSpec(memory_space=pltpu.VMEM), pl.BlockSpec(memory_space=pltpu.SMEM)
    params = pltpu.CompilerParams(vmem_limit_bytes=VMEM_LIMIT)

    mine = lax.dynamic_slice_in_dim(obs_owner, my_index * leaf_dev, leaf_dev)
    counts = jnp.sum((obs_owner.reshape(n_dev, leaf_dev) == my_index).astype(jnp.int32), axis=1)
    live = (jnp.arange(capacity, dtype=jnp.int32)[None, :] < counts[:, None]).astype(jnp.int32).reshape(slot_table)

    packed, dest = pl.pallas_call(
        functools.partial(pack_sources, capacity, n_dev),
        out_shape=(
            jax.ShapeDtypeStruct((n_dev * block_rows, points), F32),
            jax.ShapeDtypeStruct((leaf_dev,), jnp.int32),
        ),
        in_specs=[smem, smem, vmem, vmem],
        out_specs=(vmem, smem),
        scratch_shapes=[pltpu.SMEM((n_dev,), jnp.int32)],
        compiler_params=params,
        name="pack_sources",
    )(mine, leaf_center.T.reshape(-1), src_coords.transpose(1, 0, 2), src_charge)
    recv = lax.all_to_all(
        packed.reshape(n_dev, block_rows, points), AXES, split_axis=0, concat_axis=0, tiled=True
    ).reshape(n_dev * block_rows, points)

    rim_rows = from_behind(parent_local[parent_local.shape[0] - RIM :], AXES, 1)
    parents = jnp.concatenate([rim_rows, parent_local], axis=0)
    moved = jnp.einsum("pr,oqr->opq", parents, l2l_ops, precision=lax.Precision.HIGHEST)
    stacked = moved.reshape(8 * parents.shape[0], width)
    leaf_local, packed_dens = pl.pallas_call(
        functools.partial(route_leaves, parents.shape[0]),
        out_shape=(
            jax.ShapeDtypeStruct((leaf_dev, width), F32),
            jax.ShapeDtypeStruct((slot_table, width), F32),
        ),
        in_specs=[smem, smem, vmem, vmem],
        out_specs=(vmem, vmem),
        compiler_params=params,
        name="route_leaves",
    )(child_octant * parents.shape[0] + parent_slot, dest, child_m2l, stacked)
    dens = lax.all_to_all(
        packed_dens.reshape(n_dev, capacity, width), AXES, split_axis=0, concat_axis=0, tiled=True
    ).reshape(slot_table, width)

    obs = obs_offset.transpose(1, 0, 2)
    pairs = slot_table * near_slots.shape[1] * points * points
    near = pl.pallas_call(
        functools.partial(near_kernel, capacity, n_dev),
        out_shape=jax.ShapeDtypeStruct((slot_table, points), F32),
        in_specs=[smem, vmem, vmem],
        out_specs=vmem,
        scratch_shapes=[
            pltpu.VMEM((slot_table, FEATS, points), BF16),
            pltpu.VMEM((slot_table, FEATS, points), BF16),
            pltpu.VMEM((GROUP * FEATS, points), F32),
            pltpu.VMEM((GROUP * FEATS, points), F32),
        ],
        compiler_params=params,
        cost_estimate=pl.CostEstimate(flops=70 * pairs, bytes_accessed=5 * 10**6, transcendentals=pairs),
        name="near_field",
    )(near_slots.reshape(-1), recv, obs)
    surface = jnp.asarray(surface_feats(-(-width // 128) * 128))
    potential = pl.pallas_call(
        far_kernel,
        out_shape=jax.ShapeDtypeStruct((slot_table, points), F32),
        in_specs=[vmem, vmem, vmem, smem, vmem],
        out_specs=vmem,
        scratch_shapes=[
            pltpu.VMEM((slot_table, FEATS, points), BF16),
            pltpu.VMEM((GROUP * FEATS, points), F32),
        ],
        compiler_params=params,
        cost_estimate=pl.CostEstimate(flops=10**10, bytes_accessed=5 * 10**6, transcendentals=10**7),
        name="far_field",
    )(dens, obs, near, live, surface)
    return (leaf_local, potential)


def solution(mesh):
    placed = (
        P(AXES, None),
        P(AXES),
        P(AXES),
        P(AXES, None),
        P(),
        P(AXES, None),
        P(AXES, None, None),
        P(AXES, None),
        P(),
        P(AXES, None, None),
        P(AXES, None),
    )
    return jax.shard_map(
        on_device,
        mesh=mesh,
        in_specs=placed,
        out_specs=(P(AXES, None), P(AXES, None)),
        check_vma=False,
    )
```

time: 867 us -> 741 us (0.85); the launches traced: 855 us -> 740 us
  Pallas kernels: 0 us -> 662 us
  other arithmetic: 553 us -> 0.2 us
  local copies, waits for them, and re-layouts: 183 us -> 8.3 us
  waiting for transfers between devices: 58.8 us -> 38.1 us
  loops' own time: 17.7 us -> 0 us
  starting transfers between devices: 34.6 us -> 24 us
    pallas_call x0 -> x4, Pallas kernels: none -> 662 us  [the longest x1 343 us: on_device(): pl.pallas_call(functools.partial(near_kernel, capacity, n_dev), out_shape...]
    reduce_sum x8 -> x1, other arithmetic: 544 us -> 0.12 us  [on_device(): jnp.sum((obs_owner.reshape(n_dev, leaf_dev) == my_index).astype(jnp.int32...]
    gather x33 -> x0, local copies, waits for them, and re-layouts: 70.6 us -> none  [the longest x32 68.3 us: fetch_rows(): return (recv_coords[index], recv_charge[index])]
    slice x18 -> x1, local copies, waits for them, and re-layouts: 57.3 us -> 0.01 us  [on_device(): rim_rows = from_behind(parent_local[parent_local.shape[0] - RIM:], AXES, 1)]
    scatter x4 -> x0, local copies, waits for them, and re-layouts: 39.5 us -> none  [the longest x1 31.4 us: on_device(): jnp.zeros((slot_table, 3, points), jnp.float32).at[dest_row].set(src_coords)]
    all_to_all x4 -> x2, waiting for transfers between devices: 58.8 us -> 37.6 us  [the longest x1 37.6 us: on_device(): lax.all_to_all(packed.reshape(n_dev, block_rows, points), AXES, split_axi...]
    another operation x1 -> x0, loops' own time: 17.7 us -> none  [on_device(): lax.map(block_total, (recv_dens.reshape(count_blocks, block, width), obs_...]
    all_to_all x4 -> x2, starting transfers between devices: 32.4 us -> 21.9 us  [the longest x1 14.5 us: on_device(): lax.all_to_all(packed_dens.reshape(n_dev, capacity, width), AXES, split_a...]
  transfers between devices with their start and end apart: 5 -> 3, of which waited for: 3 -> 2; matrix products, arithmetic and copies ran while one was open for 7% -> 1% of each run, Pallas kernels for 0% -> 47%
where the time goes in v1:
time: 741 us; the launch traced here: 740 us
  Pallas kernels  662 us (89%)
  waiting for transfers between devices  38.1 us (5%)
  starting transfers between devices  24 us (3%)
  local copies, waits for them, and re-layouts  8.3 us (1%)
    pallas_call x1, Pallas kernels, on_device(): pl.pallas_call(functools.partial(near_kernel, capacity, n_dev), out_shape...  343 us
    pallas_call x1, Pallas kernels, on_device(): pl.pallas_call(far_kernel, out_shape=jax.ShapeDtypeStruct((slot_table, po...  308 us
    all_to_all x1, waiting for transfers between devices, on_device(): lax.all_to_all(packed.reshape(n_dev, block_rows, points), AXES, split_axi...  37.6 us
  transfers between devices with their start and end apart: 3, of which 2 were waited for; matrix products, arithmetic and copies ran while one was open for 1% of the time, Pallas kernels for 47%

profile of v1, /device:TPU:0, one launch (start us, length us, event | category | flops | bytes accessed | tf_op | source)
XLA Modules:
  0.0 740.1 jit_solution(15129073123073857373)
XLA Ops:
  0.6 0.7 reshape.37.center_ref
  1.3 0.8 dynamic_slice.3.owner_ref
  2.1 1.1 copy-done
  3.2 0.9 copy-done.1
  4.2 7.1 pack_sources.1
  11.3 7.4 %all-to-all-start.1 = ((f32[32,136,128]{2,1,0:T(8,128)}), f32[32,136,128]{2,1,0:T(8,128)}, u32[]{:S(2)}, u32[]{:S(2)}) async-start(f32[32,136,128]{2,1,0:T(8,128)} %bitcast.8), calls=%async_computation.1 | async-start | bytes 4456448 | tf_op jit(solution)/shard_map/all_to_all | solution.py:278
  18.8 2.1 collective-permute-start
  20.9 0.3 copy.19.m2l_ref
  21.2 0.5 collective-permute-done
  21.7 6.2 fusion
  27.9 4.9 route_leaves.1
  32.9 37.6 %all-to-all-done.1 = f32[32,136,128]{2,1,0:T(8,128)} async-done(((f32[32,136,128]{2,1,0:T(8,128)}), f32[32,136,128]{2,1,0:T(8,128)}, u32[]{:S(2)}, u32[]{:S(2)}) %all-to-all-start.1) | async-done | bytes 2228256 | tf_op jit(solution)/shard_map/all_to_all | solution.py:278
  70.4 14.5 %all-to-all-start = ((f32[32,32,296]{2,1,0:T(8,128)}), f32[32,32,296]{2,1,0:T(8,128)S(1)}, u32[]{:S(2)}, u32[]{:S(2)}) async-start(f32[32,32,296]{2,1,0:T(8,128)} %bitcast.19), calls=%async_computation | async-start | bytes 3145728 | tf_op jit(solution)/shard_map/all_to_all | solution.py:297
  85.0 0.1 reduce_sum.9
  85.1 0.1 fusion.3
  85.2 0.1 reshape.45.live_ref
  85.2 0.2 copy.20
  85.4 0.3 reshape.41.slots_ref
  85.7 1.1 copy.21
  86.8 1.4 copy-done.2
  88.2 342.5 %near_field.1.near_ref = f32[1024,128]{1,0:T(8,128)S(1)} custom-call(s32[8192]{0:T(1024)S(1)} %reshape.41.slots_ref, f32[4352,128]{1,0:T(8,128)} %bitcast.9.recv_ref, f32[3,1024,128]{2,1,0:T(8,128)S(1)} %bitcast.17), custom_call_target="tpu_custom_call" | custom-call | flops 9395240960 | bytes 5000000 | tf_op jit(solution)/shard_map/near_field/pallas_call | solution.py:303
  430.7 0.0 copy-start.3
  430.7 1.4 copy-done.3
  432.1 308.0 %far_field.1 = f32[1024,128]{1,0:T(8,128)} custom-call(f32[1024,296]{1,0:T(8,128)S(1)} %bitcast.15, f32[3,1024,128]{2,1,0:T(8,128)S(1)} %bitcast.18, f32[1024,128]{1,0:T(8,128)S(1)} %near_field.1.near_ref, s32[1024]{0:T(1024)S(1)} %reshape.45.live_ref, bf16[32,384]{1,0:T(8,128)(2,1)S(1)} %copy-done.4), custom_call_target="tpu_custom_call" | custom-call | flops 10000000000 | bytes 5000000 | tf_op jit(solution)/shard_map/far_field/pallas_call | solution.py:319
  (22 shorter events, 0.1 us)
Async XLA Ops:
  2.1 1.1 copy-start
  3.2 0.9 copy-start.1
  11.3 7.5 %copy-start.6 = (f32[64,296]{1,0:T(8,128)S(1)}, f32[64,296]{1,0:T(8,128)}, u32[]{:S(2)}) copy-start(f32[64,296]{1,0:T(8,128)} %param.12) | copy-start | bytes 227332
  11.3 9.6 %copy-start.9 = (s32[512]{0:T(512)S(1)}, s32[512]{0:T(512)}, u32[]{:S(2)}) copy-start(s32[512]{0:T(512)} %param.13) | copy-start | bytes 6148
  11.3 9.6 %copy-start.10 = (s32[512]{0:T(512)S(1)}, s32[512]{0:T(512)}, u32[]{:S(2)}) copy-start(s32[512]{0:T(512)} %param.14) | copy-start | bytes 6148
  11.3 9.6 %copy-start.5 = (f32[512,296]{0,1:T(8,128)S(1)}, f32[512,296]{0,1:T(8,128)}, u32[]{:S(2)}) copy-start(f32[512,296]{0,1:T(8,128)} %param.15) | copy-start | bytes 1818628
  11.3 59.1 %all-to-all-start.1 = ((f32[32,136,128]{2,1,0:T(8,128)}), f32[32,136,128]{2,1,0:T(8,128)}, u32[]{:S(2)}, u32[]{:S(2)}) async-start(f32[32,136,128]{2,1,0:T(8,128)} %bitcast.8), calls=%async_computation.1 | async-start | bytes 4456448 | tf_op jit(solution)/shard_map/all_to_all | solution.py:278
  18.8 2.9 collective-permute-start
  27.9 57.0 %copy-start.7 = (s32[16384]{0:T(1024)S(1)}, s32[16384]{0:T(1024)}, u32[]{:S(2)}) copy-start(s32[16384]{0:T(1024)} %param.20) | copy-start | bytes 196612
  27.9 57.3 %copy-start.8 = (s32[1024,8]{0,1:T(8,128)S(1)}, s32[1024,8]{0,1:T(8,128)}, u32[]{:S(2)}) copy-start(s32[1024,8]{0,1:T(8,128)} %param.22) | copy-start | bytes 98308
  70.4 360.2 %all-to-all-start = ((f32[32,32,296]{2,1,0:T(8,128)}), f32[32,32,296]{2,1,0:T(8,128)S(1)}, u32[]{:S(2)}, u32[]{:S(2)}) async-start(f32[32,32,296]{2,1,0:T(8,128)} %bitcast.19), calls=%async_computation | async-start | bytes 3145728 | tf_op jit(solution)/shard_map/all_to_all | solution.py:297
  86.8 1.4 copy-start.2
  88.2 342.5 %copy-start.4 = (bf16[32,384]{1,0:T(8,128)(2,1)S(1)}, bf16[32,384]{1,0:T(8,128)(2,1)}, u32[]{:S(2)}) copy-start(bf16[32,384]{1,0:T(8,128)(2,1)} %constant.20.clone.surface_ref) | copy-start | bytes 73732
  430.7 1.4 copy-start.3

commit v2 on v1

--- a/solution.py
+++ b/solution.py
@@ -18,7 +18,6 @@
 AXES = ("grp", "dom")
 FEATS = 32
 GROUP = 8
-UNROLL = 2
 VMEM_LIMIT = 50 * 1024 * 1024
 
 F32 = jnp.float32
@@ -70,11 +69,6 @@
     return high, mid, rest - mid
 
 
-def put_feats(stage_ref, rows, is_target):
-    for f, row in enumerate(rows):
-        stage_ref[pl.ds(f, GROUP, stride=FEATS), :] = row
-
-
 def point_rows(coords, extra, is_target):
     norm = coords[0] * coords[0] + coords[1] * coords[1] + coords[2] * coords[2] + extra
     ones = jnp.ones_like(norm)
@@ -100,15 +94,9 @@
 def lane_sums(block):
     high = block.astype(BF16)
     low = (block - high.astype(F32)).astype(BF16)
-    ones = jnp.ones((8, block.shape[1]), BF16)
-    dims = (((1,), (1,)), ((), ()))
-    total = lax.dot_general(ones, high, dims, preferred_element_type=F32)
-    total = total + lax.dot_general(ones, low, dims, preferred_element_type=F32)
-    return total[0:1]
-
-
-def pair_sq(left, right):
-    return lax.dot_general(left, right, (((0,), (0,)), ((), ())), preferred_element_type=F32)
+    ones = jnp.ones((GROUP, 2 * block.shape[1]), BF16)
+    pieces = jnp.concatenate([high, low], axis=1)
+    return lax.dot_general(ones, pieces, (((1,), (1,)), ((), ())), preferred_element_type=F32)
 
 
 def pack_sources(capacity, n_dev, owner_ref, center_ref, coords_ref, charge_ref, out_ref, dest_ref, count_ref):
@@ -154,8 +142,26 @@
     lax.fori_loop(0, m2l_ref.shape[0], step, 0, unroll=4)
 
 
-def near_kernel(capacity, n_dev, slots_ref, recv_ref, obs_ref, out_ref, source_ref, target_ref, stage_a, stage_b):
+def near_kernel(
+    capacity,
+    n_dev,
+    slots_ref,
+    recv_ref,
+    obs_ref,
+    out_ref,
+    source_ref,
+    target_ref,
+    charge_ref,
+    stage_a,
+    stage_b,
+    left_a,
+    left_b,
+    total_a,
+    total_b,
+):
     rows = 4 * capacity + 8
+    blocks = out_ref.shape[0] // GROUP
+    sub = lax.broadcasted_iota(jnp.int32, (GROUP, out_ref.shape[1]), 0)
     clear_stage(stage_a)
     clear_stage(stage_b)
 
@@ -174,35 +180,61 @@
                 for c in range(3)
             ]
             store_feats(stage_b, target_ref, slot, point_rows(targets, SOFT_SQ, True))
+            charge_ref[pl.ds(slot, GROUP), :] = recv_ref[
+                pl.ds(base + 3 * capacity + g * GROUP, GROUP), :
+            ]
         return carry
 
     lax.fori_loop(0, n_dev, prepare, 0)
 
-    def charge_row(slot):
-        dev = slot // capacity
-        return recv_ref[pl.ds(dev * rows + 3 * capacity + slot - dev * capacity, 1), :]
-
-    def one_row(r):
-        left = target_ref[r]
+    def turn(block, u, left_ref):
+        left_ref[u] = target_ref[block * GROUP + u].T
+
+    def pair_work(block, u, left_ref, total_ref):
+        left = left_ref[u]
+        at = (block * GROUP + u) * GROUP
         total = None
         for p in range(4):
-            first, second = slots_ref[8 * r + 2 * p], slots_ref[8 * r + 2 * p + 1]
+            first, second = slots_ref[at + 2 * p], slots_ref[at + 2 * p + 1]
             right = jnp.concatenate([source_ref[first], source_ref[second]], axis=1)
-            inverse = lax.rsqrt(pair_sq(left, right))
-            part = inverse[:, :128] * charge_row(first) + inverse[:, 128:] * charge_row(second)
+            inverse = lax.rsqrt(jnp.dot(left, right, preferred_element_type=F32))
+            part = (
+                inverse[:, :128] * charge_ref[pl.ds(first, 1), :]
+                + inverse[:, 128:] * charge_ref[pl.ds(second, 1), :]
+            )
             total = part if total is None else total + part
-        out_ref[pl.ds(r, 1), :] = lane_sums(total)
+        total_ref[u] = total
+
+    def half(before, block, after, left_now, left_next, total_before, total_now):
+        sums = None
+        for u in range(GROUP):
+            turn(after, u, left_next)
+            pair_work(block, u, left_now, total_now)
+            part = lane_sums(total_before[u])
+            sums = part if sums is None else jnp.where(sub == u, part, sums)
+        out_ref[pl.ds(pl.multiple_of(before * GROUP, GROUP), GROUP), :] = sums
+
+    for u in range(GROUP):
+        turn(0, u, left_a)
+    total_b[...] = jnp.zeros_like(total_b)
 
     def step(i, carry):
-        for u in range(UNROLL):
-            one_row(i * UNROLL + u)
-        return carry
-
-    lax.fori_loop(0, out_ref.shape[0] // UNROLL, step, 0)
-
-
-def far_kernel(dens_ref, obs_ref, near_ref, live_ref, surface_ref, out_ref, target_ref, stage_a):
+        one, two = 2 * i, 2 * i + 1
+        half(jnp.maximum(one - 1, 0), one, two, left_a, left_b, total_b, total_a)
+        half(one, two, jnp.minimum(two + 1, blocks - 1), left_b, left_a, total_a, total_b)
+        return carry
+
+    lax.fori_loop(0, blocks // 2, step, 0)
+    sums = None
+    for u in range(GROUP):
+        part = lane_sums(total_b[u])
+        sums = part if sums is None else jnp.where(sub == u, part, sums)
+    out_ref[pl.ds((blocks - 1) * GROUP, GROUP), :] = sums
+
+
+def far_kernel(dens_ref, obs_ref, near_ref, live_ref, surface_ref, out_ref, target_ref, turned_ref, stage_a):
     width = dens_ref.shape[1]
+    points = out_ref.shape[1]
     clear_stage(stage_a)
 
     def prepare(g, carry):
@@ -212,28 +244,35 @@
         return carry
 
     lax.fori_loop(0, out_ref.shape[0] // GROUP, prepare, 0)
-
-    def one_row(r):
-        inverse = lax.rsqrt(pair_sq(target_ref[r], surface_ref[...]))
-        row = dens_ref[pl.ds(r, 1), :]
-        total = None
-        for first in range(0, width, 128):
-            last = min(first + 128, width)
-            part = inverse[:, first:last] * row[:, first:last]
-            if last - first < 128:
-                part = jnp.concatenate([part, jnp.zeros((128, 128 - last + first), F32)], axis=1)
-            total = part if total is None else total + part
-        return lane_sums(total)
-
-    def step(i, carry):
-        for u in range(UNROLL):
-            r = i * UNROLL + u
-            far = one_row(r) * (1.0 / (FOUR_PI * HALF_WIDTH))
-            near = near_ref[pl.ds(r, 1), :] * (1.0 / FOUR_PI)
-            out_ref[pl.ds(r, 1), :] = jnp.where(live_ref[r] > 0, far + near, 0.0)
-        return carry
-
-    lax.fori_loop(0, out_ref.shape[0] // UNROLL, step, 0)
+    sub = lax.broadcasted_iota(jnp.int32, (GROUP, points), 0)
+
+    def tile(t, carry):
+        first_row = pl.multiple_of(t * 128, 128)
+        turned_ref[...] = dens_ref[pl.ds(first_row, 128), :].T
+
+        def group(g, carry):
+            dens = pltpu.roll(turned_ref[...], lax.rem(128 - g * GROUP, 128), 1)
+            slot = pl.multiple_of(first_row + g * GROUP, GROUP)
+            far = jnp.zeros((GROUP, points), F32)
+            for u in range(0, GROUP, 2):
+                right = jnp.concatenate([target_ref[slot + u], target_ref[slot + u + 1]], axis=1)
+                inverse = lax.rsqrt(jnp.dot(surface_ref[...], right, preferred_element_type=F32))
+                for v in range(2):
+                    terms = inverse[:, v * points : (v + 1) * points] * dens[:, u + v : u + v + 1]
+                    row = jnp.sum(terms, axis=0, keepdims=True)
+                    far = jnp.where(sub == u + v, row, far)
+            near = near_ref[pl.ds(slot, GROUP), :]
+            total = far * (1.0 / (FOUR_PI * HALF_WIDTH)) + near * (1.0 / FOUR_PI)
+            alive = jnp.zeros((GROUP, points), jnp.int32)
+            for u in range(GROUP):
+                alive = jnp.where(sub == u, live_ref[slot + u], alive)
+            out_ref[pl.ds(slot, GROUP), :] = jnp.where(alive > 0, total, 0.0)
+            return carry
+
+        lax.fori_loop(0, 128 // GROUP, group, 0)
+        return carry
+
+    lax.fori_loop(0, out_ref.shape[0] // 128, tile, 0)
 
 
 def on_device(
@@ -308,14 +347,19 @@
         scratch_shapes=[
             pltpu.VMEM((slot_table, FEATS, points), BF16),
             pltpu.VMEM((slot_table, FEATS, points), BF16),
+            pltpu.VMEM((slot_table, points), F32),
             pltpu.VMEM((GROUP * FEATS, points), F32),
             pltpu.VMEM((GROUP * FEATS, points), F32),
+            pltpu.VMEM((GROUP, points, FEATS), BF16),
+            pltpu.VMEM((GROUP, points, FEATS), BF16),
+            pltpu.VMEM((GROUP, points, points), F32),
+            pltpu.VMEM((GROUP, points, points), F32),
         ],
         compiler_params=params,
         cost_estimate=pl.CostEstimate(flops=70 * pairs, bytes_accessed=5 * 10**6, transcendentals=pairs),
         name="near_field",
     )(near_slots.reshape(-1), recv, obs)
-    surface = jnp.asarray(surface_feats(-(-width // 128) * 128))
+    surface = jnp.asarray(surface_feats(width).T)
     potential = pl.pallas_call(
         far_kernel,
         out_shape=jax.ShapeDtypeStruct((slot_table, points), F32),
@@ -323,6 +367,7 @@
         out_specs=vmem,
         scratch_shapes=[
             pltpu.VMEM((slot_table, FEATS, points), BF16),
+            pltpu.VMEM((width, 128), F32),
             pltpu.VMEM((GROUP * FEATS, points), F32),
         ],
         compiler_params=params,

time: 741 us -> 268 us (0.36)
  Pallas kernels: 662 us -> 190 us
    pallas_call x1, Pallas kernels: 343 us -> 103 us  [on_device(): pl.pallas_call(functools.partial(near_kernel, capacity, n_dev), out_shape...]
    pallas_call x1, Pallas kernels: 308 us -> 74.8 us  [on_device(): pl.pallas_call(far_kernel, out_shape=jax.ShapeDtypeStruct((slot_table, po...]
  transfers between devices with their start and end apart: 3 -> 3, of which waited for: 2 -> 2; matrix products, arithmetic and copies ran while one was open for 1% -> 3% of each run, Pallas kernels for 47% -> 40%
where the time goes in v2:
time: 268 us; the launch traced here: 267 us
  Pallas kernels  190 us (71%)
  waiting for transfers between devices  38.1 us (14%)
  starting transfers between devices  24 us (9%)
  local copies, waits for them, and re-layouts  8.29 us (3%)
  matrix products  6.23 us (2%)
    pallas_call x1, Pallas kernels, on_device(): pl.pallas_call(functools.partial(near_kernel, capacity, n_dev), out_shape...  103 us
    pallas_call x1, Pallas kernels, on_device(): pl.pallas_call(far_kernel, out_shape=jax.ShapeDtypeStruct((slot_table, po...  74.8 us
    all_to_all x1, waiting for transfers between devices, on_device(): lax.all_to_all(packed.reshape(n_dev, block_rows, points), AXES, split_axi...  37.6 us
    all_to_all x1, starting transfers between devices, on_device(): lax.all_to_all(packed_dens.reshape(n_dev, capacity, width), AXES, split_a...  14.5 us
    all_to_all x1, starting transfers between devices, on_device(): lax.all_to_all(packed.reshape(n_dev, block_rows, points), AXES, split_axi...  7.42 us
    pallas_call x1, Pallas kernels, on_device(): pl.pallas_call(functools.partial(pack_sources, capacity, n_dev), out_shap...  7.07 us
    unnamed x25, local copies, waits for them, and re-layouts  6.48 us
    dot_general x1, matrix products, on_device(): jnp.einsum('pr,oqr->opq', parents, l2l_ops, precision=lax.Precision.HIGHEST)  6.23 us
  transfers between devices with their start and end apart: 3, of which 2 were waited for; matrix products, arithmetic and copies ran while one was open for 3% of the time, Pallas kernels for 40%

profile of v2, /device:TPU:0, one launch (start us, length us, event | category | flops | bytes accessed | tf_op | source)
XLA Modules:
  0.0 267.2 jit_solution(7813318529594607836)
XLA Ops:
  0.6 0.7 reshape.37.center_ref
  1.3 0.8 dynamic_slice.3.owner_ref
  2.1 1.1 copy-done
  3.2 0.9 copy-done.1
  4.2 7.1 %pack_sources.1 = (f32[4352,128]{1,0:T(8,128)}, s32[512]{0:T(512)S(1)}) custom-call(s32[512]{0:T(512)S(1)} %dynamic_slice.3.owner_ref, f32[1536]{0:T(1024)S(1)} %reshape.37.center_ref, f32[3,512,128]{2,1,0:T(8,128)S(1)} %bitcast.16, f32[512,128]{1,0:T(8,128)S(1)} %copy-done.1), custom_call_target="tpu_custom_call" | custom-call | tf_op jit(solution)/shard_map/pack_sources/pallas_call | solution.py:305
  11.3 7.4 %all-to-all-start.1 = ((f32[32,136,128]{2,1,0:T(8,128)}), f32[32,136,128]{2,1,0:T(8,128)}, u32[]{:S(2)}, u32[]{:S(2)}) async-start(f32[32,136,128]{2,1,0:T(8,128)} %bitcast.8), calls=%async_computation.1 | async-start | bytes 4456448 | tf_op jit(solution)/shard_map/all_to_all | solution.py:317
  18.8 2.1 collective-permute-start
  20.9 0.3 copy.19.m2l_ref
  21.2 0.5 collective-permute-done
  21.7 6.2 %fusion = f32[80,8,296]{2,0,1:T(8,128)S(1)} fusion(f32[8,296,296]{2,1,0:T(8,128)} %param.16, f32[64,296]{1,0:T(8,128)S(1)} %copy-done.6, f32[16,296]{1,0:T(8,128)S(1)} %collective-permute-done), kind=kOutput, calls=%fused_computation.1 | convolution fusion | flops 672914560 | bytes 3656192 | tf_op jit(solution)/shard_map/pr,oqr->opq/dot_general | solution.py:323
  27.9 4.9 %route_leaves.1 = (f32[512,296]{1,0:T(8,128)S(1)}, f32[1024,296]{1,0:T(8,128)}) custom-call(s32[512]{0:T(512)S(1)} %multiply_add_fusion.index_ref, s32[512]{0:T(512)S(1)} %get-tuple-element.6.dest_ref, f32[512,296]{1,0:T(8,128)S(1)} %copy.19.m2l_ref, f32[640,296]{1,0:T(8,128)S(1)} %bitcast.14), custom_call_target="tpu_custom_call" | custom-call | tf_op jit(solution)/shard_map/route_leaves/pallas_call | solution.py:325
  32.9 37.6 %all-to-all-done.1 = f32[32,136,128]{2,1,0:T(8,128)} async-done(((f32[32,136,128]{2,1,0:T(8,128)}), f32[32,136,128]{2,1,0:T(8,128)}, u32[]{:S(2)}, u32[]{:S(2)}) %all-to-all-start.1) | async-done | bytes 2228256 | tf_op jit(solution)/shard_map/all_to_all | solution.py:317
  70.4 14.5 %all-to-all-start = ((f32[32,32,296]{2,1,0:T(8,128)}), f32[32,32,296]{2,1,0:T(8,128)S(1)}, u32[]{:S(2)}, u32[]{:S(2)}) async-start(f32[32,32,296]{2,1,0:T(8,128)} %bitcast.19), calls=%async_computation | async-start | bytes 3145728 | tf_op jit(solution)/shard_map/all_to_all | solution.py:336
  85.0 0.1 reduce_sum.9
  85.1 0.1 fusion.3
  85.2 0.1 reshape.45.live_ref
  85.2 0.2 copy.20
  85.4 0.3 reshape.41.slots_ref
  85.7 1.1 copy.21
  86.8 1.4 copy-done.2
  88.2 102.8 %near_field.1.near_ref = f32[1024,128]{1,0:T(8,128)S(1)} custom-call(s32[8192]{0:T(1024)S(1)} %reshape.41.slots_ref, f32[4352,128]{1,0:T(8,128)} %bitcast.9.recv_ref, f32[3,1024,128]{2,1,0:T(8,128)S(1)} %bitcast.17), custom_call_target="tpu_custom_call" | custom-call | flops 9395240960 | bytes 5000000 | tf_op jit(solution)/shard_map/near_field/pallas_call | solution.py:342
  190.9 0.0 copy-done.4
  191.0 1.4 copy-done.3
  192.4 74.8 %far_field.1 = f32[1024,128]{1,0:T(8,128)} custom-call(f32[1024,296]{1,0:T(8,128)S(1)} %bitcast.15, f32[3,1024,128]{2,1,0:T(8,128)S(1)} %bitcast.18, f32[1024,128]{1,0:T(8,128)S(1)} %near_field.1.near_ref, s32[1024]{0:T(1024)S(1)} %reshape.45.live_ref, bf16[296,32]{1,0:T(8,128)(2,1)S(1)} %copy-done.4), custom_call_target="tpu_custom_call" | custom-call | flops 10000000000 | bytes 5000000 | tf_op jit(solution)/shard_map/far_field/pallas_call | solution.py:363
  (22 shorter events, 0.1 us)
Async XLA Ops:
  2.1 1.1 copy-start
  3.2 0.9 copy-start.1
  11.3 7.5 %copy-start.6 = (f32[64,296]{1,0:T(8,128)S(1)}, f32[64,296]{1,0:T(8,128)}, u32[]{:S(2)}) copy-start(f32[64,296]{1,0:T(8,128)} %param.12) | copy-start | bytes 227332
  11.3 9.6 %copy-start.9 = (s32[512]{0:T(512)S(1)}, s32[512]{0:T(512)}, u32[]{:S(2)}) copy-start(s32[512]{0:T(512)} %param.13) | copy-start | bytes 6148
  11.3 9.6 %copy-start.10 = (s32[512]{0:T(512)S(1)}, s32[512]{0:T(512)}, u32[]{:S(2)}) copy-start(s32[512]{0:T(512)} %param.14) | copy-start | bytes 6148
  11.3 9.6 %copy-start.5 = (f32[512,296]{0,1:T(8,128)S(1)}, f32[512,296]{0,1:T(8,128)}, u32[]{:S(2)}) copy-start(f32[512,296]{0,1:T(8,128)} %param.15) | copy-start | bytes 1818628
  11.3 59.1 %all-to-all-start.1 = ((f32[32,136,128]{2,1,0:T(8,128)}), f32[32,136,128]{2,1,0:T(8,128)}, u32[]{:S(2)}, u32[]{:S(2)}) async-start(f32[32,136,128]{2,1,0:T(8,128)} %bitcast.8), calls=%async_computation.1 | async-start | bytes 4456448 | tf_op jit(solution)/shard_map/all_to_all | solution.py:317
  18.8 2.9 %collective-permute-start = (f32[16,296]{1,0:T(8,128)S(1)}, f32[16,296]{1,0:T(8,128)S(1)}, u32[]{:S(2)}, u32[]{:S(2)}) collective-permute-start(f32[16,296]{1,0:T(8,128)S(1)} %slice.3), channel_id=1, source_target_pairs={{0,1},{1,2},{2,3},{3,4},{4,5},{5,6},{6,7},{7,8},{8,9},{9,10},{10,1... | collective-permute-start | bytes 56840 | tf_op jit(solution)/shard_map/ppermute | solution.py:30
  27.9 57.0 %copy-start.7 = (s32[16384]{0:T(1024)S(1)}, s32[16384]{0:T(1024)}, u32[]{:S(2)}) copy-start(s32[16384]{0:T(1024)} %param.20) | copy-start | bytes 196612
  27.9 57.3 %copy-start.8 = (s32[1024,8]{0,1:T(8,128)S(1)}, s32[1024,8]{0,1:T(8,128)}, u32[]{:S(2)}) copy-start(s32[1024,8]{0,1:T(8,128)} %param.22) | copy-start | bytes 98308
  70.4 120.5 %all-to-all-start = ((f32[32,32,296]{2,1,0:T(8,128)}), f32[32,32,296]{2,1,0:T(8,128)S(1)}, u32[]{:S(2)}, u32[]{:S(2)}) async-start(f32[32,32,296]{2,1,0:T(8,128)} %bitcast.19), calls=%async_computation | async-start | bytes 3145728 | tf_op jit(solution)/shard_map/all_to_all | solution.py:336
  86.8 1.4 copy-start.2
  88.2 102.8 %copy-start.4 = (bf16[296,32]{1,0:T(8,128)(2,1)S(1)}, bf16[296,32]{1,0:T(8,128)(2,1)}, u32[]{:S(2)}) copy-start(bf16[296,32]{1,0:T(8,128)(2,1)} %constant.20.clone.surface_ref) | copy-start | bytes 56836
  191.0 1.4 copy-start.3

commit v3 on v2

--- a/solution.py
+++ b/solution.py
@@ -30,36 +30,17 @@
     return lax.ppermute(block, axis, route)
 
 
-def surface_points():
-    grid = np.linspace(-1.0, 1.0, ORDER)
-    points = np.stack(np.meshgrid(grid, grid, grid, indexing="ij"), 0).reshape(3, -1)
-    on_surface = np.max(np.abs(points), axis=0) > 1.0 - 1e-09
-    return (points[:, on_surface] * RADIUS).astype(np.float32)
-
-
-def surface_feats(lanes):
-    points = surface_points()
-    short = jnp.bfloat16
-
-    def pieces(value):
-        high = value.astype(short)
-        rest = value - high.astype(np.float32)
-        mid = rest.astype(short)
-        low = (rest - mid.astype(np.float32)).astype(short)
-        return high, mid, low
-
-    table = np.zeros((FEATS, lanes), short)
-    width = points.shape[1]
-    for c in range(3):
-        high, mid, low = pieces(points[c])
-        for i, piece in enumerate((high, high, high, mid, mid, low)):
-            table[6 * c + i, :width] = piece
-    norm = np.ones((lanes,), np.float32)
-    norm[:width] = np.sum(points.astype(np.float64) ** 2, axis=0).astype(np.float32)
-    table[18:21] = 1.0
-    for i, piece in enumerate(pieces(norm)):
-        table[21 + i] = piece
-    return table
+def surface_grid():
+    axis = (np.linspace(-1.0, 1.0, ORDER) * RADIUS).astype(np.float32)
+    ends = (0, ORDER - 1)
+    points = [
+        (i, j, k)
+        for i in range(ORDER)
+        for j in range(ORDER)
+        for k in range(ORDER)
+        if i in ends or j in ends or k in ends
+    ]
+    return [float(value) for value in axis], points
 
 
 def split(value):
@@ -99,24 +80,15 @@
     return lax.dot_general(ones, pieces, (((1,), (1,)), ((), ())), preferred_element_type=F32)
 
 
-def pack_sources(capacity, n_dev, owner_ref, center_ref, coords_ref, charge_ref, out_ref, dest_ref, count_ref):
+def pack_sources(capacity, owner_ref, rank_ref, center_ref, coords_ref, charge_ref, out_ref):
     rows = 4 * capacity + 8
     leaves = charge_ref.shape[0]
     lane = lax.broadcasted_iota(jnp.int32, (8, 128), 1)
     sub = lax.broadcasted_iota(jnp.int32, (8, 128), 0)
 
-    def clear(i, carry):
-        count_ref[i] = 0
-        return carry
-
-    lax.fori_loop(0, n_dev, clear, 0)
-
     def step(j, carry):
-        owner = owner_ref[j]
-        rank = count_ref[owner]
-        count_ref[owner] = rank + 1
-        dest_ref[j] = owner * capacity + rank
-        base = owner * rows
+        rank = rank_ref[j]
+        base = owner_ref[j] * rows
         for c in range(3):
             out_ref[pl.ds(base + c * capacity + rank, 1), :] = coords_ref[c, pl.ds(j, 1), :]
         out_ref[pl.ds(base + 3 * capacity + rank, 1), :] = charge_ref[pl.ds(j, 1), :]
@@ -129,14 +101,14 @@
         out_ref[place, :] = jnp.where(lane == rank, value, out_ref[place, :])
         return carry
 
-    lax.fori_loop(0, leaves, step, 0, unroll=2)
-
-
-def route_leaves(parents, index_ref, dest_ref, m2l_ref, moved_ref, leaf_ref, out_ref):
+    lax.fori_loop(0, leaves, step, 0, unroll=4)
+
+
+def route_leaves(index_ref, dest_ref, m2l_ref, moved_ref, leaf_ref, out_ref):
     def step(j, carry):
         row = m2l_ref[pl.ds(j, 1), :] + moved_ref[pl.ds(index_ref[j], 1), :]
         leaf_ref[pl.ds(j, 1), :] = row
-        out_ref[pl.ds(dest_ref[j], 1), :] = row
+        out_ref[pl.ds(dest_ref[j], 1), : row.shape[1]] = row
         return carry
 
     lax.fori_loop(0, m2l_ref.shape[0], step, 0, unroll=4)
@@ -232,47 +204,47 @@
     out_ref[pl.ds((blocks - 1) * GROUP, GROUP), :] = sums
 
 
-def far_kernel(dens_ref, obs_ref, near_ref, live_ref, surface_ref, out_ref, target_ref, turned_ref, stage_a):
-    width = dens_ref.shape[1]
-    points = out_ref.shape[1]
-    clear_stage(stage_a)
-
-    def prepare(g, carry):
-        slot = pl.multiple_of(g * GROUP, GROUP)
-        targets = [obs_ref[c, pl.ds(slot, GROUP), :] for c in range(3)]
-        store_feats(stage_a, target_ref, slot, point_rows(targets, 0.0, True))
-        return carry
-
-    lax.fori_loop(0, out_ref.shape[0] // GROUP, prepare, 0)
-    sub = lax.broadcasted_iota(jnp.int32, (GROUP, points), 0)
+def far_kernel(dens_ref, obs_ref, near_ref, live_ref, out_ref, turned_ref, point_ref, far_ref):
+    axis, surface = surface_grid()
+    number = {point: q for q, point in enumerate(surface)}
+    side = out_ref.shape[1]
 
     def tile(t, carry):
-        first_row = pl.multiple_of(t * 128, 128)
-        turned_ref[...] = dens_ref[pl.ds(first_row, 128), :].T
-
-        def group(g, carry):
-            dens = pltpu.roll(turned_ref[...], lax.rem(128 - g * GROUP, 128), 1)
-            slot = pl.multiple_of(first_row + g * GROUP, GROUP)
-            far = jnp.zeros((GROUP, points), F32)
-            for u in range(0, GROUP, 2):
-                right = jnp.concatenate([target_ref[slot + u], target_ref[slot + u + 1]], axis=1)
-                inverse = lax.rsqrt(jnp.dot(surface_ref[...], right, preferred_element_type=F32))
-                for v in range(2):
-                    terms = inverse[:, v * points : (v + 1) * points] * dens[:, u + v : u + v + 1]
-                    row = jnp.sum(terms, axis=0, keepdims=True)
-                    far = jnp.where(sub == u + v, row, far)
-            near = near_ref[pl.ds(slot, GROUP), :]
-            total = far * (1.0 / (FOUR_PI * HALF_WIDTH)) + near * (1.0 / FOUR_PI)
-            alive = jnp.zeros((GROUP, points), jnp.int32)
-            for u in range(GROUP):
-                alive = jnp.where(sub == u, live_ref[slot + u], alive)
-            out_ref[pl.ds(slot, GROUP), :] = jnp.where(alive > 0, total, 0.0)
+        first = pl.multiple_of(t * side, side)
+        for column in range(0, dens_ref.shape[1], side):
+            turned_ref[pl.ds(column, side), :] = dens_ref[pl.ds(first, side), pl.ds(column, side)].T
+        for c in range(3):
+            point_ref[c] = obs_ref[c, pl.ds(first, side), :].T
+
+        def points(b, carry):
+            place = pl.ds(pl.multiple_of(b * GROUP, GROUP), GROUP)
+            squares = []
+            for c in range(3):
+                value = point_ref[c, place, :]
+                squares.append([(value - at) * (value - at) for at in axis])
+            totals = [jnp.zeros((GROUP, side), F32) for _ in range(4)]
+            turn = 0
+            for j in range(ORDER):
+                for k in range(ORDER):
+                    partial = squares[1][j] + squares[2][k]
+                    for i in range(ORDER):
+                        q = number.get((i, j, k))
+                        if q is None:
+                            continue
+                        inverse = lax.rsqrt(squares[0][i] + partial)
+                        totals[turn] = totals[turn] + inverse * turned_ref[pl.ds(q, 1), :]
+                        turn = (turn + 1) % 4
+            far_ref[place, :] = (totals[0] + totals[1]) + (totals[2] + totals[3])
             return carry
 
-        lax.fori_loop(0, 128 // GROUP, group, 0)
-        return carry
-
-    lax.fori_loop(0, out_ref.shape[0] // 128, tile, 0)
+        lax.fori_loop(0, side // GROUP, points, 0)
+        near = near_ref[pl.ds(first, side), :].T
+        total = far_ref[...] * (1.0 / (FOUR_PI * HALF_WIDTH)) + near * (1.0 / FOUR_PI)
+        total = jnp.where(live_ref[pl.ds(t, 1), :] > 0, total, 0.0)
+        out_ref[pl.ds(first, side), :] = total.T
+        return carry
+
+    lax.fori_loop(0, out_ref.shape[0] // side, tile, 0)
 
 
 def on_device(
@@ -294,6 +266,7 @@
     points = obs_offset.shape[2]
     capacity = slot_table // n_dev
     block_rows = 4 * capacity + 8
+    lanes = -(-width // points) * points
     my_index = lax.axis_index(AXES)
     vmem, smem = pl.BlockSpec(memory_space=pltpu.VMEM), pl.BlockSpec(memory_space=pltpu.SMEM)
     params = pltpu.CompilerParams(vmem_limit_bytes=VMEM_LIMIT)
@@ -302,18 +275,17 @@
     counts = jnp.sum((obs_owner.reshape(n_dev, leaf_dev) == my_index).astype(jnp.int32), axis=1)
     live = (jnp.arange(capacity, dtype=jnp.int32)[None, :] < counts[:, None]).astype(jnp.int32).reshape(slot_table)
 
-    packed, dest = pl.pallas_call(
-        functools.partial(pack_sources, capacity, n_dev),
-        out_shape=(
-            jax.ShapeDtypeStruct((n_dev * block_rows, points), F32),
-            jax.ShapeDtypeStruct((leaf_dev,), jnp.int32),
-        ),
-        in_specs=[smem, smem, vmem, vmem],
-        out_specs=(vmem, smem),
-        scratch_shapes=[pltpu.SMEM((n_dev,), jnp.int32)],
+    leaf_at = jnp.arange(leaf_dev, dtype=jnp.int32)
+    same = (mine[:, None] == mine[None, :]) & (leaf_at[None, :] < leaf_at[:, None])
+    rank = jnp.sum(same.astype(jnp.int32), axis=1)
+    packed = pl.pallas_call(
+        functools.partial(pack_sources, capacity),
+        out_shape=jax.ShapeDtypeStruct((n_dev * block_rows, points), F32),
+        in_specs=[smem, smem, smem, vmem, vmem],
+        out_specs=vmem,
         compiler_params=params,
         name="pack_sources",
-    )(mine, leaf_center.T.reshape(-1), src_coords.transpose(1, 0, 2), src_charge)
+    )(mine, rank, leaf_center.T.reshape(-1), src_coords.transpose(1, 0, 2), src_charge)
     recv = lax.all_to_all(
         packed.reshape(n_dev, block_rows, points), AXES, split_axis=0, concat_axis=0, tiled=True
     ).reshape(n_dev * block_rows, points)
@@ -323,19 +295,19 @@
     moved = jnp.einsum("pr,oqr->opq", parents, l2l_ops, precision=lax.Precision.HIGHEST)
     stacked = moved.reshape(8 * parents.shape[0], width)
     leaf_local, packed_dens = pl.pallas_call(
-        functools.partial(route_leaves, parents.shape[0]),
+        route_leaves,
         out_shape=(
             jax.ShapeDtypeStruct((leaf_dev, width), F32),
-            jax.ShapeDtypeStruct((slot_table, width), F32),
+            jax.ShapeDtypeStruct((slot_table, lanes), F32),
         ),
         in_specs=[smem, smem, vmem, vmem],
         out_specs=(vmem, vmem),
         compiler_params=params,
         name="route_leaves",
-    )(child_octant * parents.shape[0] + parent_slot, dest, child_m2l, stacked)
+    )(child_octant * parents.shape[0] + parent_slot, mine * capacity + rank, child_m2l, stacked)
     dens = lax.all_to_all(
-        packed_dens.reshape(n_dev, capacity, width), AXES, split_axis=0, concat_axis=0, tiled=True
-    ).reshape(slot_table, width)
+        packed_dens.reshape(n_dev, capacity, lanes), AXES, split_axis=0, concat_axis=0, tiled=True
+    ).reshape(slot_table, lanes)
 
     obs = obs_offset.transpose(1, 0, 2)
     pairs = slot_table * near_slots.shape[1] * points * points
@@ -359,21 +331,20 @@
         cost_estimate=pl.CostEstimate(flops=70 * pairs, bytes_accessed=5 * 10**6, transcendentals=pairs),
         name="near_field",
     )(near_slots.reshape(-1), recv, obs)
-    surface = jnp.asarray(surface_feats(width).T)
     potential = pl.pallas_call(
         far_kernel,
         out_shape=jax.ShapeDtypeStruct((slot_table, points), F32),
-        in_specs=[vmem, vmem, vmem, smem, vmem],
+        in_specs=[vmem, vmem, vmem, vmem],
         out_specs=vmem,
         scratch_shapes=[
-            pltpu.VMEM((slot_table, FEATS, points), BF16),
-            pltpu.VMEM((width, 128), F32),
-            pltpu.VMEM((GROUP * FEATS, points), F32),
+            pltpu.VMEM((lanes, points), F32),
+            pltpu.VMEM((3, points, points), F32),
+            pltpu.VMEM((points, points), F32),
         ],
         compiler_params=params,
         cost_estimate=pl.CostEstimate(flops=10**10, bytes_accessed=5 * 10**6, transcendentals=10**7),
         name="far_field",
-    )(dens, obs, near, live, surface)
+    )(dens, obs, near, live.reshape(slot_table // points, points))
     return (leaf_local, potential)
 
 

time: 268 us -> 218 us (0.81)
  Pallas kernels: 190 us -> 140 us
    pallas_call x1, Pallas kernels: 74.8 us -> 26.8 us  [on_device(): pl.pallas_call(far_kernel, out_shape=jax.ShapeDtypeStruct((slot_table, po...]
    unnamed x25 -> x23, local copies, waits for them, and re-layouts: 6.48 us -> 6.48 us
  transfers between devices with their start and end apart: 3 -> 3, of which waited for: 2 -> 2; matrix products, arithmetic and copies ran while one was open for 3% -> 4% of each run, Pallas kernels for 40% -> 49%
where the time goes in v3:
time: 218 us
  Pallas kernels  140 us (64%)
  waiting for transfers between devices  38 us (17%)
  starting transfers between devices  24 us (11%)
  local copies, waits for them, and re-layouts  8.55 us (4%)
  matrix products  6.23 us (3%)
    pallas_call x1, Pallas kernels, on_device(): pl.pallas_call(functools.partial(near_kernel, capacity, n_dev), out_shape...  103 us
    all_to_all x1, waiting for transfers between devices, on_device(): lax.all_to_all(packed.reshape(n_dev, block_rows, points), AXES, split_axi...  37.6 us
    pallas_call x1, Pallas kernels, on_device(): pl.pallas_call(far_kernel, out_shape=jax.ShapeDtypeStruct((slot_table, po...  26.8 us
    all_to_all x1, starting transfers between devices, on_device(): lax.all_to_all(packed_dens.reshape(n_dev, capacity, lanes), AXES, split_a...  14.5 us
    all_to_all x1, starting transfers between devices, on_device(): lax.all_to_all(packed.reshape(n_dev, block_rows, points), AXES, split_axi...  7.42 us
    unnamed x23, local copies, waits for them, and re-layouts  6.48 us
    dot_general x1, matrix products, on_device(): jnp.einsum('pr,oqr->opq', parents, l2l_ops, precision=lax.Precision.HIGHEST)  6.23 us
    pallas_call x1, Pallas kernels, on_device(): pl.pallas_call(functools.partial(pack_sources, capacity), out_shape=jax.S...  5.27 us
  transfers between devices with their start and end apart: 3, of which 2 were waited for; matrix products, arithmetic and copies ran while one was open for 4% of the time, Pallas kernels for 49%

profile of v3, /device:TPU:0, one launch (start us, length us, event | category | flops | bytes accessed | tf_op | source)
XLA Modules:
  0.0 217.8 jit_solution(10289458980485241788)
XLA Ops:
  0.6 0.8 dynamic_slice.3.owner_ref
  1.4 0.3 convert_reduce_fusion.rank_ref
  1.7 0.7 reshape.41.center_ref
  2.4 1.1 copy-done
  3.5 0.9 copy-done.1
  4.4 5.3 %pack_sources.1 = f32[4352,128]{1,0:T(8,128)} custom-call(s32[512]{0:T(512)S(1)} %dynamic_slice.3.owner_ref, s32[512]{0:T(512)S(1)} %convert_reduce_fusion.rank_ref, f32[1536]{0:T(1024)S(1)} %reshape.41.center_ref, f32[3,512,128]{2,1,0:T(8,128)S(1)} %bitcast.16, f32[512,128]{1,0:T(8,128)S(1)} %copy-done.1), custom_call_target="tpu_custom_call" | custom-call | tf_op jit(solution)/shard_map/pack_sources/pallas_call | solution.py:281
  9.7 7.4 %all-to-all-start.1 = ((f32[32,136,128]{2,1,0:T(8,128)}), f32[32,136,128]{2,1,0:T(8,128)}, u32[]{:S(2)}, u32[]{:S(2)}) async-start(f32[32,136,128]{2,1,0:T(8,128)} %bitcast.8), calls=%async_computation.1 | async-start | bytes 4456448 | tf_op jit(solution)/shard_map/all_to_all | solution.py:289
  17.2 2.1 collective-permute-start
  19.3 0.1 multiply_add_fusion.dest_ref
  19.4 0.3 copy.18.m2l_ref
  19.7 0.4 collective-permute-done
  20.1 6.2 %fusion.1 = f32[80,8,296]{2,0,1:T(8,128)S(1)} fusion(f32[8,296,296]{2,1,0:T(8,128)} %param.15, f32[64,296]{1,0:T(8,128)S(1)} %copy-done.5, f32[16,296]{1,0:T(8,128)S(1)} %collective-permute-done), kind=kOutput, calls=%fused_computation.4 | convolution fusion | flops 672914560 | bytes 3656192 | tf_op jit(solution)/shard_map/pr,oqr->opq/dot_general | solution.py:295
  26.4 4.9 %route_leaves.1 = (f32[512,296]{1,0:T(8,128)S(1)}, f32[1024,384]{1,0:T(8,128)}) custom-call(s32[512]{0:T(512)S(1)} %multiply_add_fusion.1.index_ref, s32[512]{0:T(512)S(1)} %multiply_add_fusion.dest_ref, f32[512,296]{1,0:T(8,128)S(1)} %copy.18.m2l_ref, f32[640,296]{1,0:T(8,128)S(1)} %bitcast.14), custom_call_target="tpu_custom_call" | custom-call | tf_op jit(solution)/shard_map/route_leaves/pallas_call | solution.py:297
  31.3 37.6 %all-to-all-done.1 = f32[32,136,128]{2,1,0:T(8,128)} async-done(((f32[32,136,128]{2,1,0:T(8,128)}), f32[32,136,128]{2,1,0:T(8,128)}, u32[]{:S(2)}, u32[]{:S(2)}) %all-to-all-start.1) | async-done | bytes 2228256 | tf_op jit(solution)/shard_map/all_to_all | solution.py:289
  68.9 14.5 %all-to-all-start = ((f32[32,32,384]{2,1,0:T(8,128)}), f32[32,32,384]{2,1,0:T(8,128)S(1)}, u32[]{:S(2)}, u32[]{:S(2)}) async-start(f32[32,32,384]{2,1,0:T(8,128)} %bitcast.19), calls=%async_computation | async-start | bytes 3145728 | tf_op jit(solution)/shard_map/all_to_all | solution.py:308
  83.4 0.2 copy.19
  83.6 0.3 reshape.40.slots_ref
  83.8 0.1 reduce_sum.19
  84.2 0.1 lt.43
  84.3 1.1 copy.20
  85.4 1.4 copy-done.2
  86.8 102.7 %near_field.1.near_ref = f32[1024,128]{1,0:T(8,128)S(1)} custom-call(s32[8192]{0:T(1024)S(1)} %reshape.40.slots_ref, f32[4352,128]{1,0:T(8,128)} %bitcast.9.recv_ref, f32[3,1024,128]{2,1,0:T(8,128)S(1)} %bitcast.17), custom_call_target="tpu_custom_call" | custom-call | flops 9395240960 | bytes 5000000 | tf_op jit(solution)/shard_map/near_field/pallas_call | solution.py:314
  189.6 1.4 copy-done.3
  191.0 26.8 %far_field.1 = f32[1024,128]{1,0:T(8,128)} custom-call(f32[1024,384]{1,0:T(8,128)S(1)} %bitcast.15, f32[3,1024,128]{2,1,0:T(8,128)S(1)} %bitcast.18, f32[1024,128]{1,0:T(8,128)S(1)} %near_field.1.near_ref, s32[8,128]{1,0:T(8,128)S(1)} %compare_convert_fusion.1.live_ref), custom_call_target="tpu_custom_call" | custom-call | flops 10000000000 | bytes 5000000 | tf_op jit(solution)/shard_map/far_field/pallas_call | solution.py:334
  (26 shorter events, 0.3 us)
Async XLA Ops:
  2.4 1.1 copy-start
  3.5 0.9 copy-start.1
  9.7 7.5 %copy-start.5 = (f32[64,296]{1,0:T(8,128)S(1)}, f32[64,296]{1,0:T(8,128)}, u32[]{:S(2)}) copy-start(f32[64,296]{1,0:T(8,128)} %param.11) | copy-start | bytes 227332
  9.7 9.6 %copy-start.8 = (s32[512]{0:T(512)S(1)}, s32[512]{0:T(512)}, u32[]{:S(2)}) copy-start(s32[512]{0:T(512)} %param.12) | copy-start | bytes 6148
  9.7 9.6 %copy-start.9 = (s32[512]{0:T(512)S(1)}, s32[512]{0:T(512)}, u32[]{:S(2)}) copy-start(s32[512]{0:T(512)} %param.13) | copy-start | bytes 6148
  9.7 9.6 %copy-start.6 = (s32[16384]{0:T(1024)S(1)}, s32[16384]{0:T(1024)}, u32[]{:S(2)}) copy-start(s32[16384]{0:T(1024)} %param.19) | copy-start | bytes 196612
  9.7 9.7 %copy-start.4 = (f32[512,296]{0,1:T(8,128)S(1)}, f32[512,296]{0,1:T(8,128)}, u32[]{:S(2)}) copy-start(f32[512,296]{0,1:T(8,128)} %param.14) | copy-start | bytes 1818628
  9.7 59.1 %all-to-all-start.1 = ((f32[32,136,128]{2,1,0:T(8,128)}), f32[32,136,128]{2,1,0:T(8,128)}, u32[]{:S(2)}, u32[]{:S(2)}) async-start(f32[32,136,128]{2,1,0:T(8,128)} %bitcast.8), calls=%async_computation.1 | async-start | bytes 4456448 | tf_op jit(solution)/shard_map/all_to_all | solution.py:289
  17.2 2.9 %collective-permute-start = (f32[16,296]{1,0:T(8,128)S(1)}, f32[16,296]{1,0:T(8,128)S(1)}, u32[]{:S(2)}, u32[]{:S(2)}) collective-permute-start(f32[16,296]{1,0:T(8,128)S(1)} %slice.3), channel_id=1, source_target_pairs={{0,1},{1,2},{2,3},{3,4},{4,5},{5,6},{6,7},{7,8},{8,9},{9,10},{10,1... | collective-permute-start | bytes 56840 | tf_op jit(solution)/shard_map/ppermute | solution.py:30
  26.3 57.0 %copy-start.7 = (s32[1024,8]{0,1:T(8,128)S(1)}, s32[1024,8]{0,1:T(8,128)}, u32[]{:S(2)}) copy-start(s32[1024,8]{0,1:T(8,128)} %param.21) | copy-start | bytes 98308
  68.9 120.7 %all-to-all-start = ((f32[32,32,384]{2,1,0:T(8,128)}), f32[32,32,384]{2,1,0:T(8,128)S(1)}, u32[]{:S(2)}, u32[]{:S(2)}) async-start(f32[32,32,384]{2,1,0:T(8,128)} %bitcast.19), calls=%async_computation | async-start | bytes 3145728 | tf_op jit(solution)/shard_map/all_to_all | solution.py:308
  85.4 1.4 copy-start.2
  189.5 1.4 copy-start.3

commit v4 on v3

--- a/solution.py
+++ b/solution.py
@@ -70,14 +70,6 @@
 
 def clear_stage(stage_ref):
     stage_ref[...] = jnp.zeros_like(stage_ref)
-
-
-def lane_sums(block):
-    high = block.astype(BF16)
-    low = (block - high.astype(F32)).astype(BF16)
-    ones = jnp.ones((GROUP, 2 * block.shape[1]), BF16)
-    pieces = jnp.concatenate([high, low], axis=1)
-    return lax.dot_general(ones, pieces, (((1,), (1,)), ((), ())), preferred_element_type=F32)
 
 
 def pack_sources(capacity, owner_ref, rank_ref, center_ref, coords_ref, charge_ref, out_ref):
@@ -133,7 +125,8 @@
 ):
     rows = 4 * capacity + 8
     blocks = out_ref.shape[0] // GROUP
-    sub = lax.broadcasted_iota(jnp.int32, (GROUP, out_ref.shape[1]), 0)
+    side = out_ref.shape[1]
+    lane = lax.broadcasted_iota(jnp.int32, (side, side), 1)
     clear_stage(stage_a)
     clear_stage(stage_b)
 
@@ -177,14 +170,26 @@
             total = part if total is None else total + part
         total_ref[u] = total
 
+    def put_sums(block, total_ref):
+        tile, column = block * GROUP // side, lax.rem(block * GROUP, side)
+        place = pl.ds(pl.multiple_of(tile * side, side), side)
+
+        def add_row(sums, u):
+            row = jnp.sum(total_ref[u], axis=1, keepdims=True)
+            return jnp.where(lane == column + u, row, sums)
+
+        def finish(sums):
+            out_ref[place, :] = sums
+
+        return out_ref[place, :], add_row, finish
+
     def half(before, block, after, left_now, left_next, total_before, total_now):
-        sums = None
+        sums, add_row, finish = put_sums(before, total_before)
         for u in range(GROUP):
             turn(after, u, left_next)
             pair_work(block, u, left_now, total_now)
-            part = lane_sums(total_before[u])
-            sums = part if sums is None else jnp.where(sub == u, part, sums)
-        out_ref[pl.ds(pl.multiple_of(before * GROUP, GROUP), GROUP), :] = sums
+            sums = add_row(sums, u)
+        finish(sums)
 
     for u in range(GROUP):
         turn(0, u, left_a)
@@ -197,11 +202,10 @@
         return carry
 
     lax.fori_loop(0, blocks // 2, step, 0)
-    sums = None
+    sums, add_row, finish = put_sums(blocks - 1, total_b)
     for u in range(GROUP):
-        part = lane_sums(total_b[u])
-        sums = part if sums is None else jnp.where(sub == u, part, sums)
-    out_ref[pl.ds((blocks - 1) * GROUP, GROUP), :] = sums
+        sums = add_row(sums, u)
+    finish(sums)
 
 
 def far_kernel(dens_ref, obs_ref, near_ref, live_ref, out_ref, turned_ref, point_ref, far_ref):
@@ -238,7 +242,7 @@
             return carry
 
         lax.fori_loop(0, side // GROUP, points, 0)
-        near = near_ref[pl.ds(first, side), :].T
+        near = near_ref[pl.ds(first, side), :]
         total = far_ref[...] * (1.0 / (FOUR_PI * HALF_WIDTH)) + near * (1.0 / FOUR_PI)
         total = jnp.where(live_ref[pl.ds(t, 1), :] > 0, total, 0.0)
         out_ref[pl.ds(first, side), :] = total.T
@@ -278,6 +282,7 @@
     leaf_at = jnp.arange(leaf_dev, dtype=jnp.int32)
     same = (mine[:, None] == mine[None, :]) & (leaf_at[None, :] < leaf_at[:, None])
     rank = jnp.sum(same.astype(jnp.int32), axis=1)
+    rim_rows = from_behind(parent_local[parent_local.shape[0] - RIM :], AXES, 1)
     packed = pl.pallas_call(
         functools.partial(pack_sources, capacity),
         out_shape=jax.ShapeDtypeStruct((n_dev * block_rows, points), F32),
@@ -286,11 +291,11 @@
         compiler_params=params,
         name="pack_sources",
     )(mine, rank, leaf_center.T.reshape(-1), src_coords.transpose(1, 0, 2), src_charge)
+    packed, rim_rows = lax.optimization_barrier((packed, rim_rows))
     recv = lax.all_to_all(
         packed.reshape(n_dev, block_rows, points), AXES, split_axis=0, concat_axis=0, tiled=True
     ).reshape(n_dev * block_rows, points)
 
-    rim_rows = from_behind(parent_local[parent_local.shape[0] - RIM :], AXES, 1)
     parents = jnp.concatenate([rim_rows, parent_local], axis=0)
     moved = jnp.einsum("pr,oqr->opq", parents, l2l_ops, precision=lax.Precision.HIGHEST)
     stacked = moved.reshape(8 * parents.shape[0], width)

time: 218 us -> 214 us (0.982)
  starting transfers between devices: 24 us -> 13.6 us
  Pallas kernels: 140 us -> 143 us
    all_to_all x1, starting transfers between devices: 14.5 us -> 4.01 us  [on_device(): lax.all_to_all(packed_dens.reshape(n_dev, capacity, lanes), AXES, split_a...]
    pallas_call x1, Pallas kernels: 103 us -> 106 us  [on_device(): pl.pallas_call(functools.partial(near_kernel, capacity, n_dev), out_shape...]
    all_to_all x1, waiting for transfers between devices: 37.6 us -> 40.1 us  [on_device(): lax.all_to_all(packed.reshape(n_dev, block_rows, points), AXES, split_axi...]
  transfers between devices with their start and end apart: 3 -> 3, of which waited for: 2 -> 1; matrix products, arithmetic and copies ran while one was open for 4% -> 5% of each run, Pallas kernels for 49% -> 55%
where the time goes in v4:
time: 214 us; the launch traced here: 213 us
  Pallas kernels  143 us (67%)
  waiting for transfers between devices  40.1 us (19%)
  starting transfers between devices  13.6 us (6%)
  local copies, waits for them, and re-layouts  9.26 us (4%)
  matrix products  6.23 us (3%)
    pallas_call x1, Pallas kernels, on_device(): pl.pallas_call(functools.partial(near_kernel, capacity, n_dev), out_shape...  106 us
    all_to_all x1, waiting for transfers between devices, on_device(): lax.all_to_all(packed.reshape(n_dev, block_rows, points), AXES, split_axi...  40.1 us
    pallas_call x1, Pallas kernels, on_device(): pl.pallas_call(far_kernel, out_shape=jax.ShapeDtypeStruct((slot_table, po...  26.4 us
    all_to_all x1, starting transfers between devices, on_device(): lax.all_to_all(packed.reshape(n_dev, block_rows, points), AXES, split_axi...  7.25 us
    unnamed x23, local copies, waits for them, and re-layouts  6.46 us
    dot_general x1, matrix products, on_device(): jnp.einsum('pr,oqr->opq', parents, l2l_ops, precision=lax.Precision.HIGHEST)  6.23 us
    pallas_call x1, Pallas kernels, on_device(): pl.pallas_call(functools.partial(pack_sources, capacity), out_shape=jax.S...  5.26 us
    pallas_call x1, Pallas kernels, on_device(): pl.pallas_call(route_leaves, out_shape=(jax.ShapeDtypeStruct((leaf_dev, w...  4.94 us
  transfers between devices with their start and end apart: 3, of which 1 were waited for; matrix products, arithmetic and copies ran while one was open for 5% of the time, Pallas kernels for 55%

profile of v4, /device:TPU:0, one launch (start us, length us, event | category | flops | bytes accessed | tf_op | source)
XLA Modules:
  0.0 213.2 jit_solution(18027265469957372849)
XLA Ops:
  0.6 0.7 slice.3
  1.4 2.3 %collective-permute-start = (f32[16,296]{1,0:T(8,128)S(1)}, f32[16,296]{1,0:T(8,128)S(1)}, u32[]{:S(2)}, u32[]{:S(2)}) collective-permute-start(f32[16,296]{1,0:T(8,128)S(1)} %slice.3), channel_id=1, source_target_pairs={{0,1},{1,2},{2,3},{3,4},{4,5},{5,6},{6,7},{7,8},{8,9},{9,10},{10,1... | collective-permute-start | bytes 56840 | tf_op jit(solution)/shard_map/ppermute | solution.py:30
  3.7 0.8 dynamic_slice.3.owner_ref
  4.5 0.3 convert_reduce_fusion.rank_ref
  4.7 0.7 reshape.37.center_ref
  5.5 1.1 copy-done
  6.6 0.9 copy-done.1
  7.5 5.3 %pack_sources.1 = f32[4352,128]{1,0:T(8,128)} custom-call(s32[512]{0:T(512)S(1)} %dynamic_slice.3.owner_ref, s32[512]{0:T(512)S(1)} %convert_reduce_fusion.rank_ref, f32[1536]{0:T(1024)S(1)} %reshape.37.center_ref, f32[3,512,128]{2,1,0:T(8,128)S(1)} %bitcast.16, f32[512,128]{1,0:T(8,128)S(1)} %copy-done.1), custom_call_target="tpu_custom_call" | custom-call | tf_op jit(solution)/shard_map/pack_sources/pallas_call | solution.py:286
  12.9 7.3 %all-to-all-start.1 = ((f32[32,136,128]{2,1,0:T(8,128)}), f32[32,136,128]{2,1,0:T(8,128)}, u32[]{:S(2)}, u32[]{:S(2)}) async-start(f32[32,136,128]{2,1,0:T(8,128)} %bitcast.8), calls=%async_computation.1 | async-start | bytes 4456448 | tf_op jit(solution)/shard_map/all_to_all | solution.py:295
  20.1 0.3 copy.18.m2l_ref
  20.4 0.1 multiply_add_fusion
  20.5 6.2 %fusion.1 = f32[80,8,296]{2,0,1:T(8,128)S(1)} fusion(f32[8,296,296]{2,1,0:T(8,128)} %param.15, f32[64,296]{1,0:T(8,128)S(1)} %copy-done.5, f32[16,296]{1,0:T(8,128)S(1)} %collective-permute-done), kind=kOutput, calls=%fused_computation.4 | convolution fusion | flops 672914560 | bytes 3656192 | tf_op jit(solution)/shard_map/pr,oqr->opq/dot_general | solution.py:300
  26.8 4.9 %route_leaves.1 = (f32[512,296]{1,0:T(8,128)S(1)}, f32[1024,384]{1,0:T(8,128)}) custom-call(s32[512]{0:T(512)S(1)} %get-tuple-element.17.index_ref, s32[512]{0:T(512)S(1)} %get-tuple-element.16.dest_ref, f32[512,296]{1,0:T(8,128)S(1)} %copy.18.m2l_ref, f32[640,296]{1,0:T(8,128)S(1)} %bitcast.14), custom_call_target="tpu_custom_call" | custom-call | tf_op jit(solution)/shard_map/route_leaves/pallas_call | solution.py:302
  31.7 40.1 %all-to-all-done.1 = f32[32,136,128]{2,1,0:T(8,128)} async-done(((f32[32,136,128]{2,1,0:T(8,128)}), f32[32,136,128]{2,1,0:T(8,128)}, u32[]{:S(2)}, u32[]{:S(2)}) %all-to-all-start.1) | async-done | bytes 2228256 | tf_op jit(solution)/shard_map/all_to_all | solution.py:295
  71.8 4.0 %all-to-all-start = ((f32[32,32,384]{2,1,0:T(8,128)}), f32[32,32,384]{2,1,0:T(8,128)S(1)}, u32[]{:S(2)}, u32[]{:S(2)}) async-start(f32[32,32,384]{2,1,0:T(8,128)} %bitcast.19), calls=%async_computation | async-start | bytes 3145728 | tf_op jit(solution)/shard_map/all_to_all | solution.py:313
  75.9 0.1 lt.43
  76.0 0.1 reduce_sum.19
  76.3 0.2 copy.19
  76.5 0.3 reshape.41.slots_ref
  76.8 1.1 copy.20
  77.9 1.4 copy-done.2
  79.3 106.2 %near_field.1.near_ref = f32[1024,128]{1,0:T(8,128)S(1)} custom-call(s32[8192]{0:T(1024)S(1)} %reshape.41.slots_ref, f32[4352,128]{1,0:T(8,128)} %bitcast.9.recv_ref, f32[3,1024,128]{2,1,0:T(8,128)S(1)} %bitcast.17), custom_call_target="tpu_custom_call" | custom-call | flops 9395240960 | bytes 5000000 | tf_op jit(solution)/shard_map/near_field/pallas_call | solution.py:319
  185.5 1.4 copy-done.3
  186.9 26.4 %far_field.1 = f32[1024,128]{1,0:T(8,128)} custom-call(f32[1024,384]{1,0:T(8,128)S(1)} %bitcast.15, f32[3,1024,128]{2,1,0:T(8,128)S(1)} %bitcast.18, f32[1024,128]{1,0:T(8,128)S(1)} %near_field.1.near_ref, s32[8,128]{1,0:T(8,128)S(1)} %compare_convert_fusion.1.live_ref), custom_call_target="tpu_custom_call" | custom-call | flops 10000000000 | bytes 5000000 | tf_op jit(solution)/shard_map/far_field/pallas_call | solution.py:339
  (25 shorter events, 0.3 us)
Async XLA Ops:
  1.4 11.4 %collective-permute-start = (f32[16,296]{1,0:T(8,128)S(1)}, f32[16,296]{1,0:T(8,128)S(1)}, u32[]{:S(2)}, u32[]{:S(2)}) collective-permute-start(f32[16,296]{1,0:T(8,128)S(1)} %slice.3), channel_id=1, source_target_pairs={{0,1},{1,2},{2,3},{3,4},{4,5},{5,6},{6,7},{7,8},{8,9},{9,10},{10,1... | collective-permute-start | bytes 56840 | tf_op jit(solution)/shard_map/ppermute | solution.py:30
  5.5 1.1 copy-start
  6.6 0.9 copy-start.1
  12.8 7.3 %copy-start.4 = (f32[512,296]{0,1:T(8,128)S(1)}, f32[512,296]{0,1:T(8,128)}, u32[]{:S(2)}) copy-start(f32[512,296]{0,1:T(8,128)} %param.14) | copy-start | bytes 1818628
  12.8 7.6 %copy-start.6 = (s32[16384]{0:T(1024)S(1)}, s32[16384]{0:T(1024)}, u32[]{:S(2)}) copy-start(s32[16384]{0:T(1024)} %param.19) | copy-start | bytes 196612
  12.8 7.6 %copy-start.8 = (s32[512]{0:T(512)S(1)}, s32[512]{0:T(512)}, u32[]{:S(2)}) copy-start(s32[512]{0:T(512)} %param.12) | copy-start | bytes 6148
  12.8 7.6 %copy-start.9 = (s32[512]{0:T(512)S(1)}, s32[512]{0:T(512)}, u32[]{:S(2)}) copy-start(s32[512]{0:T(512)} %param.13) | copy-start | bytes 6148
  12.8 7.7 %copy-start.5 = (f32[64,296]{1,0:T(8,128)S(1)}, f32[64,296]{1,0:T(8,128)}, u32[]{:S(2)}) copy-start(f32[64,296]{1,0:T(8,128)} %param.11) | copy-start | bytes 227332
  12.9 59.0 %all-to-all-start.1 = ((f32[32,136,128]{2,1,0:T(8,128)}), f32[32,136,128]{2,1,0:T(8,128)}, u32[]{:S(2)}, u32[]{:S(2)}) async-start(f32[32,136,128]{2,1,0:T(8,128)} %bitcast.8), calls=%async_computation.1 | async-start | bytes 4456448 | tf_op jit(solution)/shard_map/all_to_all | solution.py:295
  26.7 49.6 %copy-start.7 = (s32[1024,8]{0,1:T(8,128)S(1)}, s32[1024,8]{0,1:T(8,128)}, u32[]{:S(2)}) copy-start(s32[1024,8]{0,1:T(8,128)} %param.21) | copy-start | bytes 98308
  71.8 113.6 %all-to-all-start = ((f32[32,32,384]{2,1,0:T(8,128)}), f32[32,32,384]{2,1,0:T(8,128)S(1)}, u32[]{:S(2)}, u32[]{:S(2)}) async-start(f32[32,32,384]{2,1,0:T(8,128)} %bitcast.19), calls=%async_computation | async-start | bytes 3145728 | tf_op jit(solution)/shard_map/all_to_all | solution.py:313
  77.9 1.4 copy-start.2
  185.4 1.4 copy-start.3

commit v5 on v3

v5 whole, which is shorter than its diff:
```python
import functools
import math

import jax
import jax.numpy as jnp
import numpy as np
from jax import lax
from jax.experimental import pallas as pl
from jax.experimental.pallas import tpu as pltpu
from jax.sharding import PartitionSpec as P

ORDER = 8
RIM = 16
RADIUS = 2.95
HALF_WIDTH = 0.5
SOFT_SQ = 0.0025
FOUR_PI = 4.0 * math.pi
AXES = ("grp", "dom")
FEATS = 32
GROUP = 8
VMEM_LIMIT = 50 * 1024 * 1024

F32 = jnp.float32
BF16 = jnp.bfloat16


def from_behind(block, axis, distance):
    devices = range(lax.axis_size(axis))
    route = [(i - distance, i) for i in devices if i - distance in devices]
    return lax.ppermute(block, axis, route)


def surface_grid():
    axis = (np.linspace(-1.0, 1.0, ORDER) * RADIUS).astype(np.float32)
    ends = (0, ORDER - 1)
    points = [
        (i, j, k)
        for i in range(ORDER)
        for j in range(ORDER)
        for k in range(ORDER)
        if i in ends or j in ends or k in ends
    ]
    return [float(value) for value in axis], points


def split(value):
    high = value.astype(BF16).astype(F32)
    rest = value - high
    mid = rest.astype(BF16).astype(F32)
    return high, mid, rest - mid


def sub_of(shape):
    return lax.broadcasted_iota(jnp.int32, shape, 0)


def stack_rows(x, y, z):
    place = sub_of((GROUP, x.shape[1])) % 4
    return jnp.where(place == 0, x, jnp.where(place == 1, y, z))


def norm_rows(points, extra):
    place = sub_of(points.shape) % 4
    squares = jnp.where(place == 3, extra, points * points)
    squares = squares + pltpu.roll(squares, 1, 0)
    return squares + pltpu.roll(squares, 2, 0)


def put_rows(pair, third, last):
    sub = sub_of(pair[0].shape)
    block = jnp.where(sub < 4, pair[0], pair[1])
    return jnp.where(sub == 3, third, jnp.where(sub == 7, last, block))


def source_pieces(points):
    high, mid, low = split(points)
    n_high, n_mid, n_low = split(norm_rows(points, 0.0))
    return jnp.concatenate(
        [
            put_rows((high, high), 1.0, 1.0),
            put_rows((high, mid), 1.0, n_high),
            put_rows((mid, low), n_mid, n_low),
            jnp.zeros_like(points),
        ],
        axis=0,
    ).astype(BF16)


def target_pieces(points):
    high, mid, low = split(-2.0 * points)
    n_high, n_mid, n_low = split(norm_rows(points, SOFT_SQ))
    return jnp.concatenate(
        [
            put_rows((high, mid), n_high, n_mid),
            put_rows((low, high), n_low, 1.0),
            put_rows((mid, high), 1.0, 1.0),
            jnp.zeros_like(points),
        ],
        axis=0,
    ).astype(BF16)


def lane_sums(block):
    high = block.astype(BF16)
    low = (block - high.astype(F32)).astype(BF16)
    ones = jnp.ones((GROUP, 2 * block.shape[1]), BF16)
    pieces = jnp.concatenate([high, low], axis=1)
    return lax.dot_general(ones, pieces, (((1,), (1,)), ((), ())), preferred_element_type=F32)


def pack_sources(capacity, owner_ref, rank_ref, center_ref, coords_ref, charge_ref, first_ref, second_ref, packed_ref):
    rows = 2 * capacity + 8
    leaves, points = charge_ref.shape
    n_dev = first_ref.shape[0] // rows
    lane = lax.broadcasted_iota(jnp.int32, (GROUP, points), 1)
    sub = sub_of((GROUP, points)) % 4

    def step(j, carry):
        owner, rank = owner_ref[j], rank_ref[j]
        base = owner * 4 * capacity + rank
        for c in range(3):
            packed_ref[pl.ds(base + c * capacity, 1), :] = coords_ref[c, pl.ds(j, 1), :]
        packed_ref[pl.ds(base + 3 * capacity, 1), :] = charge_ref[pl.ds(j, 1), :]
        place = pl.ds(pl.multiple_of(owner * rows + 2 * capacity, GROUP), GROUP)
        value = jnp.where(
            sub == 0,
            center_ref[j],
            jnp.where(sub == 1, center_ref[leaves + j], center_ref[2 * leaves + j]),
        )
        first_ref[place, :] = jnp.where(lane == rank, value, first_ref[place, :])
        return carry

    lax.fori_loop(0, leaves, step, 0, unroll=4)

    def halves(d, carry):
        for pair in range(2):
            for g in range(0, capacity, GROUP):
                at = d * 4 * capacity + 2 * pair * capacity + g
                left = packed_ref[pl.ds(pl.multiple_of(at, GROUP), GROUP), :]
                right = packed_ref[pl.ds(pl.multiple_of(at + capacity, GROUP), GROUP), :]
                place = pl.ds(pl.multiple_of(d * rows + pair * capacity + g, GROUP), GROUP)
                first_ref[place, :] = jnp.where(
                    lane < points // 2, left, pltpu.roll(right, points // 2, 1)
                )
                place = pl.ds(pl.multiple_of((2 * d + pair) * capacity + g, GROUP), GROUP)
                second_ref[place, :] = jnp.where(
                    lane < points // 2, pltpu.roll(left, points // 2, 1), right
                )
        return carry

    lax.fori_loop(0, n_dev, halves, 0)


def route_leaves(index_ref, dest_ref, m2l_ref, moved_ref, leaf_ref, out_ref):
    def step(j, carry):
        row = m2l_ref[pl.ds(j, 1), :] + moved_ref[pl.ds(index_ref[j], 1), :]
        leaf_ref[pl.ds(j, 1), :] = row
        out_ref[pl.ds(dest_ref[j], 1), : row.shape[1]] = row
        return carry

    lax.fori_loop(0, m2l_ref.shape[0], step, 0, unroll=4)


def near_kernel(
    capacity,
    n_dev,
    rows,
    center_rows,
    slots_ref,
    recv_ref,
    center_ref,
    obs_ref,
    out_ref,
    source_ref,
    charge_ref,
    stage_ref,
    left_a,
    left_b,
    total_a,
    total_b,
):
    points = out_ref.shape[1]
    half = points // 2
    blocks = out_ref.shape[0] // GROUP
    sub = sub_of((GROUP, points))
    low = lax.broadcasted_iota(jnp.int32, (GROUP, points), 1) < half
    low_row = lax.broadcasted_iota(jnp.int32, (1, points), 1) < half
    low_block = lax.broadcasted_iota(jnp.int32, (FEATS, points), 1).astype(F32).astype(BF16) < half

    def both(value):
        turned = pltpu.roll(value, half, 1)
        return jnp.where(low, value, turned), jnp.where(low, turned, value)

    def prepare(s, carry):
        for g in range(0, capacity, GROUP):
            slot = pl.multiple_of(s * capacity + g, GROUP)
            at = pl.multiple_of(s * rows + g, GROUP)
            x, y = both(recv_ref[pl.ds(at, GROUP), :])
            z, charge = both(recv_ref[pl.ds(at + capacity, GROUP), :])
            charge_ref[pl.ds(slot, GROUP), :] = charge
            for c, value in enumerate((x, y, z)):
                stage_ref[pl.ds(3 * g + c * GROUP, GROUP), :] = value - 1.0
            for u in range(GROUP):
                parts = [stage_ref[pl.ds(3 * g + c * GROUP + u, 1), :] for c in range(3)]
                source_ref[slot + u] = source_pieces(stack_rows(*parts))
        return carry

    lax.fori_loop(0, n_dev, prepare, 0)

    def block_centers(block):
        dev = block * GROUP // capacity
        place = pl.ds(pl.multiple_of(dev * center_rows + 2 * capacity, GROUP), GROUP)
        column = block * GROUP - dev * capacity
        return pltpu.roll(center_ref[place, :], lax.rem(points - column, points), 1)

    def turn(block, centers, u, left_ref):
        parts = [obs_ref[c, pl.ds(block * GROUP + u, 1), :] for c in range(3)]
        targets = (centers[:, u : u + 1] - 1.0) + HALF_WIDTH * stack_rows(*parts)
        left_ref[u] = target_pieces(targets).T

    def pair_work(block, u, left_ref, total_ref):
        left = left_ref[u]
        at = (block * GROUP + u) * GROUP
        total = None
        for p in range(2):
            index = [slots_ref[at + 4 * p + n] for n in range(4)]
            sources, charges = [], []
            for n in (0, 2):
                one, two = index[n], index[n + 1]
                sources.append(jnp.where(low_block, source_ref[one], source_ref[two]))
                charges.append(
                    jnp.where(low_row, charge_ref[pl.ds(one, 1), :], charge_ref[pl.ds(two, 1), :])
                )
            right = jnp.concatenate(sources, axis=1)
            inverse = lax.rsqrt(jnp.dot(left, right, preferred_element_type=F32))
            part = inverse[:, :points] * charges[0] + inverse[:, points:] * charges[1]
            total = part if total is None else total + part
        total_ref[u] = total

    def half_step(before, block, after, left_now, left_next, total_before, total_now):
        sums = None
        centers = block_centers(after)
        for u in range(GROUP):
            turn(after, centers, u, left_next)
            pair_work(block, u, left_now, total_now)
            part = lane_sums(total_before[u])
            sums = part if sums is None else jnp.where(sub == u, part, sums)
        out_ref[pl.ds(pl.multiple_of(before * GROUP, GROUP), GROUP), :] = sums

    centers = block_centers(0)
    for u in range(GROUP):
        turn(0, centers, u, left_a)
    total_b[...] = jnp.zeros_like(total_b)

    def step(i, carry):
        one, two = 2 * i, 2 * i + 1
        half_step(jnp.maximum(one - 1, 0), one, two, left_a, left_b, total_b, total_a)
        half_step(one, two, jnp.minimum(two + 1, blocks - 1), left_b, left_a, total_a, total_b)
        return carry

    lax.fori_loop(0, blocks // 2, step, 0)
    sums = None
    for u in range(GROUP):
        part = lane_sums(total_b[u])
        sums = part if sums is None else jnp.where(sub == u, part, sums)
    out_ref[pl.ds((blocks - 1) * GROUP, GROUP), :] = sums


def far_kernel(dens_ref, obs_ref, near_ref, near_too_ref, live_ref, out_ref, turned_ref, point_ref, far_ref):
    axis, surface = surface_grid()
    number = {point: q for q, point in enumerate(surface)}
    side = out_ref.shape[1]

    def tile(t, carry):
        first = pl.multiple_of(t * side, side)
        for column in range(0, dens_ref.shape[1], side):
            turned_ref[pl.ds(column, side), :] = dens_ref[pl.ds(first, side), pl.ds(column, side)].T
        for c in range(3):
            point_ref[c] = obs_ref[c, pl.ds(first, side), :].T

        def points(b, carry):
            place = pl.ds(pl.multiple_of(b * GROUP, GROUP), GROUP)
            squares = []
            for c in range(3):
                value = point_ref[c, place, :]
                squares.append([(value - at) * (value - at) for at in axis])
            totals = [jnp.zeros((GROUP, side), F32) for _ in range(4)]
            turn = 0
            for j in range(ORDER):
                for k in range(ORDER):
                    partial = squares[1][j] + squares[2][k]
                    for i in range(ORDER):
                        q = number.get((i, j, k))
                        if q is None:
                            continue
                        inverse = lax.rsqrt(squares[0][i] + partial)
                        totals[turn] = totals[turn] + inverse * turned_ref[pl.ds(q, 1), :]
                        turn = (turn + 1) % 4
            far_ref[place, :] = (totals[0] + totals[1]) + (totals[2] + totals[3])
            return carry

        lax.fori_loop(0, side // GROUP, points, 0)
        near = (near_ref[pl.ds(first, side), :] + near_too_ref[pl.ds(first, side), :]).T
        total = far_ref[...] * (1.0 / (FOUR_PI * HALF_WIDTH)) + near * (1.0 / FOUR_PI)
        total = jnp.where(live_ref[pl.ds(t, 1), :] > 0, total, 0.0)
        out_ref[pl.ds(first, side), :] = total.T
        return carry

    lax.fori_loop(0, out_ref.shape[0] // side, tile, 0)


def on_device(
    parent_local,
    parent_slot,
    child_octant,
    child_m2l,
    l2l_ops,
    leaf_center,
    src_coords,
    src_charge,
    obs_owner,
    obs_offset,
    near_slots,
):
    n_dev = lax.axis_size(AXES)
    leaf_dev, width = child_m2l.shape
    slot_table = obs_offset.shape[0]
    points = obs_offset.shape[2]
    capacity = slot_table // n_dev
    block_rows = 2 * capacity + 8
    lanes = -(-width // points) * points
    my_index = lax.axis_index(AXES)
    vmem, smem = pl.BlockSpec(memory_space=pltpu.VMEM), pl.BlockSpec(memory_space=pltpu.SMEM)
    params = pltpu.CompilerParams(vmem_limit_bytes=VMEM_LIMIT)

    mine = lax.dynamic_slice_in_dim(obs_owner, my_index * leaf_dev, leaf_dev)
    counts = jnp.sum((obs_owner.reshape(n_dev, leaf_dev) == my_index).astype(jnp.int32), axis=1)
    live = (jnp.arange(capacity, dtype=jnp.int32)[None, :] < counts[:, None]).astype(jnp.int32).reshape(slot_table)

    leaf_at = jnp.arange(leaf_dev, dtype=jnp.int32)
    same = (mine[:, None] == mine[None, :]) & (leaf_at[None, :] < leaf_at[:, None])
    rank = jnp.sum(same.astype(jnp.int32), axis=1)
    rim_rows = from_behind(parent_local[parent_local.shape[0] - RIM :], AXES, 1)
    rim_rows = from_behind(parent_local[parent_local.shape[0] - RIM :], AXES, 1)
    first_part, second_part = pl.pallas_call(
        functools.partial(pack_sources, capacity),
        out_shape=(
            jax.ShapeDtypeStruct((n_dev * block_rows, points), F32),
            jax.ShapeDtypeStruct((slot_table * 2, points), F32),
        ),
        in_specs=[smem, smem, smem, vmem, vmem],
        out_specs=(vmem, vmem),
        scratch_shapes=[pltpu.VMEM((slot_table * 4, points), F32)],
        compiler_params=params,
        name="pack_sources",
    )(mine, rank, leaf_center.T.reshape(-1), src_coords.transpose(1, 0, 2), src_charge)
    first_part, rim_rows = lax.optimization_barrier((first_part, rim_rows))

    def exchange(packed):
        blocks = packed.reshape(n_dev, -1, packed.shape[1])
        got = lax.all_to_all(blocks, AXES, split_axis=0, concat_axis=0, tiled=True)
        return got.reshape(packed.shape)

    first_recv = exchange(first_part)
    second_part, first_recv = lax.optimization_barrier((second_part, first_recv))
    second_recv = exchange(second_part)
    parents = jnp.concatenate([rim_rows, parent_local], axis=0)
    moved = jnp.einsum("pr,oqr->opq", parents, l2l_ops, precision=lax.Precision.HIGHEST)
    stacked = moved.reshape(8 * parents.shape[0], width)
    leaf_local, packed_dens = pl.pallas_call(
        route_leaves,
        out_shape=(
            jax.ShapeDtypeStruct((leaf_dev, width), F32),
            jax.ShapeDtypeStruct((slot_table, lanes), F32),
        ),
        in_specs=[smem, smem, vmem, vmem],
        out_specs=(vmem, vmem),
        compiler_params=params,
        name="route_leaves",
    )(child_octant * parents.shape[0] + parent_slot, mine * capacity + rank, child_m2l, stacked)
    packed_dens, second_recv = lax.optimization_barrier((packed_dens, second_recv))
    dens = exchange(packed_dens)

    obs = obs_offset.transpose(1, 0, 2)
    slots = near_slots.reshape(-1)
    pairs = slot_table * near_slots.shape[1] * points * points // 2

    def near_part(recv, name):
        return pl.pallas_call(
            functools.partial(near_kernel, capacity, n_dev, recv.shape[0] // n_dev, block_rows),
            out_shape=jax.ShapeDtypeStruct((slot_table, points), F32),
            in_specs=[smem, vmem, vmem, vmem],
            out_specs=vmem,
            scratch_shapes=[
                pltpu.VMEM((slot_table, FEATS, points), BF16),
                pltpu.VMEM((slot_table, points), F32),
                pltpu.VMEM((3 * capacity, points), F32),
                pltpu.VMEM((GROUP, points, FEATS), BF16),
                pltpu.VMEM((GROUP, points, FEATS), BF16),
                pltpu.VMEM((GROUP, points, points), F32),
                pltpu.VMEM((GROUP, points, points), F32),
            ],
            compiler_params=params,
            cost_estimate=pl.CostEstimate(
                flops=70 * pairs, bytes_accessed=5 * 10**6, transcendentals=pairs
            ),
            name=name,
        )(slots, recv, first_recv, obs)

    near = near_part(first_recv, "near_first")
    near_too = near_part(second_recv, "near_second")
    potential = pl.pallas_call(
        far_kernel,
        out_shape=jax.ShapeDtypeStruct((slot_table, points), F32),
        in_specs=[vmem, vmem, vmem, vmem, vmem],
        out_specs=vmem,
        scratch_shapes=[
            pltpu.VMEM((lanes, points), F32),
            pltpu.VMEM((3, points, points), F32),
            pltpu.VMEM((points, points), F32),
        ],
        compiler_params=params,
        cost_estimate=pl.CostEstimate(flops=10**10, bytes_accessed=5 * 10**6, transcendentals=10**7),
        name="far_field",
    )(dens, obs, near, near_too, live.reshape(slot_table // points, points))
    return (leaf_local, potential)


def solution(mesh):
    placed = (
        P(AXES, None),
        P(AXES),
        P(AXES),
        P(AXES, None),
        P(),
        P(AXES, None),
        P(AXES, None, None),
        P(AXES, None),
        P(),
        P(AXES, None, None),
        P(AXES, None),
    )
    return jax.shard_map(
        on_device,
        mesh=mesh,
        in_specs=placed,
        out_specs=(P(AXES, None), P(AXES, None)),
        check_vma=False,
    )
```

time: 218 us -> 268 us (1.23)
  blocking collectives: 0 us -> 37.6 us
  Pallas kernels: 140 us -> 177 us
  waiting for transfers between devices: 38 us -> 14 us
  starting transfers between devices: 24 us -> 9.43 us
  local copies, waits for them, and re-layouts: 8.55 us -> 17 us
  other arithmetic: 0.47 us -> 4.14 us
    all_to_all x0 -> x1, blocking collectives: none -> 37.6 us  [exchange(): got = lax.all_to_all(blocks, AXES, split_axis=0, concat_axis=0, tiled=True)]
    pallas_call x2 -> x3, Pallas kernels: 108 us -> 144 us  [the longest x2 137 us: near_part(): pl.pallas_call(functools.partial(near_kernel, capacity, n_dev, recv.shape...]
    all_to_all x2, waiting for transfers between devices: 37.6 us -> 13.9 us  [exchange(): got = lax.all_to_all(blocks, AXES, split_axis=0, concat_axis=0, tiled=True)]
    all_to_all x2, starting transfers between devices: 21.9 us -> 7.08 us  [exchange(): got = lax.all_to_all(blocks, AXES, split_axis=0, concat_axis=0, tiled=True)]
    unnamed x23, local copies, waits for them, and re-layouts: 6.48 us -> 9.2 us
  transfers between devices with their start and end apart: 3 -> 3, of which waited for: 2 -> 1; matrix products, arithmetic and copies ran while one was open for 4% -> 8% of each run, Pallas kernels for 49% -> 56%
where the time goes in v5:
time: 268 us; the launch traced here: 266 us
  Pallas kernels  177 us (66%)
  blocking collectives  37.6 us (14%)
  local copies, waits for them, and re-layouts  17 us (6%)
  waiting for transfers between devices  14 us (5%)
  starting transfers between devices  9.43 us (4%)
  matrix products  6.24 us (2%)
  other arithmetic  4.14 us (2%)
    pallas_call x2, Pallas kernels, near_part(): pl.pallas_call(functools.partial(near_kernel, capacity, n_dev, recv.shape...  137 us
    all_to_all x1, blocking collectives, exchange(): got = lax.all_to_all(blocks, AXES, split_axis=0, concat_axis=0, tiled=True)  37.6 us
    pallas_call x1, Pallas kernels, on_device(): pl.pallas_call(far_kernel, out_shape=jax.ShapeDtypeStruct((slot_table, po...  28.2 us
    all_to_all x2, waiting for transfers between devices, exchange(): got = lax.all_to_all(blocks, AXES, split_axis=0, concat_axis=0, tiled=True)  13.9 us
    unnamed x23, local copies, waits for them, and re-layouts  9.2 us
    pallas_call x1, Pallas kernels, on_device(): pl.pallas_call(functools.partial(pack_sources, capacity), out_shape=(jax....  7.14 us
    all_to_all x2, starting transfers between devices, exchange(): got = lax.all_to_all(blocks, AXES, split_axis=0, concat_axis=0, tiled=True)  7.08 us
    dot_general x1, matrix products, on_device(): jnp.einsum('pr,oqr->opq', parents, l2l_ops, precision=lax.Precision.HIGHEST)  6.24 us
  transfers between devices with their start and end apart: 3, of which 1 were waited for; matrix products, arithmetic and copies ran while one was open for 8% of the time, Pallas kernels for 56%

profile of v5, /device:TPU:0, one launch (start us, length us, event | category | flops | bytes accessed | tf_op | source)
XLA Modules:
  0.0 266.4 jit_solution(10742760406444063637)
XLA Ops:
  1.4 2.3 collective-permute-start
  3.7 0.8 dynamic_slice.3.owner_ref
  5.5 1.1 copy-done
  6.6 0.9 copy-done.1
  7.5 7.1 %pack_sources.1 = (f32[2304,128]{1,0:T(8,128)S(1)}, f32[2048,128]{1,0:T(8,128)}) custom-call(s32[512]{0:T(512)S(1)} %dynamic_slice.3.owner_ref, s32[512]{0:T(512)S(1)} %convert_reduce_fusion.rank_ref, f32[1536]{0:T(1024)S(1)} %reshape.43.center_ref, f32[3,512,128]{2,1,0:T(8,128)S(1)} %bitcast.22, f32[512,128]{1,0:T(8,128)S(1)} %copy-done.1), custom_call_target="tpu_custom_call" | custom-call | tf_op jit(solution)/shard_map/pack_sources/pallas_call | solution.py:345
  14.7 37.6 %all_to_all.15 = f32[32,72,128]{2,1,0:T(8,128)S(1)} all-to-all(f32[32,72,128]{2,1,0:T(8,128)S(1)} %bitcast.21), channel_id=1, replica_groups=mesh['grp'=4,'dom'=8] {'grp','dom'}, dimensions={0} | all-to-all | bytes 2359296 | tf_op jit(solution)/shard_map/all_to_all | solution.py:361
  52.3 3.5 %all-to-all-start.1 = ((f32[32,64,128]{2,1,0:T(8,128)}), f32[32,64,128]{2,1,0:T(8,128)}, u32[]{:S(2)}, u32[]{:S(2)}) async-start(f32[32,64,128]{2,1,0:T(8,128)} %bitcast.7), calls=%async_computation.1 | async-start | bytes 2097152 | tf_op jit(solution)/shard_map/all_to_all | solution.py:361
  56.1 0.8 multiply_add_fusion
  56.9 6.2 %fusion.1 = f32[80,8,296]{2,0,1:T(8,128)S(1)} fusion(f32[8,296,296]{2,1,0:T(8,128)} %param.15, f32[64,296]{1,0:T(8,128)S(1)} %copy-done.7, f32[16,296]{1,0:T(8,128)S(1)} %collective-permute-done), kind=kOutput, calls=%fused_computation.4 | convolution fusion | flops 672914560 | bytes 3656192 | tf_op jit(solution)/shard_map/pr,oqr->opq/dot_general | solution.py:368
  63.1 4.9 %route_leaves.1 = (f32[512,296]{1,0:T(8,128)S(1)}, f32[1024,384]{1,0:T(8,128)}) custom-call(s32[512]{0:T(512)S(1)} %get-tuple-element.29.index_ref, s32[512]{0:T(512)S(1)} %get-tuple-element.28.dest_ref, f32[512,296]{1,0:T(8,128)S(1)} %copy.18.m2l_ref, f32[640,296]{1,0:T(8,128)S(1)} %bitcast.16), custom_call_target="tpu_custom_call" | custom-call | tf_op jit(solution)/shard_map/route_leaves/pallas_call | solution.py:370
  68.1 13.9 %all-to-all-done.1 = f32[32,64,128]{2,1,0:T(8,128)} async-done(((f32[32,64,128]{2,1,0:T(8,128)}), f32[32,64,128]{2,1,0:T(8,128)}, u32[]{:S(2)}, u32[]{:S(2)}) %all-to-all-start.1) | async-done | bytes 1048608 | tf_op jit(solution)/shard_map/all_to_all | solution.py:361
  82.0 3.5 %all-to-all-start.2 = ((f32[32,32,384]{2,1,0:T(8,128)}), f32[32,32,384]{2,1,0:T(8,128)S(1)}, u32[]{:S(2)}, u32[]{:S(2)}) async-start(f32[32,32,384]{2,1,0:T(8,128)} %bitcast.26), calls=%async_computation.2 | async-start | bytes 3145728 | tf_op jit(solution)/shard_map/all_to_all | solution.py:361
  85.6 1.8 copy.19
  87.3 1.9 reshape.51.slots_ref
  89.2 1.5 compare_convert_fusion
  90.7 1.5 reshape.52
  92.2 1.0 reduce_sum.19
  96.0 1.1 copy.20
  97.8 1.4 copy-done.3
  99.3 68.1 %near_first.1.near_ref = f32[1024,128]{1,0:T(8,128)S(1)} custom-call(s32[8192]{0:T(1024)S(1)} %copy-done.2, f32[2304,128]{1,0:T(8,128)S(1)} %bitcast.18, f32[2304,128]{1,0:T(8,128)S(1)} %bitcast.19, f32[3,1024,128]{2,1,0:T(8,128)S(1)} %bitcast.25), custom_call_target="tpu_custom_call" | custom-call | flops 4697620480 | bytes 5000000 | tf_op jit(solution)/shard_map/near_first/pallas_call | solution.py:389
  167.4 68.9 %near_second.1.near_too_ref = f32[1024,128]{1,0:T(8,128)S(1)} custom-call(s32[8192]{0:T(1024)S(1)} %copy-done.2, f32[2048,128]{1,0:T(8,128)} %bitcast.8.recv_ref, f32[2304,128]{1,0:T(8,128)S(1)} %bitcast.20, f32[3,1024,128]{2,1,0:T(8,128)} %bitcast.23), custom_call_target="tpu_custom_call" | custom-call | flops 4697620480 | bytes 5000000 | tf_op jit(solution)/shard_map/near_second/pallas_call | solution.py:389
  236.3 0.8 copy-done.4
  237.1 1.0 copy-done.5
  238.2 28.2 %far_field.1 = f32[1024,128]{1,0:T(8,128)} custom-call(f32[1024,384]{1,0:T(8,128)S(1)} %bitcast.17, f32[3,1024,128]{2,1,0:T(8,128)} %bitcast.24, f32[1024,128]{1,0:T(8,128)S(1)} %near_first.1.near_ref, f32[1024,128]{1,0:T(8,128)S(1)} %copy-done.5, s32[8,128]{1,0:T(8,128)S(1)} %compare_convert_fusion.1.live_ref), custom_call_target="tpu_custom_call" | custom-call | flops 10000000000 | bytes 5000000 | tf_op jit(solution)/shard_map/far_field/pallas_call | solution.py:412
  (27 shorter events, 5.6 us)
Async XLA Ops:
  1.4 13.3 %collective-permute-start = (f32[16,296]{1,0:T(8,128)S(1)}, f32[16,296]{1,0:T(8,128)S(1)}, u32[]{:S(2)}, u32[]{:S(2)}) collective-permute-start(f32[16,296]{1,0:T(8,128)S(1)} %slice.3), channel_id=1, source_target_pairs={{0,1},{1,2},{2,3},{3,4},{4,5},{5,6},{6,7},{7,8},{8,9},{9,10},{10,1... | collective-permute-start | bytes 56840 | tf_op jit(solution)/shard_map/ppermute | solution.py:30
  5.5 1.1 copy-start
  6.6 0.9 copy-start.1
  52.3 3.6 %copy-start.6 = (f32[512,296]{0,1:T(8,128)S(1)}, f32[512,296]{0,1:T(8,128)}, u32[]{:S(2)}) copy-start(f32[512,296]{0,1:T(8,128)} %param.14) | copy-start | bytes 1818628
  52.3 3.8 %copy-start.8 = (s32[512]{0:T(512)S(1)}, s32[512]{0:T(512)}, u32[]{:S(2)}) copy-start(s32[512]{0:T(512)} %param.12) | copy-start | bytes 6148
  52.3 3.8 %copy-start.9 = (s32[512]{0:T(512)S(1)}, s32[512]{0:T(512)}, u32[]{:S(2)}) copy-start(s32[512]{0:T(512)} %param.13) | copy-start | bytes 6148
  52.3 4.6 %copy-start.7 = (f32[64,296]{1,0:T(8,128)S(1)}, f32[64,296]{1,0:T(8,128)}, u32[]{:S(2)}) copy-start(f32[64,296]{1,0:T(8,128)} %param.11) | copy-start | bytes 227332
  52.3 29.7 %all-to-all-start.1 = ((f32[32,64,128]{2,1,0:T(8,128)}), f32[32,64,128]{2,1,0:T(8,128)}, u32[]{:S(2)}, u32[]{:S(2)}) async-start(f32[32,64,128]{2,1,0:T(8,128)} %bitcast.7), calls=%async_computation.1 | async-start | bytes 2097152 | tf_op jit(solution)/shard_map/all_to_all | solution.py:361
  82.0 155.1 %all-to-all-start.2 = ((f32[32,32,384]{2,1,0:T(8,128)}), f32[32,32,384]{2,1,0:T(8,128)S(1)}, u32[]{:S(2)}, u32[]{:S(2)}) async-start(f32[32,32,384]{2,1,0:T(8,128)} %bitcast.26), calls=%async_computation.2 | async-start | bytes 3145728 | tf_op jit(solution)/shard_map/all_to_all | solution.py:361
  97.1 0.8 copy-start.2
  97.8 1.4 copy-start.3
  236.3 0.8 copy-start.4
  237.1 1.0 copy-start.5

commit v6 on v4

--- a/solution.py
+++ b/solution.py
@@ -18,7 +18,7 @@
 AXES = ("grp", "dom")
 FEATS = 32
 GROUP = 8
-VMEM_LIMIT = 50 * 1024 * 1024
+VMEM_LIMIT = 32 * 1024 * 1024
 
 F32 = jnp.float32
 BF16 = jnp.bfloat16
@@ -72,28 +72,35 @@
     stage_ref[...] = jnp.zeros_like(stage_ref)
 
 
-def pack_sources(capacity, owner_ref, rank_ref, center_ref, coords_ref, charge_ref, out_ref):
-    rows = 4 * capacity + 8
-    leaves = charge_ref.shape[0]
-    lane = lax.broadcasted_iota(jnp.int32, (8, 128), 1)
-    sub = lax.broadcasted_iota(jnp.int32, (8, 128), 0)
-
+def lane_sums(block):
+    high = block.astype(BF16)
+    low = (block - high.astype(F32)).astype(BF16)
+    ones = jnp.ones((GROUP, 2 * block.shape[1]), BF16)
+    pieces = jnp.concatenate([high, low], axis=1)
+    return lax.dot_general(ones, pieces, (((1,), (1,)), ((), ())), preferred_element_type=F32)
+
+
+def pack_sources(capacity, owner_ref, rank_ref, coords_ref, charge_ref, out_ref):
     def step(j, carry):
-        rank = rank_ref[j]
-        base = owner_ref[j] * rows
+        at = owner_ref[j] * 4 * capacity + rank_ref[j]
         for c in range(3):
-            out_ref[pl.ds(base + c * capacity + rank, 1), :] = coords_ref[c, pl.ds(j, 1), :]
-        out_ref[pl.ds(base + 3 * capacity + rank, 1), :] = charge_ref[pl.ds(j, 1), :]
-        place = pl.ds(pl.multiple_of(base + 4 * capacity, 8), 8)
-        value = jnp.where(
-            sub == 0,
-            center_ref[j],
-            jnp.where(sub == 1, center_ref[leaves + j], center_ref[2 * leaves + j]),
-        )
-        out_ref[place, :] = jnp.where(lane == rank, value, out_ref[place, :])
-        return carry
-
-    lax.fori_loop(0, leaves, step, 0, unroll=4)
+            out_ref[pl.ds(at + c * capacity, 1), :] = coords_ref[c, pl.ds(j, 1), :]
+        out_ref[pl.ds(at + 3 * capacity, 1), :] = charge_ref[pl.ds(j, 1), :]
+        return carry
+
+    lax.fori_loop(0, charge_ref.shape[0], step, 0, unroll=8)
+
+
+def target_kernel(points_ref, out_ref, stage_ref):
+    clear_stage(stage_ref)
+
+    def prepare(g, carry):
+        slot = pl.multiple_of(g * GROUP, GROUP)
+        coords = [points_ref[c, pl.ds(slot, GROUP), :] for c in range(3)]
+        store_feats(stage_ref, out_ref, slot, point_rows(coords, SOFT_SQ, True))
+        return carry
+
+    lax.fori_loop(0, out_ref.shape[0] // GROUP, prepare, 0, unroll=2)
 
 
 def route_leaves(index_ref, dest_ref, m2l_ref, moved_ref, leaf_ref, out_ref):
@@ -111,43 +118,31 @@
     n_dev,
     slots_ref,
     recv_ref,
-    obs_ref,
+    target_ref,
     out_ref,
+    turned_ref,
     source_ref,
-    target_ref,
     charge_ref,
-    stage_a,
-    stage_b,
+    stage_ref,
     left_a,
     left_b,
     total_a,
     total_b,
 ):
-    rows = 4 * capacity + 8
     blocks = out_ref.shape[0] // GROUP
     side = out_ref.shape[1]
     lane = lax.broadcasted_iota(jnp.int32, (side, side), 1)
-    clear_stage(stage_a)
-    clear_stage(stage_b)
+    sub = lax.broadcasted_iota(jnp.int32, (GROUP, side), 0)
+    clear_stage(stage_ref)
+    turned_ref[...] = jnp.zeros_like(turned_ref)
 
     def prepare(s, carry):
-        base = pl.multiple_of(s * rows, 8)
-        centers = recv_ref[pl.ds(base + 4 * capacity, 8), :].T
-        for g in range(capacity // GROUP):
-            slot = pl.multiple_of(s * capacity + g * GROUP, GROUP)
-            coords = [
-                recv_ref[pl.ds(base + c * capacity + g * GROUP, GROUP), :] - 1.0 for c in range(3)
-            ]
-            store_feats(stage_a, source_ref, slot, point_rows(coords, 0.0, False))
-            targets = [
-                (centers[g * GROUP : (g + 1) * GROUP, c : c + 1] - 1.0)
-                + HALF_WIDTH * obs_ref[c, pl.ds(slot, GROUP), :]
-                for c in range(3)
-            ]
-            store_feats(stage_b, target_ref, slot, point_rows(targets, SOFT_SQ, True))
-            charge_ref[pl.ds(slot, GROUP), :] = recv_ref[
-                pl.ds(base + 3 * capacity + g * GROUP, GROUP), :
-            ]
+        for g in range(0, capacity, GROUP):
+            slot = pl.multiple_of(s * capacity + g, GROUP)
+            at = pl.multiple_of(s * 4 * capacity + g, GROUP)
+            coords = [recv_ref[pl.ds(at + c * capacity, GROUP), :] - 1.0 for c in range(3)]
+            store_feats(stage_ref, source_ref, slot, point_rows(coords, 0.0, False))
+            charge_ref[pl.ds(slot, GROUP), :] = recv_ref[pl.ds(at + 3 * capacity, GROUP), :]
         return carry
 
     lax.fori_loop(0, n_dev, prepare, 0)
@@ -171,24 +166,29 @@
         total_ref[u] = total
 
     def put_sums(block, total_ref):
-        tile, column = block * GROUP // side, lax.rem(block * GROUP, side)
-        place = pl.ds(pl.multiple_of(tile * side, side), side)
+        column = lax.rem(block * GROUP, side)
+        place = pl.ds(pl.multiple_of(block * GROUP - column, side), side)
+        rows, columns = jnp.zeros((GROUP, side), F32), turned_ref[place, :]
 
         def add_row(sums, u):
+            rows, columns = sums
+            if u < GROUP // 2:
+                return jnp.where(sub == u, lane_sums(total_ref[u]), rows), columns
             row = jnp.sum(total_ref[u], axis=1, keepdims=True)
-            return jnp.where(lane == column + u, row, sums)
+            return rows, jnp.where(lane == column + u, row, columns)
 
         def finish(sums):
-            out_ref[place, :] = sums
-
-        return out_ref[place, :], add_row, finish
+            out_ref[pl.ds(pl.multiple_of(block * GROUP, GROUP), GROUP), :] = sums[0]
+            turned_ref[place, :] = sums[1]
+
+        return (rows, columns), add_row, finish
 
     def half(before, block, after, left_now, left_next, total_before, total_now):
         sums, add_row, finish = put_sums(before, total_before)
         for u in range(GROUP):
             turn(after, u, left_next)
             pair_work(block, u, left_now, total_now)
-            sums = add_row(sums, u)
+            sums = add_row(sums, (u % 2) * (GROUP // 2) + u // 2)
         finish(sums)
 
     for u in range(GROUP):
@@ -208,7 +208,7 @@
     finish(sums)
 
 
-def far_kernel(dens_ref, obs_ref, near_ref, live_ref, out_ref, turned_ref, point_ref, far_ref):
+def far_kernel(dens_ref, obs_ref, near_ref, turned_near_ref, live_ref, out_ref, turned_ref, far_ref):
     axis, surface = surface_grid()
     number = {point: q for q, point in enumerate(surface)}
     side = out_ref.shape[1]
@@ -217,14 +217,12 @@
         first = pl.multiple_of(t * side, side)
         for column in range(0, dens_ref.shape[1], side):
             turned_ref[pl.ds(column, side), :] = dens_ref[pl.ds(first, side), pl.ds(column, side)].T
-        for c in range(3):
-            point_ref[c] = obs_ref[c, pl.ds(first, side), :].T
 
         def points(b, carry):
             place = pl.ds(pl.multiple_of(b * GROUP, GROUP), GROUP)
             squares = []
             for c in range(3):
-                value = point_ref[c, place, :]
+                value = obs_ref[c, place, pl.ds(first, side)]
                 squares.append([(value - at) * (value - at) for at in axis])
             totals = [jnp.zeros((GROUP, side), F32) for _ in range(4)]
             turn = 0
@@ -242,7 +240,7 @@
             return carry
 
         lax.fori_loop(0, side // GROUP, points, 0)
-        near = near_ref[pl.ds(first, side), :]
+        near = near_ref[pl.ds(first, side), :].T + turned_near_ref[pl.ds(first, side), :]
         total = far_ref[...] * (1.0 / (FOUR_PI * HALF_WIDTH)) + near * (1.0 / FOUR_PI)
         total = jnp.where(live_ref[pl.ds(t, 1), :] > 0, total, 0.0)
         out_ref[pl.ds(first, side), :] = total.T
@@ -269,16 +267,15 @@
     slot_table = obs_offset.shape[0]
     points = obs_offset.shape[2]
     capacity = slot_table // n_dev
-    block_rows = 4 * capacity + 8
+    block_rows = 4 * capacity
     lanes = -(-width // points) * points
     my_index = lax.axis_index(AXES)
     vmem, smem = pl.BlockSpec(memory_space=pltpu.VMEM), pl.BlockSpec(memory_space=pltpu.SMEM)
     params = pltpu.CompilerParams(vmem_limit_bytes=VMEM_LIMIT)
 
     mine = lax.dynamic_slice_in_dim(obs_owner, my_index * leaf_dev, leaf_dev)
-    counts = jnp.sum((obs_owner.reshape(n_dev, leaf_dev) == my_index).astype(jnp.int32), axis=1)
-    live = (jnp.arange(capacity, dtype=jnp.int32)[None, :] < counts[:, None]).astype(jnp.int32).reshape(slot_table)
-
+    center_rows = leaf_center.T.reshape(3 * leaf_dev // points, points)
+    all_centers = lax.all_gather(center_rows, AXES, axis=0, tiled=True).reshape(n_dev, 3, leaf_dev)
     leaf_at = jnp.arange(leaf_dev, dtype=jnp.int32)
     same = (mine[:, None] == mine[None, :]) & (leaf_at[None, :] < leaf_at[:, None])
     rank = jnp.sum(same.astype(jnp.int32), axis=1)
@@ -286,15 +283,35 @@
     packed = pl.pallas_call(
         functools.partial(pack_sources, capacity),
         out_shape=jax.ShapeDtypeStruct((n_dev * block_rows, points), F32),
-        in_specs=[smem, smem, smem, vmem, vmem],
+        in_specs=[smem, smem, vmem, vmem],
         out_specs=vmem,
         compiler_params=params,
         name="pack_sources",
-    )(mine, rank, leaf_center.T.reshape(-1), src_coords.transpose(1, 0, 2), src_charge)
-    packed, rim_rows = lax.optimization_barrier((packed, rim_rows))
+    )(mine, rank, src_coords.transpose(1, 0, 2), src_charge)
+    packed, rim_rows, obs_owner, obs_offset, near_slots, child_m2l = lax.optimization_barrier(
+        (packed, rim_rows, obs_owner, obs_offset, near_slots, child_m2l)
+    )
     recv = lax.all_to_all(
         packed.reshape(n_dev, block_rows, points), AXES, split_axis=0, concat_axis=0, tiled=True
     ).reshape(n_dev * block_rows, points)
+
+    to_me = (obs_owner.reshape(n_dev, leaf_dev) == my_index).astype(jnp.int32)
+    order = jnp.cumsum(to_me, axis=1) * to_me
+    counts = jnp.sum(to_me, axis=1)
+    slot_at = jnp.arange(capacity, dtype=jnp.int32)
+    live = (slot_at[None, :] < counts[:, None]).astype(jnp.int32).reshape(slot_table // points, points)
+
+    chosen = order[:, None, :] == slot_at[None, :, None] + 1
+    centers = jnp.stack(
+        [
+            jnp.sum(jnp.where(chosen, all_centers[:, c, None, :], 0.0), axis=2).reshape(slot_table)
+            for c in range(3)
+        ]
+    )
+    obs = obs_offset.transpose(1, 0, 2)
+    turned_obs = obs.transpose(0, 2, 1)
+    slots = near_slots.reshape(-1)
+    target_points = (centers - 1.0)[:, :, None] + HALF_WIDTH * obs
 
     parents = jnp.concatenate([rim_rows, parent_local], axis=0)
     moved = jnp.einsum("pr,oqr->opq", parents, l2l_ops, precision=lax.Precision.HIGHEST)
@@ -310,22 +327,34 @@
         compiler_params=params,
         name="route_leaves",
     )(child_octant * parents.shape[0] + parent_slot, mine * capacity + rank, child_m2l, stacked)
+    targets = pl.pallas_call(
+        target_kernel,
+        out_shape=jax.ShapeDtypeStruct((slot_table, FEATS, points), BF16),
+        in_specs=[vmem],
+        out_specs=vmem,
+        scratch_shapes=[pltpu.VMEM((GROUP * FEATS, points), F32)],
+        compiler_params=params,
+        name="target_pieces",
+    )(target_points)
+    packed_dens, targets, slots, live, turned_obs = lax.optimization_barrier(
+        (packed_dens, targets, slots, live, turned_obs)
+    )
     dens = lax.all_to_all(
         packed_dens.reshape(n_dev, capacity, lanes), AXES, split_axis=0, concat_axis=0, tiled=True
     ).reshape(slot_table, lanes)
 
-    obs = obs_offset.transpose(1, 0, 2)
     pairs = slot_table * near_slots.shape[1] * points * points
-    near = pl.pallas_call(
+    near, turned_near = pl.pallas_call(
         functools.partial(near_kernel, capacity, n_dev),
-        out_shape=jax.ShapeDtypeStruct((slot_table, points), F32),
+        out_shape=(
+            jax.ShapeDtypeStruct((slot_table, points), F32),
+            jax.ShapeDtypeStruct((slot_table, points), F32),
+        ),
         in_specs=[smem, vmem, vmem],
-        out_specs=vmem,
+        out_specs=(vmem, vmem),
         scratch_shapes=[
             pltpu.VMEM((slot_table, FEATS, points), BF16),
-            pltpu.VMEM((slot_table, FEATS, points), BF16),
             pltpu.VMEM((slot_table, points), F32),
-            pltpu.VMEM((GROUP * FEATS, points), F32),
             pltpu.VMEM((GROUP * FEATS, points), F32),
             pltpu.VMEM((GROUP, points, FEATS), BF16),
             pltpu.VMEM((GROUP, points, FEATS), BF16),
@@ -335,21 +364,20 @@
         compiler_params=params,
         cost_estimate=pl.CostEstimate(flops=70 * pairs, bytes_accessed=5 * 10**6, transcendentals=pairs),
         name="near_field",
-    )(near_slots.reshape(-1), recv, obs)
+    )(slots, recv, targets)
     potential = pl.pallas_call(
         far_kernel,
         out_shape=jax.ShapeDtypeStruct((slot_table, points), F32),
-        in_specs=[vmem, vmem, vmem, vmem],
+        in_specs=[vmem, vmem, vmem, vmem, vmem],
         out_specs=vmem,
         scratch_shapes=[
             pltpu.VMEM((lanes, points), F32),
-            pltpu.VMEM((3, points, points), F32),
             pltpu.VMEM((points, points), F32),
         ],
         compiler_params=params,
         cost_estimate=pl.CostEstimate(flops=10**10, bytes_accessed=5 * 10**6, transcendentals=10**7),
         name="far_field",
-    )(dens, obs, near, live.reshape(slot_table // points, points))
+    )(dens, turned_obs, near, turned_near, live)
     return (leaf_local, potential)
 
 

time: 214 us -> 256 us (1.20)
  blocking collectives: 0 us -> 70.1 us
  waiting for transfers between devices: 40.1 us -> 0.01 us
  local copies, waits for them, and re-layouts: 9.26 us -> 22.6 us
  Pallas kernels: 143 us -> 136 us
  other arithmetic: 0.46 us -> 4.4 us
  starting transfers between devices: 13.6 us -> 16.3 us
    all_gather x0 -> x1, blocking collectives: none -> 70.1 us  [on_device(): lax.all_gather(center_rows, AXES, axis=0, tiled=True)]
    all_to_all x1, waiting for transfers between devices: 40.1 us -> 0.01 us  [on_device(): lax.all_to_all(packed.reshape(n_dev, block_rows, points), AXES, split_axi...]
    pallas_call x1, Pallas kernels: 106 us -> 93.9 us  [on_device(): pl.pallas_call(functools.partial(near_kernel, capacity, n_dev), out_shape...]
    pallas_call x0 -> x1, Pallas kernels: none -> 7.86 us  [on_device(): pl.pallas_call(target_kernel, out_shape=jax.ShapeDtypeStruct((slot_table,...]
    unnamed x23 -> x46, local copies, waits for them, and re-layouts: 6.46 us -> 13.4 us
    optimization_barrier x0 -> x3, local copies, waits for them, and re-layouts: none -> 3.5 us  [on_device(): lax.optimization_barrier((packed, rim_rows, obs_owner, obs_offset, near_s...]
    all_to_all x1, starting transfers between devices: 4.01 us -> 6.79 us  [on_device(): lax.all_to_all(packed_dens.reshape(n_dev, capacity, lanes), AXES, split_a...]
  transfers between devices with their start and end apart: 3 -> 3, of which waited for: 1 -> 0; matrix products, arithmetic and copies ran while one was open for 5% -> 7% of each run, Pallas kernels for 55% -> 43%
where the time goes in v6:
time: 256 us; the launch traced here: 255 us
  Pallas kernels  136 us (53%)
  blocking collectives  70.1 us (27%)
  local copies, waits for them, and re-layouts  22.6 us (9%)
  starting transfers between devices  16.3 us (6%)
  other arithmetic  4.4 us (2%)
  matrix products  4.24 us (2%)
    pallas_call x1, Pallas kernels, on_device(): pl.pallas_call(functools.partial(near_kernel, capacity, n_dev), out_shape...  93.9 us
    all_gather x1, blocking collectives, on_device(): lax.all_gather(center_rows, AXES, axis=0, tiled=True)  70.1 us
    pallas_call x1, Pallas kernels, on_device(): pl.pallas_call(far_kernel, out_shape=jax.ShapeDtypeStruct((slot_table, po...  27.8 us
    unnamed x46, local copies, waits for them, and re-layouts  13.4 us
    pallas_call x1, Pallas kernels, on_device(): pl.pallas_call(target_kernel, out_shape=jax.ShapeDtypeStruct((slot_table,...  7.86 us
    all_to_all x1, starting transfers between devices, on_device(): lax.all_to_all(packed.reshape(n_dev, block_rows, points), AXES, split_axi...  7.14 us
    all_to_all x1, starting transfers between devices, on_device(): lax.all_to_all(packed_dens.reshape(n_dev, capacity, lanes), AXES, split_a...  6.79 us
  transfers between devices with their start and end apart: 3, of which 0 were waited for; matrix products, arithmetic and copies ran while one was open for 7% of the time, Pallas kernels for 43%

profile of v6, /device:TPU:0, one launch (start us, length us, event | category | flops | bytes accessed | tf_op | source)
XLA Modules:
  0.0 255.1 jit_solution(11838610352991756138)
XLA Ops:
  0.6 0.7 slice.18
  1.4 2.3 collective-permute-start
  3.7 0.8 dynamic_slice.3.owner_ref
  4.8 1.1 copy-done.4
  5.9 0.9 copy-done.7
  6.8 3.1 %pack_sources.1 = f32[4096,128]{1,0:T(8,128)} custom-call(s32[512]{0:T(512)S(1)} %dynamic_slice.3.owner_ref, s32[512]{0:T(512)S(1)} %convert_reduce_fusion.rank_ref, f32[3,512,128]{2,1,0:T(8,128)S(1)} %bitcast.33, f32[512,128]{1,0:T(8,128)S(1)} %copy-done.7), custom_call_target="tpu_custom_call" | custom-call | tf_op jit(solution)/shard_map/pack_sources/pallas_call | solution.py:283
  10.0 7.1 %all-to-all-start.1 = ((f32[32,128,128]{2,1,0:T(8,128)}), f32[32,128,128]{2,1,0:T(8,128)S(1)}, u32[]{:S(2)}, u32[]{:S(2)}) async-start(f32[32,128,128]{2,1,0:T(8,128)} %bitcast.10), calls=%async_computation.1 | async-start | bytes 4194304 | tf_op jit(solution)/shard_map/all_to_all | solution.py:294
  17.8 70.1 %all-gather = f32[32,12,128]{2,1,0:T(8,128)S(1)} all-gather(f32[1,12,128]{2,1,0:T(8,128)S(1)} %reshape.108), channel_id=1, replica_groups=mesh['grp'=4,'dom'=8] {'grp','dom'}, dimensions={0}, use_global_device_ids=true | all-gather | bytes 202752 | tf_op jit(solution)/shard_map/all_gather | solution.py:278
  88.3 1.2 reduce-window.6
  89.9 0.8 fusion
  94.4 3.0 %copy.32 = f32[1024,3,128]{0,2,1:T(8,128)} copy(f32[1024,3,128]{2,0,1:T(8,128)} %param.20) | data formatting | bytes 3145728 | tf_op jit(solution)/shard_map/optimization_barrier | solution.py:291
  97.5 1.9 bitcast_add_fusion.points_ref
  99.4 7.9 %target_pieces.1.target_ref = bf16[1024,32,128]{2,1,0:T(8,128)(2,1)S(1)} custom-call(f32[3,1024,128]{2,1,0:T(8,128)S(1)} %bitcast_add_fusion.points_ref), custom_call_target="tpu_custom_call" | custom-call | tf_op jit(solution)/shard_map/target_pieces/pallas_call | solution.py:330
  107.2 3.2 %copy-done = bf16[1024,32,128]{2,1,0:T(8,128)(2,1)} copy-done((bf16[1024,32,128]{2,1,0:T(8,128)(2,1)}, bf16[1024,32,128]{2,1,0:T(8,128)(2,1)S(1)}, u32[]{:S(2)}) %copy-start) | copy-done | bytes 8388632
  110.5 4.2 %fusion.4 = f32[80,8,296]{2,0,1:T(8,128)S(1)} fusion(f32[8,296,296]{2,1,0:T(8,128)S(1)} %copy-done.8, f32[64,296]{1,0:T(8,128)S(1)} %copy-done.10, f32[16,296]{1,0:T(8,128)S(1)} %collective-permute-done), kind=kOutput, calls=%fused_computation.11 | convolution fusion | flops 672914560 | bytes 3656192 | tf_op jit(solution)/shard_map/pr,oqr->opq/dot_general | solution.py:317
  114.7 3.8 %route_leaves.1 = (f32[512,296]{1,0:T(8,128)S(1)}, f32[1024,384]{1,0:T(8,128)S(1)}) custom-call(s32[512]{0:T(512)S(1)} %get-tuple-element.51.index_ref, s32[512]{0:T(512)S(1)} %get-tuple-element.50.dest_ref, f32[512,296]{1,0:T(8,128)S(1)} %copy.28.m2l_ref, f32[640,296]{1,0:T(8,128)S(1)} %bitcast.29), custom_call_target="tpu_custom_call" | custom-call | tf_op jit(solution)/shard_map/route_leaves/pallas_call | solution.py:319
  118.5 1.2 copy-done.3
  119.7 0.9 copy-done.5
  120.6 6.8 %all-to-all-start = ((f32[32,32,384]{2,1,0:T(8,128)}), f32[32,32,384]{2,1,0:T(8,128)}, u32[]{:S(2)}, u32[]{:S(2)}) async-start(f32[32,32,384]{2,1,0:T(8,128)} %bitcast.32), calls=%async_computation | async-start | bytes 3145728 | tf_op jit(solution)/shard_map/all_to_all | solution.py:342
  127.4 1.1 copy.33
  128.5 3.4 %copy-done.1 = bf16[1024,32,128]{2,1,0:T(8,128)(2,1)S(1)} copy-done((bf16[1024,32,128]{2,1,0:T(8,128)(2,1)S(1)}, bf16[1024,32,128]{2,1,0:T(8,128)(2,1)}, u32[]{:S(2)}) %copy-start.1) | copy-done | bytes 8388632
  131.9 93.9 %near_field.1 = (f32[1024,128]{1,0:T(8,128)S(1)}, f32[1024,128]{1,0:T(8,128)S(1)}) custom-call(s32[8192]{0:T(1024)S(1)} %reshape.102.slots_ref, f32[4096,128]{1,0:T(8,128)S(1)} %bitcast.30, bf16[1024,32,128]{2,1,0:T(8,128)(2,1)S(1)} %copy-done.1), custom_call_target="tpu_custom_call" | custom-call | flops 9395240960 | bytes 5000000 | tf_op jit(solution)/shard_map/near_field/pallas_call | solution.py:347
  225.8 1.4 copy-done.2
  227.3 27.8 %far_field.1 = f32[1024,128]{1,0:T(8,128)} custom-call(f32[1024,384]{1,0:T(8,128)} %bitcast.9.dens_ref, f32[3,128,1024]{2,1,0:T(8,128)S(1)} %bitcast.31, f32[1024,128]{1,0:T(8,128)S(1)} %get-tuple-element.29.near_ref, f32[1024,128]{1,0:T(8,128)S(1)} %get-tuple-element.30.turned_near_ref, s32[8,128]{1,0:T(8,128)S(1)} %compare_convert_fusion.live_ref), custom_call_target="tpu_custom_call" | custom-call | flops 10000000000 | bytes 5000000 | tf_op jit(solution)/shard_map/far_field/pallas_call | solution.py:368
  (66 shorter events, 5.3 us)
Async XLA Ops:
  1.4 8.6 %collective-permute-start = (f32[16,296]{1,0:T(8,128)S(1)}, f32[16,296]{1,0:T(8,128)S(1)}, u32[]{:S(2)}, u32[]{:S(2)}) collective-permute-start(f32[16,296]{1,0:T(8,128)S(1)} %slice.18), channel_id=1, source_target_pairs={{0,1},{1,2},{2,3},{3,4},{4,5},{5,6},{6,7},{7,8},{8,9},{9,10},{10,1... | collective-permute-start | bytes 56840 | tf_op jit(solution)/shard_map/ppermute | solution.py:30
  4.7 1.1 copy-start.4
  5.9 0.9 copy-start.7
  10.0 7.8 %copy-start.17 = (f32[512,3]{0,1:T(4,128)S(1)}, f32[512,3]{0,1:T(4,128)}, u32[]{:S(2)}) copy-start(f32[512,3]{0,1:T(4,128)} %param.16) | copy-start | bytes 18436
  10.0 78.2 %copy-start.11 = (s32[16384]{0:T(1024)S(1)}, s32[16384]{0:T(1024)}, u32[]{:S(2)}) copy-start(s32[16384]{0:T(1024)} %param.19) | copy-start | bytes 196612
  10.0 78.2 %copy-start.18 = (s32[512]{0:T(512)S(1)}, s32[512]{0:T(512)}, u32[]{:S(2)}) copy-start(s32[512]{0:T(512)} %param.12) | copy-start | bytes 6148
  10.0 78.2 %copy-start.19 = (s32[512]{0:T(512)S(1)}, s32[512]{0:T(512)}, u32[]{:S(2)}) copy-start(s32[512]{0:T(512)} %param.13) | copy-start | bytes 6148
  10.0 110.6 %all-to-all-start.1 = ((f32[32,128,128]{2,1,0:T(8,128)}), f32[32,128,128]{2,1,0:T(8,128)S(1)}, u32[]{:S(2)}, u32[]{:S(2)}) async-start(f32[32,128,128]{2,1,0:T(8,128)} %bitcast.10), calls=%async_computation.1 | async-start | bytes 4194304 | tf_op jit(solution)/shard_map/all_to_all | solution.py:294
  17.1 76.5 %copy-start.12 = (s32[1024,8]{0,1:T(8,128)S(1)}, s32[1024,8]{0,1:T(8,128)}, u32[]{:S(2)}) copy-start(s32[1024,8]{0,1:T(8,128)} %param.21) | copy-start | bytes 98308
  17.2 76.9 %copy-start.9 = (f32[512,296]{0,1:T(8,128)S(1)}, f32[512,296]{0,1:T(8,128)}, u32[]{:S(2)}) copy-start(f32[512,296]{0,1:T(8,128)} %param.14) | copy-start | bytes 1818628
  94.3 3.1 %copy-start.13 = (f32[1,1024]{1,0:T(1,128)S(1)}, f32[1,1024]{1,0:T(1,128)}, u32[]{:S(2)}) copy-start(f32[1,1024]{1,0:T(1,128)} %stack.9) | copy-start | bytes 12292
  94.4 3.1 %copy-start.14 = (f32[1,1024]{1,0:T(1,128)S(1)}, f32[1,1024]{1,0:T(1,128)}, u32[]{:S(2)}) copy-start(f32[1,1024]{1,0:T(1,128)} %stack.11) | copy-start | bytes 12292
  94.4 3.1 %copy-start.15 = (f32[1,1024]{1,0:T(1,128)S(1)}, f32[1,1024]{1,0:T(1,128)}, u32[]{:S(2)}) copy-start(f32[1,1024]{1,0:T(1,128)} %stack.10) | copy-start | bytes 12292
  99.3 11.1 %copy-start.8 = (f32[8,296,296]{2,1,0:T(8,128)S(1)}, f32[8,296,296]{2,1,0:T(8,128)}, u32[]{:S(2)}) copy-start(f32[8,296,296]{2,1,0:T(8,128)} %param.15) | copy-start | bytes 8411140
  99.4 11.1 %copy-start.10 = (f32[64,296]{1,0:T(8,128)S(1)}, f32[64,296]{1,0:T(8,128)}, u32[]{:S(2)}) copy-start(f32[64,296]{1,0:T(8,128)} %param.11) | copy-start | bytes 227332
  107.2 3.2 %copy-start = (bf16[1024,32,128]{2,1,0:T(8,128)(2,1)}, bf16[1024,32,128]{2,1,0:T(8,128)(2,1)S(1)}, u32[]{:S(2)}) copy-start(bf16[1024,32,128]{2,1,0:T(8,128)(2,1)S(1)} %target_pieces.1.target_ref) | copy-start | bytes 25165828
  110.5 10.1 %copy-start.16 = (s32[8,128]{1,0:T(8,128)S(1)}, s32[8,128]{1,0:T(8,128)}, u32[]{:S(2)}) copy-start(s32[8,128]{1,0:T(8,128)} %lt.47) | copy-start | bytes 12292
  110.5 10.1 %copy-start.20 = (s32[128]{0:T(128)S(1)}, s32[128]{0:T(128)}, u32[]{:S(2)}) copy-start(s32[128]{0:T(128)} %lt.43) | copy-start | bytes 1540
  118.5 1.2 copy-start.3
  119.7 0.9 copy-start.5
  120.6 6.8 %copy-start.6 = (f32[512,296]{1,0:T(8,128)S(1)}, f32[512,296]{1,0:T(8,128)}, u32[]{:S(2)}) copy-start(f32[512,296]{1,0:T(8,128)} %copy-done.5) | copy-start | bytes 1818628
  120.6 105.2 %all-to-all-start = ((f32[32,32,384]{2,1,0:T(8,128)}), f32[32,32,384]{2,1,0:T(8,128)}, u32[]{:S(2)}, u32[]{:S(2)}) async-start(f32[32,32,384]{2,1,0:T(8,128)} %bitcast.32), calls=%async_computation | async-start | bytes 3145728 | tf_op jit(solution)/shard_map/all_to_all | solution.py:342
  128.5 3.4 %copy-start.1 = (bf16[1024,32,128]{2,1,0:T(8,128)(2,1)S(1)}, bf16[1024,32,128]{2,1,0:T(8,128)(2,1)}, u32[]{:S(2)}) copy-start(bf16[1024,32,128]{2,1,0:T(8,128)(2,1)} %copy-done) | copy-start | bytes 25165828
  225.8 1.4 copy-start.2

commit v7 on v3

--- a/solution.py
+++ b/solution.py
@@ -18,7 +18,7 @@
 AXES = ("grp", "dom")
 FEATS = 32
 GROUP = 8
-VMEM_LIMIT = 50 * 1024 * 1024
+VMEM_LIMIT = 40 * 1024 * 1024
 
 F32 = jnp.float32
 BF16 = jnp.bfloat16
@@ -50,26 +50,37 @@
     return high, mid, rest - mid
 
 
-def point_rows(coords, extra, is_target):
+SOURCE_ORDER = ("h", "h", "h", "m", "m", "l")
+TARGET_ORDER = ("h", "m", "l", "h", "m", "h")
+N_PIECES = 14
+
+
+def spread_matrix(order, norm_first):
+    start = {"h": 0, "m": 3, "l": 6}
+    pieces = [start[name] + c for c in range(3) for name in order]
+    pieces += [9, 10, 11, 12, 12, 12] if norm_first else [12, 12, 12, 9, 10, 11]
+    table = np.zeros((GROUP * FEATS, N_PIECES * GROUP), jnp.bfloat16)
+    for u in range(GROUP):
+        for f, piece in enumerate(pieces):
+            table[u * FEATS + f, piece * GROUP + u] = 1.0
+    return table
+
+
+def piece_rows(coords, extra, scale):
     norm = coords[0] * coords[0] + coords[1] * coords[1] + coords[2] * coords[2] + extra
-    ones = jnp.ones_like(norm)
-    rows = []
-    for value in coords:
-        high, mid, low = split(-2.0 * value if is_target else value)
-        rows += [high, mid, low, high, mid, high] if is_target else [high, high, high, mid, mid, low]
-    norms = list(split(norm))
-    rows += norms + [ones] * 3 if is_target else [ones] * 3 + norms
-    return rows
-
-
-def store_feats(stage_ref, out_ref, base, rows):
-    for f, row in enumerate(rows):
-        stage_ref[pl.ds(f, GROUP, stride=FEATS), :] = row
-    out_ref[pl.ds(base, GROUP)] = stage_ref[...].reshape(GROUP, FEATS, row.shape[1]).astype(BF16)
-
-
-def clear_stage(stage_ref):
-    stage_ref[...] = jnp.zeros_like(stage_ref)
+    parts = [split(scale * value) for value in coords]
+    rows = [part[level] for level in range(3) for part in parts]
+    rows += list(split(norm)) + [jnp.ones_like(norm), jnp.zeros_like(norm)]
+    return jnp.concatenate(rows, axis=0).astype(BF16)
+
+
+def spread(matrix_ref, blocks, out_ref, slot):
+    pieces = jnp.concatenate(blocks, axis=1)
+    rows = jnp.dot(matrix_ref[...], pieces, preferred_element_type=F32).astype(BF16)
+    lanes = blocks[0].shape[1]
+    for i in range(2):
+        block = rows[:, i * lanes : (i + 1) * lanes].reshape(GROUP, FEATS, lanes)
+        out_ref[pl.ds(slot + i * GROUP, GROUP)] = block
 
 
 def lane_sums(block):
@@ -85,6 +96,7 @@
     leaves = charge_ref.shape[0]
     lane = lax.broadcasted_iota(jnp.int32, (8, 128), 1)
     sub = lax.broadcasted_iota(jnp.int32, (8, 128), 0)
+    out_ref[...] = jnp.zeros_like(out_ref)
 
     def step(j, carry):
         rank = rank_ref[j]
@@ -116,16 +128,15 @@
 
 def near_kernel(
     capacity,
-    n_dev,
     slots_ref,
     recv_ref,
     obs_ref,
+    source_matrix_ref,
+    target_matrix_ref,
     out_ref,
     source_ref,
     target_ref,
     charge_ref,
-    stage_a,
-    stage_b,
     left_a,
     left_b,
     total_a,
@@ -133,31 +144,33 @@
 ):
     rows = 4 * capacity + 8
     blocks = out_ref.shape[0] // GROUP
-    sub = lax.broadcasted_iota(jnp.int32, (GROUP, out_ref.shape[1]), 0)
-    clear_stage(stage_a)
-    clear_stage(stage_b)
-
-    def prepare(s, carry):
-        base = pl.multiple_of(s * rows, 8)
-        centers = recv_ref[pl.ds(base + 4 * capacity, 8), :].T
-        for g in range(capacity // GROUP):
-            slot = pl.multiple_of(s * capacity + g * GROUP, GROUP)
-            coords = [
-                recv_ref[pl.ds(base + c * capacity + g * GROUP, GROUP), :] - 1.0 for c in range(3)
-            ]
-            store_feats(stage_a, source_ref, slot, point_rows(coords, 0.0, False))
-            targets = [
-                (centers[g * GROUP : (g + 1) * GROUP, c : c + 1] - 1.0)
-                + HALF_WIDTH * obs_ref[c, pl.ds(slot, GROUP), :]
+    side = out_ref.shape[1]
+    sub = lax.broadcasted_iota(jnp.int32, (GROUP, side), 0)
+
+    def prepare(i, carry):
+        first = pl.multiple_of(i * 2 * GROUP, 2 * GROUP)
+        sources, targets = [], []
+        for g in range(2):
+            slot = pl.multiple_of(first + g * GROUP, GROUP)
+            dev = slot // capacity
+            column = slot - dev * capacity
+            base = dev * rows
+            at = pl.multiple_of(base + column, GROUP)
+            coords = [recv_ref[pl.ds(at + c * capacity, GROUP), :] - 1.0 for c in range(3)]
+            sources.append(piece_rows(coords, 0.0, 1.0))
+            charge_ref[pl.ds(slot, GROUP), :] = recv_ref[pl.ds(at + 3 * capacity, GROUP), :]
+            tile = recv_ref[pl.ds(pl.multiple_of(base + 4 * capacity, GROUP), GROUP), :]
+            centers = pltpu.roll(tile, lax.rem(side - column, side), 1).T
+            points = [
+                (centers[:GROUP, c : c + 1] - 1.0) + HALF_WIDTH * obs_ref[c, pl.ds(slot, GROUP), :]
                 for c in range(3)
             ]
-            store_feats(stage_b, target_ref, slot, point_rows(targets, SOFT_SQ, True))
-            charge_ref[pl.ds(slot, GROUP), :] = recv_ref[
-                pl.ds(base + 3 * capacity + g * GROUP, GROUP), :
-            ]
-        return carry
-
-    lax.fori_loop(0, n_dev, prepare, 0)
+            targets.append(piece_rows(points, SOFT_SQ, -2.0))
+        spread(source_matrix_ref, sources, source_ref, first)
+        spread(target_matrix_ref, targets, target_ref, first)
+        return carry
+
+    lax.fori_loop(0, blocks // 2, prepare, 0, unroll=2)
 
     def turn(block, u, left_ref):
         left_ref[u] = target_ref[block * GROUP + u].T
@@ -272,12 +285,10 @@
     params = pltpu.CompilerParams(vmem_limit_bytes=VMEM_LIMIT)
 
     mine = lax.dynamic_slice_in_dim(obs_owner, my_index * leaf_dev, leaf_dev)
-    counts = jnp.sum((obs_owner.reshape(n_dev, leaf_dev) == my_index).astype(jnp.int32), axis=1)
-    live = (jnp.arange(capacity, dtype=jnp.int32)[None, :] < counts[:, None]).astype(jnp.int32).reshape(slot_table)
-
     leaf_at = jnp.arange(leaf_dev, dtype=jnp.int32)
     same = (mine[:, None] == mine[None, :]) & (leaf_at[None, :] < leaf_at[:, None])
     rank = jnp.sum(same.astype(jnp.int32), axis=1)
+    rim_rows = from_behind(parent_local[parent_local.shape[0] - RIM :], AXES, 1)
     packed = pl.pallas_call(
         functools.partial(pack_sources, capacity),
         out_shape=jax.ShapeDtypeStruct((n_dev * block_rows, points), F32),
@@ -286,11 +297,18 @@
         compiler_params=params,
         name="pack_sources",
     )(mine, rank, leaf_center.T.reshape(-1), src_coords.transpose(1, 0, 2), src_charge)
+    packed, rim_rows, obs_owner, near_slots = lax.optimization_barrier(
+        (packed, rim_rows, obs_owner, near_slots)
+    )
+    counts = jnp.sum((obs_owner.reshape(n_dev, leaf_dev) == my_index).astype(jnp.int32), axis=1)
+    live = (jnp.arange(capacity, dtype=jnp.int32)[None, :] < counts[:, None]).astype(jnp.int32).reshape(slot_table)
+
+    live = live.reshape(slot_table // points, points)
+    slots = near_slots.reshape(-1)
     recv = lax.all_to_all(
         packed.reshape(n_dev, block_rows, points), AXES, split_axis=0, concat_axis=0, tiled=True
     ).reshape(n_dev * block_rows, points)
 
-    rim_rows = from_behind(parent_local[parent_local.shape[0] - RIM :], AXES, 1)
     parents = jnp.concatenate([rim_rows, parent_local], axis=0)
     moved = jnp.einsum("pr,oqr->opq", parents, l2l_ops, precision=lax.Precision.HIGHEST)
     stacked = moved.reshape(8 * parents.shape[0], width)
@@ -305,6 +323,7 @@
         compiler_params=params,
         name="route_leaves",
     )(child_octant * parents.shape[0] + parent_slot, mine * capacity + rank, child_m2l, stacked)
+    packed_dens, slots, live = lax.optimization_barrier((packed_dens, slots, live))
     dens = lax.all_to_all(
         packed_dens.reshape(n_dev, capacity, lanes), AXES, split_axis=0, concat_axis=0, tiled=True
     ).reshape(slot_table, lanes)
@@ -312,16 +331,14 @@
     obs = obs_offset.transpose(1, 0, 2)
     pairs = slot_table * near_slots.shape[1] * points * points
     near = pl.pallas_call(
-        functools.partial(near_kernel, capacity, n_dev),
+        functools.partial(near_kernel, capacity),
         out_shape=jax.ShapeDtypeStruct((slot_table, points), F32),
-        in_specs=[smem, vmem, vmem],
+        in_specs=[smem, vmem, vmem, vmem, vmem],
         out_specs=vmem,
         scratch_shapes=[
             pltpu.VMEM((slot_table, FEATS, points), BF16),
             pltpu.VMEM((slot_table, FEATS, points), BF16),
             pltpu.VMEM((slot_table, points), F32),
-            pltpu.VMEM((GROUP * FEATS, points), F32),
-            pltpu.VMEM((GROUP * FEATS, points), F32),
             pltpu.VMEM((GROUP, points, FEATS), BF16),
             pltpu.VMEM((GROUP, points, FEATS), BF16),
             pltpu.VMEM((GROUP, points, points), F32),
@@ -330,7 +347,13 @@
         compiler_params=params,
         cost_estimate=pl.CostEstimate(flops=70 * pairs, bytes_accessed=5 * 10**6, transcendentals=pairs),
         name="near_field",
-    )(near_slots.reshape(-1), recv, obs)
+    )(
+        slots,
+        recv,
+        obs,
+        jnp.asarray(spread_matrix(SOURCE_ORDER, False)),
+        jnp.asarray(spread_matrix(TARGET_ORDER, True)),
+    )
     potential = pl.pallas_call(
         far_kernel,
         out_shape=jax.ShapeDtypeStruct((slot_table, points), F32),
@@ -344,7 +367,7 @@
         compiler_params=params,
         cost_estimate=pl.CostEstimate(flops=10**10, bytes_accessed=5 * 10**6, transcendentals=10**7),
         name="far_field",
-    )(dens, obs, near, live.reshape(slot_table // points, points))
+    )(dens, obs, near, live)
     return (leaf_local, potential)
 
 

time: 218 us -> 212 us (0.972)
  starting transfers between devices: 24 us -> 13.6 us
  local copies, waits for them, and re-layouts: 8.55 us -> 14.2 us
  waiting for transfers between devices: 38 us -> 35.5 us
    all_to_all x1, starting transfers between devices: 14.5 us -> 4.12 us  [on_device(): lax.all_to_all(packed_dens.reshape(n_dev, capacity, lanes), AXES, split_a...]
    unnamed x23 -> x30, local copies, waits for them, and re-layouts: 6.48 us -> 9.39 us
  transfers between devices with their start and end apart: 3 -> 3, of which waited for: 2 -> 1; matrix products, arithmetic and copies ran while one was open for 4% -> 6% of each run, Pallas kernels for 49% -> 53%
where the time goes in v7:
time: 212 us
  Pallas kernels  141 us (67%)
  waiting for transfers between devices  35.5 us (17%)
  local copies, waits for them, and re-layouts  14.2 us (7%)
  starting transfers between devices  13.6 us (6%)
  matrix products  6.23 us (3%)
    pallas_call x1, Pallas kernels, on_device(): pl.pallas_call(functools.partial(near_kernel, capacity), out_shape=jax.Sh...  103 us
    all_to_all x1, waiting for transfers between devices, on_device(): lax.all_to_all(packed.reshape(n_dev, block_rows, points), AXES, split_axi...  35.4 us
    pallas_call x1, Pallas kernels, on_device(): pl.pallas_call(far_kernel, out_shape=jax.ShapeDtypeStruct((slot_table, po...  28.2 us
    unnamed x30, local copies, waits for them, and re-layouts  9.39 us
    all_to_all x1, starting transfers between devices, on_device(): lax.all_to_all(packed.reshape(n_dev, block_rows, points), AXES, split_axi...  7.14 us
    dot_general x1, matrix products, on_device(): jnp.einsum('pr,oqr->opq', parents, l2l_ops, precision=lax.Precision.HIGHEST)  6.23 us
    pallas_call x1, Pallas kernels, on_device(): pl.pallas_call(functools.partial(pack_sources, capacity), out_shape=jax.S...  5.44 us
  transfers between devices with their start and end apart: 3, of which 1 were waited for; matrix products, arithmetic and copies ran while one was open for 6% of the time, Pallas kernels for 53%

profile of v7, /device:TPU:0, one launch (start us, length us, event | category | flops | bytes accessed | tf_op | source)
XLA Modules:
  0.0 211.6 jit_solution(16232757847456822566)
XLA Ops:
  0.6 0.7 slice.3
  1.4 2.3 %collective-permute-start = (f32[16,296]{1,0:T(8,128)S(1)}, f32[16,296]{1,0:T(8,128)S(1)}, u32[]{:S(2)}, u32[]{:S(2)}) collective-permute-start(f32[16,296]{1,0:T(8,128)S(1)} %slice.3), channel_id=1, source_target_pairs={{0,1},{1,2},{2,3},{3,4},{4,5},{5,6},{6,7},{7,8},{8,9},{9,10},{10,1... | collective-permute-start | bytes 56840 | tf_op jit(solution)/shard_map/ppermute | solution.py:30
  3.7 0.8 dynamic_slice.3.owner_ref
  4.5 0.3 convert_reduce_fusion.rank_ref
  4.7 0.7 reshape.37.center_ref
  5.5 1.1 copy-done.1
  6.6 0.9 copy-done.4
  7.5 5.4 %pack_sources.1 = f32[4352,128]{1,0:T(8,128)} custom-call(s32[512]{0:T(512)S(1)} %dynamic_slice.3.owner_ref, s32[512]{0:T(512)S(1)} %convert_reduce_fusion.rank_ref, f32[1536]{0:T(1024)S(1)} %reshape.37.center_ref, f32[3,512,128]{2,1,0:T(8,128)S(1)} %bitcast.17, f32[512,128]{1,0:T(8,128)S(1)} %copy-done.4), custom_call_target="tpu_custom_call" | custom-call | tf_op jit(solution)/shard_map/pack_sources/pallas_call | solution.py:292
  13.0 7.1 %all-to-all-start.1 = ((f32[32,136,128]{2,1,0:T(8,128)}), f32[32,136,128]{2,1,0:T(8,128)S(1)}, u32[]{:S(2)}, u32[]{:S(2)}) async-start(f32[32,136,128]{2,1,0:T(8,128)} %bitcast.8), calls=%async_computation.1 | async-start | bytes 4456448 | tf_op jit(solution)/shard_map/all_to_all | solution.py:308
  20.3 1.3 copy.20.m2l_ref
  21.8 0.1 reduce_sum.19
  22.1 1.0 copy.21
  23.1 1.3 reshape.39.slots_ref
  24.4 6.2 %fusion.1 = f32[80,8,296]{2,0,1:T(8,128)S(1)} fusion(f32[8,296,296]{2,1,0:T(8,128)} %param.17, f32[64,296]{1,0:T(8,128)S(1)} %copy-done.9, f32[16,296]{1,0:T(8,128)S(1)} %collective-permute-done), kind=kOutput, calls=%fused_computation.4 | convolution fusion | flops 672914560 | bytes 3656192 | tf_op jit(solution)/shard_map/pr,oqr->opq/dot_general | solution.py:313
  30.6 3.8 %route_leaves.1 = (f32[512,296]{1,0:T(8,128)S(1)}, f32[1024,384]{1,0:T(8,128)S(1)}) custom-call(s32[512]{0:T(512)S(1)} %get-tuple-element.27.index_ref, s32[512]{0:T(512)S(1)} %get-tuple-element.26.dest_ref, f32[512,296]{1,0:T(8,128)S(1)} %copy.20.m2l_ref, f32[640,296]{1,0:T(8,128)S(1)} %bitcast.14), custom_call_target="tpu_custom_call" | custom-call | tf_op jit(solution)/shard_map/route_leaves/pallas_call | solution.py:315
  34.4 1.1 copy-done
  35.5 0.9 copy-done.2
  36.4 35.4 %all-to-all-done.1 = f32[32,136,128]{2,1,0:T(8,128)S(1)} async-done(((f32[32,136,128]{2,1,0:T(8,128)}), f32[32,136,128]{2,1,0:T(8,128)S(1)}, u32[]{:S(2)}, u32[]{:S(2)}) %all-to-all-start.1) | async-done | bytes 2228256 | tf_op jit(solution)/shard_map/all_to_all | solution.py:308
  71.9 4.1 %all-to-all-start = ((f32[32,32,384]{2,1,0:T(8,128)}), f32[32,32,384]{2,1,0:T(8,128)}, u32[]{:S(2)}, u32[]{:S(2)}) async-start(f32[32,32,384]{2,1,0:T(8,128)} %bitcast.16), calls=%async_computation | async-start | bytes 3145728 | tf_op jit(solution)/shard_map/all_to_all | solution.py:327
  76.0 1.1 copy.22
  77.1 1.4 copy-done.5
  78.5 103.4 %near_field.1.near_ref = f32[1024,128]{1,0:T(8,128)S(1)} custom-call(s32[8192]{0:T(1024)S(1)} %reshape.39.slots_ref, f32[4352,128]{1,0:T(8,128)S(1)} %bitcast.15, f32[3,1024,128]{2,1,0:T(8,128)S(1)} %bitcast.18, bf16[256,112]{1,0:T(8,128)(2,1)S(1)} %copy-done.8, bf16[256,112]{1,0:T(8,128)(2,1)S(1)} %copy-done.7), custom_call_target="tpu_custom_call" | custom-call | flops 9395240960 | bytes 5000000 | tf_op jit(solution)/shard_map/near_field/pallas_call | solution.py:333
  182.0 1.4 copy-done.6
  183.4 28.2 %far_field.1 = f32[1024,128]{1,0:T(8,128)} custom-call(f32[1024,384]{1,0:T(8,128)} %bitcast.6.dens_ref, f32[3,1024,128]{2,1,0:T(8,128)S(1)} %bitcast.19, f32[1024,128]{1,0:T(8,128)S(1)} %near_field.1.near_ref, s32[8,128]{1,0:T(8,128)S(1)} %compare_convert_fusion.1.live_ref), custom_call_target="tpu_custom_call" | custom-call | flops 10000000000 | bytes 5000000 | tf_op jit(solution)/shard_map/far_field/pallas_call | solution.py:357
  (33 shorter events, 0.5 us)
Async XLA Ops:
  1.4 11.6 %collective-permute-start = (f32[16,296]{1,0:T(8,128)S(1)}, f32[16,296]{1,0:T(8,128)S(1)}, u32[]{:S(2)}, u32[]{:S(2)}) collective-permute-start(f32[16,296]{1,0:T(8,128)S(1)} %slice.3), channel_id=1, source_target_pairs={{0,1},{1,2},{2,3},{3,4},{4,5},{5,6},{6,7},{7,8},{8,9},{9,10},{10,1... | collective-permute-start | bytes 56840 | tf_op jit(solution)/shard_map/ppermute | solution.py:30
  5.5 1.1 copy-start.1
  6.6 0.9 copy-start.4
  13.0 8.6 %copy-start.10 = (s32[16384]{0:T(1024)S(1)}, s32[16384]{0:T(1024)}, u32[]{:S(2)}) copy-start(s32[16384]{0:T(1024)} %param.21) | copy-start | bytes 196612
  13.0 8.6 %copy-start.12 = (s32[512]{0:T(512)S(1)}, s32[512]{0:T(512)}, u32[]{:S(2)}) copy-start(s32[512]{0:T(512)} %param.14) | copy-start | bytes 6148
  13.0 8.6 %copy-start.13 = (s32[512]{0:T(512)S(1)}, s32[512]{0:T(512)}, u32[]{:S(2)}) copy-start(s32[512]{0:T(512)} %param.15) | copy-start | bytes 6148
  13.0 9.1 %copy-start.11 = (s32[1024,8]{0,1:T(8,128)S(1)}, s32[1024,8]{0,1:T(8,128)}, u32[]{:S(2)}) copy-start(s32[1024,8]{0,1:T(8,128)} %param.23) | copy-start | bytes 98308
  13.0 58.9 %all-to-all-start.1 = ((f32[32,136,128]{2,1,0:T(8,128)}), f32[32,136,128]{2,1,0:T(8,128)S(1)}, u32[]{:S(2)}, u32[]{:S(2)}) async-start(f32[32,136,128]{2,1,0:T(8,128)} %bitcast.8), calls=%async_computation.1 | async-start | bytes 4456448 | tf_op jit(solution)/shard_map/all_to_all | solution.py:308
  20.2 4.2 %copy-start.9 = (f32[64,296]{1,0:T(8,128)S(1)}, f32[64,296]{1,0:T(8,128)}, u32[]{:S(2)}) copy-start(f32[64,296]{1,0:T(8,128)} %param.13) | copy-start | bytes 227332
  34.4 1.1 copy-start
  35.5 0.9 copy-start.2
  36.4 39.6 %copy-start.3 = (f32[512,296]{1,0:T(8,128)S(1)}, f32[512,296]{1,0:T(8,128)}, u32[]{:S(2)}) copy-start(f32[512,296]{1,0:T(8,128)} %copy-done.2) | copy-start | bytes 1818628
  71.9 5.2 %copy-start.7 = (bf16[256,112]{1,0:T(8,128)(2,1)S(1)}, bf16[256,112]{1,0:T(8,128)(2,1)}, u32[]{:S(2)}) copy-start(bf16[256,112]{1,0:T(8,128)(2,1)} %constant.25.clone.target_matrix_ref) | copy-start | bytes 172036
  71.9 5.2 %copy-start.8 = (bf16[256,112]{1,0:T(8,128)(2,1)S(1)}, bf16[256,112]{1,0:T(8,128)(2,1)}, u32[]{:S(2)}) copy-start(bf16[256,112]{1,0:T(8,128)(2,1)} %constant.24.clone.source_matrix_ref) | copy-start | bytes 172036
  71.9 110.0 %all-to-all-start = ((f32[32,32,384]{2,1,0:T(8,128)}), f32[32,32,384]{2,1,0:T(8,128)}, u32[]{:S(2)}, u32[]{:S(2)}) async-start(f32[32,32,384]{2,1,0:T(8,128)} %bitcast.16), calls=%async_computation | async-start | bytes 3145728 | tf_op jit(solution)/shard_map/all_to_all | solution.py:327
  77.1 1.4 copy-start.5
  181.9 1.4 copy-start.6

commit v8 on v7

--- a/solution.py
+++ b/solution.py
@@ -44,25 +44,26 @@
 
 
 def split(value):
-    high = value.astype(BF16).astype(F32)
-    rest = value - high
-    mid = rest.astype(BF16).astype(F32)
-    return high, mid, rest - mid
+    high = value.astype(BF16)
+    rest = value - high.astype(F32)
+    mid = rest.astype(BF16)
+    return high, mid, (rest - mid.astype(F32)).astype(BF16)
 
 
 SOURCE_ORDER = ("h", "h", "h", "m", "m", "l")
 TARGET_ORDER = ("h", "m", "l", "h", "m", "h")
-N_PIECES = 14
+N_PIECES = 13
+PACK = 2 * GROUP
 
 
 def spread_matrix(order, norm_first):
     start = {"h": 0, "m": 3, "l": 6}
     pieces = [start[name] + c for c in range(3) for name in order]
     pieces += [9, 10, 11, 12, 12, 12] if norm_first else [12, 12, 12, 9, 10, 11]
-    table = np.zeros((GROUP * FEATS, N_PIECES * GROUP), jnp.bfloat16)
-    for u in range(GROUP):
+    table = np.zeros((PACK * FEATS, N_PIECES * PACK), jnp.bfloat16)
+    for u in range(PACK):
         for f, piece in enumerate(pieces):
-            table[u * FEATS + f, piece * GROUP + u] = 1.0
+            table[u * FEATS + f, piece * PACK + u] = 1.0
     return table
 
 
@@ -70,17 +71,17 @@
     norm = coords[0] * coords[0] + coords[1] * coords[1] + coords[2] * coords[2] + extra
     parts = [split(scale * value) for value in coords]
     rows = [part[level] for level in range(3) for part in parts]
-    rows += list(split(norm)) + [jnp.ones_like(norm), jnp.zeros_like(norm)]
-    return jnp.concatenate(rows, axis=0).astype(BF16)
+    rows += list(split(norm)) + [jnp.ones(norm.shape, BF16)]
+    return jnp.concatenate(rows, axis=0)
 
 
 def spread(matrix_ref, blocks, out_ref, slot):
     pieces = jnp.concatenate(blocks, axis=1)
-    rows = jnp.dot(matrix_ref[...], pieces, preferred_element_type=F32).astype(BF16)
+    rows = jnp.dot(matrix_ref[...], pieces, preferred_element_type=F32)
     lanes = blocks[0].shape[1]
     for i in range(2):
-        block = rows[:, i * lanes : (i + 1) * lanes].reshape(GROUP, FEATS, lanes)
-        out_ref[pl.ds(slot + i * GROUP, GROUP)] = block
+        block = rows[:, i * lanes : (i + 1) * lanes].astype(BF16).reshape(PACK, FEATS, lanes)
+        out_ref[pl.ds(slot + i * PACK, PACK)] = block
 
 
 def lane_sums(block):
@@ -147,30 +148,39 @@
     side = out_ref.shape[1]
     sub = lax.broadcasted_iota(jnp.int32, (GROUP, side), 0)
 
+    def group_points(slot):
+        dev = slot // capacity
+        column = slot - dev * capacity
+        base = dev * rows
+        at = pl.multiple_of(base + column, GROUP)
+        coords = [recv_ref[pl.ds(at + c * capacity, GROUP), :] - 1.0 for c in range(3)]
+        charge_ref[pl.ds(slot, GROUP), :] = recv_ref[pl.ds(at + 3 * capacity, GROUP), :]
+        tile = recv_ref[pl.ds(pl.multiple_of(base + 4 * capacity, GROUP), GROUP), :]
+        centers = pltpu.roll(tile, lax.rem(side - column, side), 1).T
+        targets = [
+            (centers[:GROUP, c : c + 1] - 1.0) + HALF_WIDTH * obs_ref[c, pl.ds(slot, GROUP), :]
+            for c in range(3)
+        ]
+        return coords, targets
+
     def prepare(i, carry):
-        first = pl.multiple_of(i * 2 * GROUP, 2 * GROUP)
+        first = pl.multiple_of(i * 2 * PACK, 2 * PACK)
         sources, targets = [], []
-        for g in range(2):
-            slot = pl.multiple_of(first + g * GROUP, GROUP)
-            dev = slot // capacity
-            column = slot - dev * capacity
-            base = dev * rows
-            at = pl.multiple_of(base + column, GROUP)
-            coords = [recv_ref[pl.ds(at + c * capacity, GROUP), :] - 1.0 for c in range(3)]
+        for half in range(2):
+            one, two = (
+                group_points(pl.multiple_of(first + half * PACK + g * GROUP, GROUP)) for g in range(2)
+            )
+            coords, points = (
+                [jnp.concatenate([left, right], axis=0) for left, right in zip(one[k], two[k])]
+                for k in range(2)
+            )
             sources.append(piece_rows(coords, 0.0, 1.0))
-            charge_ref[pl.ds(slot, GROUP), :] = recv_ref[pl.ds(at + 3 * capacity, GROUP), :]
-            tile = recv_ref[pl.ds(pl.multiple_of(base + 4 * capacity, GROUP), GROUP), :]
-            centers = pltpu.roll(tile, lax.rem(side - column, side), 1).T
-            points = [
-                (centers[:GROUP, c : c + 1] - 1.0) + HALF_WIDTH * obs_ref[c, pl.ds(slot, GROUP), :]
-                for c in range(3)
-            ]
             targets.append(piece_rows(points, SOFT_SQ, -2.0))
         spread(source_matrix_ref, sources, source_ref, first)
         spread(target_matrix_ref, targets, target_ref, first)
         return carry
 
-    lax.fori_loop(0, blocks // 2, prepare, 0, unroll=2)
+    lax.fori_loop(0, out_ref.shape[0] // (2 * PACK), prepare, 0, unroll=2)
 
     def turn(block, u, left_ref):
         left_ref[u] = target_ref[block * GROUP + u].T
@@ -250,7 +260,7 @@
             far_ref[place, :] = (totals[0] + totals[1]) + (totals[2] + totals[3])
             return carry
 
-        lax.fori_loop(0, side // GROUP, points, 0)
+        lax.fori_loop(0, side // GROUP, points, 0, unroll=2)
         near = near_ref[pl.ds(first, side), :].T
         total = far_ref[...] * (1.0 / (FOUR_PI * HALF_WIDTH)) + near * (1.0 / FOUR_PI)
         total = jnp.where(live_ref[pl.ds(t, 1), :] > 0, total, 0.0)

time: 212 us -> 205 us (0.967)
  Pallas kernels: 141 us -> 132 us
    pallas_call x1, Pallas kernels: 103 us -> 95.5 us  [on_device(): pl.pallas_call(functools.partial(near_kernel, capacity), out_shape=jax.Sh...]
  transfers between devices with their start and end apart: 3 -> 3, of which waited for: 1 -> 1; matrix products, arithmetic and copies ran while one was open for 6% -> 6% of each run, Pallas kernels for 53% -> 51%
where the time goes in v8:
time: 205 us; the launch traced here: 204 us
  Pallas kernels  132 us (64%)
  waiting for transfers between devices  35.5 us (17%)
  local copies, waits for them, and re-layouts  15.2 us (7%)
  starting transfers between devices  13.6 us (7%)
  matrix products  6.23 us (3%)
    pallas_call x1, Pallas kernels, on_device(): pl.pallas_call(functools.partial(near_kernel, capacity), out_shape=jax.Sh...  95.5 us
    all_to_all x1, waiting for transfers between devices, on_device(): lax.all_to_all(packed.reshape(n_dev, block_rows, points), AXES, split_axi...  35.4 us
    pallas_call x1, Pallas kernels, on_device(): pl.pallas_call(far_kernel, out_shape=jax.ShapeDtypeStruct((slot_table, po...  27.4 us
    unnamed x30, local copies, waits for them, and re-layouts  10.3 us
    all_to_all x1, starting transfers between devices, on_device(): lax.all_to_all(packed.reshape(n_dev, block_rows, points), AXES, split_axi...  7.14 us
    dot_general x1, matrix products, on_device(): jnp.einsum('pr,oqr->opq', parents, l2l_ops, precision=lax.Precision.HIGHEST)  6.23 us
    pallas_call x1, Pallas kernels, on_device(): pl.pallas_call(functools.partial(pack_sources, capacity), out_shape=jax.S...  5.43 us
    all_to_all x1, starting transfers between devices, on_device(): lax.all_to_all(packed_dens.reshape(n_dev, capacity, lanes), AXES, split_a...  4.12 us
  transfers between devices with their start and end apart: 3, of which 1 were waited for; matrix products, arithmetic and copies ran while one was open for 6% of the time, Pallas kernels for 51%

profile of v8, /device:TPU:0, one launch (start us, length us, event | category | flops | bytes accessed | tf_op | source)
XLA Modules:
  0.0 203.8 jit_solution(8728435116951986484)
XLA Ops:
  0.6 0.7 slice.3
  1.4 2.3 %collective-permute-start = (f32[16,296]{1,0:T(8,128)S(1)}, f32[16,296]{1,0:T(8,128)S(1)}, u32[]{:S(2)}, u32[]{:S(2)}) collective-permute-start(f32[16,296]{1,0:T(8,128)S(1)} %slice.3), channel_id=1, source_target_pairs={{0,1},{1,2},{2,3},{3,4},{4,5},{5,6},{6,7},{7,8},{8,9},{9,10},{10,1... | collective-permute-start | bytes 56840 | tf_op jit(solution)/shard_map/ppermute | solution.py:30
  3.7 0.8 dynamic_slice.3.owner_ref
  4.5 0.3 convert_reduce_fusion.rank_ref
  4.7 0.7 reshape.37.center_ref
  5.5 1.1 copy-done.1
  6.6 0.9 copy-done.4
  7.5 5.4 %pack_sources.1 = f32[4352,128]{1,0:T(8,128)} custom-call(s32[512]{0:T(512)S(1)} %dynamic_slice.3.owner_ref, s32[512]{0:T(512)S(1)} %convert_reduce_fusion.rank_ref, f32[1536]{0:T(1024)S(1)} %reshape.37.center_ref, f32[3,512,128]{2,1,0:T(8,128)S(1)} %bitcast.17, f32[512,128]{1,0:T(8,128)S(1)} %copy-done.4), custom_call_target="tpu_custom_call" | custom-call | tf_op jit(solution)/shard_map/pack_sources/pallas_call | solution.py:302
  13.0 7.1 %all-to-all-start.1 = ((f32[32,136,128]{2,1,0:T(8,128)}), f32[32,136,128]{2,1,0:T(8,128)S(1)}, u32[]{:S(2)}, u32[]{:S(2)}) async-start(f32[32,136,128]{2,1,0:T(8,128)} %bitcast.8), calls=%async_computation.1 | async-start | bytes 4456448 | tf_op jit(solution)/shard_map/all_to_all | solution.py:318
  20.3 1.3 copy.20.m2l_ref
  22.1 1.0 copy.21
  23.1 1.3 reshape.39.slots_ref
  24.4 6.2 %fusion.1 = f32[80,8,296]{2,0,1:T(8,128)S(1)} fusion(f32[8,296,296]{2,1,0:T(8,128)} %param.17, f32[64,296]{1,0:T(8,128)S(1)} %copy-done.9, f32[16,296]{1,0:T(8,128)S(1)} %collective-permute-done), kind=kOutput, calls=%fused_computation.4 | convolution fusion | flops 672914560 | bytes 3656192 | tf_op jit(solution)/shard_map/pr,oqr->opq/dot_general | solution.py:323
  30.6 3.8 %route_leaves.1 = (f32[512,296]{1,0:T(8,128)S(1)}, f32[1024,384]{1,0:T(8,128)S(1)}) custom-call(s32[512]{0:T(512)S(1)} %get-tuple-element.27.index_ref, s32[512]{0:T(512)S(1)} %get-tuple-element.26.dest_ref, f32[512,296]{1,0:T(8,128)S(1)} %copy.20.m2l_ref, f32[640,296]{1,0:T(8,128)S(1)} %bitcast.14), custom_call_target="tpu_custom_call" | custom-call | tf_op jit(solution)/shard_map/route_leaves/pallas_call | solution.py:325
  34.4 1.1 copy-done
  35.5 0.9 copy-done.2
  36.4 35.4 %all-to-all-done.1 = f32[32,136,128]{2,1,0:T(8,128)S(1)} async-done(((f32[32,136,128]{2,1,0:T(8,128)}), f32[32,136,128]{2,1,0:T(8,128)S(1)}, u32[]{:S(2)}, u32[]{:S(2)}) %all-to-all-start.1) | async-done | bytes 2228256 | tf_op jit(solution)/shard_map/all_to_all | solution.py:318
  71.9 4.1 %all-to-all-start = ((f32[32,32,384]{2,1,0:T(8,128)}), f32[32,32,384]{2,1,0:T(8,128)}, u32[]{:S(2)}, u32[]{:S(2)}) async-start(f32[32,32,384]{2,1,0:T(8,128)} %bitcast.16), calls=%async_computation | async-start | bytes 3145728 | tf_op jit(solution)/shard_map/all_to_all | solution.py:337
  76.0 1.1 copy.22
  77.1 1.4 copy-done.5
  78.5 0.9 copy-done.8
  79.5 95.5 %near_field.1.near_ref = f32[1024,128]{1,0:T(8,128)S(1)} custom-call(s32[8192]{0:T(1024)S(1)} %reshape.39.slots_ref, f32[4352,128]{1,0:T(8,128)S(1)} %bitcast.15, f32[3,1024,128]{2,1,0:T(8,128)S(1)} %bitcast.18, bf16[512,208]{1,0:T(8,128)(2,1)S(1)} %copy-done.8, bf16[512,208]{1,0:T(8,128)(2,1)S(1)} %copy-done.7), custom_call_target="tpu_custom_call" | custom-call | flops 9395240960 | bytes 5000000 | tf_op jit(solution)/shard_map/near_field/pallas_call | solution.py:343
  175.0 1.4 copy-done.6
  176.4 27.4 %far_field.1 = f32[1024,128]{1,0:T(8,128)} custom-call(f32[1024,384]{1,0:T(8,128)} %bitcast.6.dens_ref, f32[3,1024,128]{2,1,0:T(8,128)S(1)} %bitcast.19, f32[1024,128]{1,0:T(8,128)S(1)} %near_field.1.near_ref, s32[8,128]{1,0:T(8,128)S(1)} %compare_convert_fusion.1.live_ref), custom_call_target="tpu_custom_call" | custom-call | flops 10000000000 | bytes 5000000 | tf_op jit(solution)/shard_map/far_field/pallas_call | solution.py:367
  (33 shorter events, 0.6 us)
Async XLA Ops:
  1.4 11.6 %collective-permute-start = (f32[16,296]{1,0:T(8,128)S(1)}, f32[16,296]{1,0:T(8,128)S(1)}, u32[]{:S(2)}, u32[]{:S(2)}) collective-permute-start(f32[16,296]{1,0:T(8,128)S(1)} %slice.3), channel_id=1, source_target_pairs={{0,1},{1,2},{2,3},{3,4},{4,5},{5,6},{6,7},{7,8},{8,9},{9,10},{10,1... | collective-permute-start | bytes 56840 | tf_op jit(solution)/shard_map/ppermute | solution.py:30
  5.5 1.1 copy-start.1
  6.6 0.9 copy-start.4
  13.0 8.6 %copy-start.10 = (s32[16384]{0:T(1024)S(1)}, s32[16384]{0:T(1024)}, u32[]{:S(2)}) copy-start(s32[16384]{0:T(1024)} %param.21) | copy-start | bytes 196612
  13.0 8.6 %copy-start.12 = (s32[512]{0:T(512)S(1)}, s32[512]{0:T(512)}, u32[]{:S(2)}) copy-start(s32[512]{0:T(512)} %param.14) | copy-start | bytes 6148
  13.0 8.6 %copy-start.13 = (s32[512]{0:T(512)S(1)}, s32[512]{0:T(512)}, u32[]{:S(2)}) copy-start(s32[512]{0:T(512)} %param.15) | copy-start | bytes 6148
  13.0 9.1 %copy-start.11 = (s32[1024,8]{0,1:T(8,128)S(1)}, s32[1024,8]{0,1:T(8,128)}, u32[]{:S(2)}) copy-start(s32[1024,8]{0,1:T(8,128)} %param.23) | copy-start | bytes 98308
  13.0 58.9 %all-to-all-start.1 = ((f32[32,136,128]{2,1,0:T(8,128)}), f32[32,136,128]{2,1,0:T(8,128)S(1)}, u32[]{:S(2)}, u32[]{:S(2)}) async-start(f32[32,136,128]{2,1,0:T(8,128)} %bitcast.8), calls=%async_computation.1 | async-start | bytes 4456448 | tf_op jit(solution)/shard_map/all_to_all | solution.py:318
  20.2 4.2 %copy-start.9 = (f32[64,296]{1,0:T(8,128)S(1)}, f32[64,296]{1,0:T(8,128)}, u32[]{:S(2)}) copy-start(f32[64,296]{1,0:T(8,128)} %param.13) | copy-start | bytes 227332
  34.4 1.1 copy-start
  35.5 0.9 copy-start.2
  36.4 39.6 %copy-start.3 = (f32[512,296]{1,0:T(8,128)S(1)}, f32[512,296]{1,0:T(8,128)}, u32[]{:S(2)}) copy-start(f32[512,296]{1,0:T(8,128)} %copy-done.2) | copy-start | bytes 1818628
  71.9 5.2 %copy-start.7 = (bf16[512,208]{1,0:T(8,128)(2,1)S(1)}, bf16[512,208]{1,0:T(8,128)(2,1)}, u32[]{:S(2)}) copy-start(bf16[512,208]{1,0:T(8,128)(2,1)} %constant.25.clone.target_matrix_ref) | copy-start | bytes 638980
  71.9 103.1 %all-to-all-start = ((f32[32,32,384]{2,1,0:T(8,128)}), f32[32,32,384]{2,1,0:T(8,128)}, u32[]{:S(2)}, u32[]{:S(2)}) async-start(f32[32,32,384]{2,1,0:T(8,128)} %bitcast.16), calls=%async_computation | async-start | bytes 3145728 | tf_op jit(solution)/shard_map/all_to_all | solution.py:337
  77.1 1.4 copy-start.5
  78.5 0.9 copy-start.8
  175.0 1.4 copy-start.6

commit v9 on v8

--- a/solution.py
+++ b/solution.py
@@ -111,10 +111,10 @@
             center_ref[j],
             jnp.where(sub == 1, center_ref[leaves + j], center_ref[2 * leaves + j]),
         )
-        out_ref[place, :] = jnp.where(lane == rank, value, out_ref[place, :])
+        pltpu.store(out_ref.at[place, :], value, mask=lane == rank)
         return carry
 
-    lax.fori_loop(0, leaves, step, 0, unroll=4)
+    lax.fori_loop(0, leaves, step, 0, unroll=8)
 
 
 def route_leaves(index_ref, dest_ref, m2l_ref, moved_ref, leaf_ref, out_ref):
@@ -180,7 +180,7 @@
         spread(target_matrix_ref, targets, target_ref, first)
         return carry
 
-    lax.fori_loop(0, out_ref.shape[0] // (2 * PACK), prepare, 0, unroll=2)
+    lax.fori_loop(0, out_ref.shape[0] // (2 * PACK), prepare, 0, unroll=4)
 
     def turn(block, u, left_ref):
         left_ref[u] = target_ref[block * GROUP + u].T
@@ -219,7 +219,7 @@
         half(one, two, jnp.minimum(two + 1, blocks - 1), left_b, left_a, total_a, total_b)
         return carry
 
-    lax.fori_loop(0, blocks // 2, step, 0)
+    lax.fori_loop(0, blocks // 2, step, 0, unroll=2)
     sums = None
     for u in range(GROUP):
         part = lane_sums(total_b[u])

time: 205 us -> 196 us (0.956)
  Pallas kernels: 132 us -> 124 us
    pallas_call x1, Pallas kernels: 95.5 us -> 87.7 us  [on_device(): pl.pallas_call(functools.partial(near_kernel, capacity), out_shape=jax.Sh...]
  transfers between devices with their start and end apart: 3 -> 3, of which waited for: 1 -> 1; matrix products, arithmetic and copies ran while one was open for 6% -> 7% of each run, Pallas kernels for 51% -> 49%
where the time goes in v9:
time: 196 us
  Pallas kernels  124 us (63%)
  waiting for transfers between devices  35.5 us (18%)
  local copies, waits for them, and re-layouts  15.2 us (8%)
  starting transfers between devices  13.6 us (7%)
  matrix products  6.23 us (3%)
    pallas_call x1, Pallas kernels, on_device(): pl.pallas_call(functools.partial(near_kernel, capacity), out_shape=jax.Sh...  87.7 us
    all_to_all x1, waiting for transfers between devices, on_device(): lax.all_to_all(packed.reshape(n_dev, block_rows, points), AXES, split_axi...  35.4 us
    pallas_call x1, Pallas kernels, on_device(): pl.pallas_call(far_kernel, out_shape=jax.ShapeDtypeStruct((slot_table, po...  27.4 us
    unnamed x30, local copies, waits for them, and re-layouts  10.3 us
    all_to_all x1, starting transfers between devices, on_device(): lax.all_to_all(packed.reshape(n_dev, block_rows, points), AXES, split_axi...  7.14 us
    dot_general x1, matrix products, on_device(): jnp.einsum('pr,oqr->opq', parents, l2l_ops, precision=lax.Precision.HIGHEST)  6.23 us
    pallas_call x1, Pallas kernels, on_device(): pl.pallas_call(functools.partial(pack_sources, capacity), out_shape=jax.S...  5.06 us
    all_to_all x1, starting transfers between devices, on_device(): lax.all_to_all(packed_dens.reshape(n_dev, capacity, lanes), AXES, split_a...  4.12 us
  transfers between devices with their start and end apart: 3, of which 1 were waited for; matrix products, arithmetic and copies ran while one was open for 7% of the time, Pallas kernels for 49%

profile of v9, /device:TPU:0, one launch (start us, length us, event | category | flops | bytes accessed | tf_op | source)
XLA Modules:
  0.0 195.7 jit_solution(1708177521852633038)
XLA Ops:
  0.6 0.7 slice.3
  1.4 2.3 %collective-permute-start = (f32[16,296]{1,0:T(8,128)S(1)}, f32[16,296]{1,0:T(8,128)S(1)}, u32[]{:S(2)}, u32[]{:S(2)}) collective-permute-start(f32[16,296]{1,0:T(8,128)S(1)} %slice.3), channel_id=1, source_target_pairs={{0,1},{1,2},{2,3},{3,4},{4,5},{5,6},{6,7},{7,8},{8,9},{9,10},{10,1... | collective-permute-start | bytes 56840 | tf_op jit(solution)/shard_map/ppermute | solution.py:30
  3.7 0.8 dynamic_slice.3.owner_ref
  4.5 0.3 convert_reduce_fusion.rank_ref
  4.7 0.7 reshape.37.center_ref
  5.5 1.1 copy-done.1
  6.6 0.9 copy-done.4
  7.5 5.1 %pack_sources.1 = f32[4352,128]{1,0:T(8,128)} custom-call(s32[512]{0:T(512)S(1)} %dynamic_slice.3.owner_ref, s32[512]{0:T(512)S(1)} %convert_reduce_fusion.rank_ref, f32[1536]{0:T(1024)S(1)} %reshape.37.center_ref, f32[3,512,128]{2,1,0:T(8,128)S(1)} %bitcast.17, f32[512,128]{1,0:T(8,128)S(1)} %copy-done.4), custom_call_target="tpu_custom_call" | custom-call | tf_op jit(solution)/shard_map/pack_sources/pallas_call | solution.py:302
  12.6 7.1 %all-to-all-start.1 = ((f32[32,136,128]{2,1,0:T(8,128)}), f32[32,136,128]{2,1,0:T(8,128)S(1)}, u32[]{:S(2)}, u32[]{:S(2)}) async-start(f32[32,136,128]{2,1,0:T(8,128)} %bitcast.8), calls=%async_computation.1 | async-start | bytes 4456448 | tf_op jit(solution)/shard_map/all_to_all | solution.py:318
  19.9 1.3 copy.20.m2l_ref
  21.7 1.0 copy.21
  22.7 1.3 reshape.39.slots_ref
  24.0 6.2 %fusion.1 = f32[80,8,296]{2,0,1:T(8,128)S(1)} fusion(f32[8,296,296]{2,1,0:T(8,128)} %param.17, f32[64,296]{1,0:T(8,128)S(1)} %copy-done.9, f32[16,296]{1,0:T(8,128)S(1)} %collective-permute-done), kind=kOutput, calls=%fused_computation.4 | convolution fusion | flops 672914560 | bytes 3656192 | tf_op jit(solution)/shard_map/pr,oqr->opq/dot_general | solution.py:323
  30.3 3.8 %route_leaves.1 = (f32[512,296]{1,0:T(8,128)S(1)}, f32[1024,384]{1,0:T(8,128)S(1)}) custom-call(s32[512]{0:T(512)S(1)} %get-tuple-element.27.index_ref, s32[512]{0:T(512)S(1)} %get-tuple-element.26.dest_ref, f32[512,296]{1,0:T(8,128)S(1)} %copy.20.m2l_ref, f32[640,296]{1,0:T(8,128)S(1)} %bitcast.14), custom_call_target="tpu_custom_call" | custom-call | tf_op jit(solution)/shard_map/route_leaves/pallas_call | solution.py:325
  34.0 1.1 copy-done
  35.2 0.9 copy-done.2
  36.1 35.4 %all-to-all-done.1 = f32[32,136,128]{2,1,0:T(8,128)S(1)} async-done(((f32[32,136,128]{2,1,0:T(8,128)}), f32[32,136,128]{2,1,0:T(8,128)S(1)}, u32[]{:S(2)}, u32[]{:S(2)}) %all-to-all-start.1) | async-done | bytes 2228256 | tf_op jit(solution)/shard_map/all_to_all | solution.py:318
  71.5 4.1 %all-to-all-start = ((f32[32,32,384]{2,1,0:T(8,128)}), f32[32,32,384]{2,1,0:T(8,128)}, u32[]{:S(2)}, u32[]{:S(2)}) async-start(f32[32,32,384]{2,1,0:T(8,128)} %bitcast.16), calls=%async_computation | async-start | bytes 3145728 | tf_op jit(solution)/shard_map/all_to_all | solution.py:337
  75.7 1.1 copy.22
  76.7 1.4 copy-done.5
  78.1 0.9 copy-done.8
  79.1 87.7 %near_field.1.near_ref = f32[1024,128]{1,0:T(8,128)S(1)} custom-call(s32[8192]{0:T(1024)S(1)} %reshape.39.slots_ref, f32[4352,128]{1,0:T(8,128)S(1)} %bitcast.15, f32[3,1024,128]{2,1,0:T(8,128)S(1)} %bitcast.18, bf16[512,208]{1,0:T(8,128)(2,1)S(1)} %copy-done.8, bf16[512,208]{1,0:T(8,128)(2,1)S(1)} %copy-done.7), custom_call_target="tpu_custom_call" | custom-call | flops 9395240960 | bytes 5000000 | tf_op jit(solution)/shard_map/near_field/pallas_call | solution.py:343
  166.9 1.4 copy-done.6
  168.3 27.4 %far_field.1 = f32[1024,128]{1,0:T(8,128)} custom-call(f32[1024,384]{1,0:T(8,128)} %bitcast.6.dens_ref, f32[3,1024,128]{2,1,0:T(8,128)S(1)} %bitcast.19, f32[1024,128]{1,0:T(8,128)S(1)} %near_field.1.near_ref, s32[8,128]{1,0:T(8,128)S(1)} %compare_convert_fusion.1.live_ref), custom_call_target="tpu_custom_call" | custom-call | flops 10000000000 | bytes 5000000 | tf_op jit(solution)/shard_map/far_field/pallas_call | solution.py:367
  (33 shorter events, 0.6 us)
Async XLA Ops:
  1.4 11.2 %collective-permute-start = (f32[16,296]{1,0:T(8,128)S(1)}, f32[16,296]{1,0:T(8,128)S(1)}, u32[]{:S(2)}, u32[]{:S(2)}) collective-permute-start(f32[16,296]{1,0:T(8,128)S(1)} %slice.3), channel_id=1, source_target_pairs={{0,1},{1,2},{2,3},{3,4},{4,5},{5,6},{6,7},{7,8},{8,9},{9,10},{10,1... | collective-permute-start | bytes 56840 | tf_op jit(solution)/shard_map/ppermute | solution.py:30
  5.5 1.1 copy-start.1
  6.6 0.9 copy-start.4
  12.6 8.6 %copy-start.10 = (s32[16384]{0:T(1024)S(1)}, s32[16384]{0:T(1024)}, u32[]{:S(2)}) copy-start(s32[16384]{0:T(1024)} %param.21) | copy-start | bytes 196612
  12.6 8.6 %copy-start.12 = (s32[512]{0:T(512)S(1)}, s32[512]{0:T(512)}, u32[]{:S(2)}) copy-start(s32[512]{0:T(512)} %param.14) | copy-start | bytes 6148
  12.6 8.6 %copy-start.13 = (s32[512]{0:T(512)S(1)}, s32[512]{0:T(512)}, u32[]{:S(2)}) copy-start(s32[512]{0:T(512)} %param.15) | copy-start | bytes 6148
  12.6 9.1 %copy-start.11 = (s32[1024,8]{0,1:T(8,128)S(1)}, s32[1024,8]{0,1:T(8,128)}, u32[]{:S(2)}) copy-start(s32[1024,8]{0,1:T(8,128)} %param.23) | copy-start | bytes 98308
  12.6 58.9 %all-to-all-start.1 = ((f32[32,136,128]{2,1,0:T(8,128)}), f32[32,136,128]{2,1,0:T(8,128)S(1)}, u32[]{:S(2)}, u32[]{:S(2)}) async-start(f32[32,136,128]{2,1,0:T(8,128)} %bitcast.8), calls=%async_computation.1 | async-start | bytes 4456448 | tf_op jit(solution)/shard_map/all_to_all | solution.py:318
  19.8 4.2 %copy-start.9 = (f32[64,296]{1,0:T(8,128)S(1)}, f32[64,296]{1,0:T(8,128)}, u32[]{:S(2)}) copy-start(f32[64,296]{1,0:T(8,128)} %param.13) | copy-start | bytes 227332
  34.0 1.1 copy-start
  35.2 0.9 copy-start.2
  36.1 39.6 %copy-start.3 = (f32[512,296]{1,0:T(8,128)S(1)}, f32[512,296]{1,0:T(8,128)}, u32[]{:S(2)}) copy-start(f32[512,296]{1,0:T(8,128)} %copy-done.2) | copy-start | bytes 1818628
  71.5 5.2 %copy-start.7 = (bf16[512,208]{1,0:T(8,128)(2,1)S(1)}, bf16[512,208]{1,0:T(8,128)(2,1)}, u32[]{:S(2)}) copy-start(bf16[512,208]{1,0:T(8,128)(2,1)} %constant.25.clone.target_matrix_ref) | copy-start | bytes 638980
  71.5 95.3 %all-to-all-start = ((f32[32,32,384]{2,1,0:T(8,128)}), f32[32,32,384]{2,1,0:T(8,128)}, u32[]{:S(2)}, u32[]{:S(2)}) async-start(f32[32,32,384]{2,1,0:T(8,128)} %bitcast.16), calls=%async_computation | async-start | bytes 3145728 | tf_op jit(solution)/shard_map/all_to_all | solution.py:337
  76.7 1.4 copy-start.5
  78.1 0.9 copy-start.8
  166.8 1.4 copy-start.6

commit v10 on v9

--- a/solution.py
+++ b/solution.py
@@ -180,7 +180,7 @@
         spread(target_matrix_ref, targets, target_ref, first)
         return carry
 
-    lax.fori_loop(0, out_ref.shape[0] // (2 * PACK), prepare, 0, unroll=4)
+    lax.fori_loop(0, out_ref.shape[0] // (2 * PACK), prepare, 0, unroll=8)
 
     def turn(block, u, left_ref):
         left_ref[u] = target_ref[block * GROUP + u].T
@@ -219,7 +219,7 @@
         half(one, two, jnp.minimum(two + 1, blocks - 1), left_b, left_a, total_a, total_b)
         return carry
 
-    lax.fori_loop(0, blocks // 2, step, 0, unroll=2)
+    lax.fori_loop(0, blocks // 2, step, 0, unroll=4)
     sums = None
     for u in range(GROUP):
         part = lane_sums(total_b[u])

time: 196 us -> 193 us (0.985)
  Pallas kernels: 124 us -> 120 us
    pallas_call x1, Pallas kernels: 87.7 us -> 84.1 us  [on_device(): pl.pallas_call(functools.partial(near_kernel, capacity), out_shape=jax.Sh...]
  transfers between devices with their start and end apart: 3 -> 3, of which waited for: 1 -> 1; matrix products, arithmetic and copies ran while one was open for 7% -> 7% of each run, Pallas kernels for 49% -> 48%
where the time goes in v10:
time: 193 us; the launch traced here: 192 us
  Pallas kernels  120 us (62%)
  waiting for transfers between devices  35.4 us (18%)
  local copies, waits for them, and re-layouts  15.2 us (8%)
  starting transfers between devices  13.8 us (7%)
  matrix products  6.24 us (3%)
    pallas_call x1, Pallas kernels, on_device(): pl.pallas_call(functools.partial(near_kernel, capacity), out_shape=jax.Sh...  84.1 us
    all_to_all x1, waiting for transfers between devices, on_device(): lax.all_to_all(packed.reshape(n_dev, block_rows, points), AXES, split_axi...  35.4 us
    pallas_call x1, Pallas kernels, on_device(): pl.pallas_call(far_kernel, out_shape=jax.ShapeDtypeStruct((slot_table, po...  27.4 us
    unnamed x30, local copies, waits for them, and re-layouts  10.3 us
    all_to_all x1, starting transfers between devices, on_device(): lax.all_to_all(packed.reshape(n_dev, block_rows, points), AXES, split_axi...  7.14 us
    dot_general x1, matrix products, on_device(): jnp.einsum('pr,oqr->opq', parents, l2l_ops, precision=lax.Precision.HIGHEST)  6.24 us
    pallas_call x1, Pallas kernels, on_device(): pl.pallas_call(functools.partial(pack_sources, capacity), out_shape=jax.S...  5.06 us
    all_to_all x1, starting transfers between devices, on_device(): lax.all_to_all(packed_dens.reshape(n_dev, capacity, lanes), AXES, split_a...  4.3 us
  transfers between devices with their start and end apart: 3, of which 1 were waited for; matrix products, arithmetic and copies ran while one was open for 7% of the time, Pallas kernels for 48%

profile of v10, /device:TPU:0, one launch (start us, length us, event | category | flops | bytes accessed | tf_op | source)
XLA Modules:
  0.0 192.2 jit_solution(4512553357689253129)
XLA Ops:
  0.6 0.7 slice.3
  1.4 2.3 %collective-permute-start = (f32[16,296]{1,0:T(8,128)S(1)}, f32[16,296]{1,0:T(8,128)S(1)}, u32[]{:S(2)}, u32[]{:S(2)}) collective-permute-start(f32[16,296]{1,0:T(8,128)S(1)} %slice.3), channel_id=1, source_target_pairs={{0,1},{1,2},{2,3},{3,4},{4,5},{5,6},{6,7},{7,8},{8,9},{9,10},{10,1... | collective-permute-start | bytes 56840 | tf_op jit(solution)/shard_map/ppermute | solution.py:30
  3.7 0.8 dynamic_slice.3.owner_ref
  4.5 0.3 convert_reduce_fusion.rank_ref
  4.7 0.7 reshape.37.center_ref
  5.5 1.1 copy-done.1
  6.6 0.9 copy-done.4
  7.5 5.1 %pack_sources.1 = f32[4352,128]{1,0:T(8,128)} custom-call(s32[512]{0:T(512)S(1)} %dynamic_slice.3.owner_ref, s32[512]{0:T(512)S(1)} %convert_reduce_fusion.rank_ref, f32[1536]{0:T(1024)S(1)} %reshape.37.center_ref, f32[3,512,128]{2,1,0:T(8,128)S(1)} %bitcast.17, f32[512,128]{1,0:T(8,128)S(1)} %copy-done.4), custom_call_target="tpu_custom_call" | custom-call | tf_op jit(solution)/shard_map/pack_sources/pallas_call | solution.py:302
  12.6 7.1 %all-to-all-start.1 = ((f32[32,136,128]{2,1,0:T(8,128)}), f32[32,136,128]{2,1,0:T(8,128)S(1)}, u32[]{:S(2)}, u32[]{:S(2)}) async-start(f32[32,136,128]{2,1,0:T(8,128)} %bitcast.8), calls=%async_computation.1 | async-start | bytes 4456448 | tf_op jit(solution)/shard_map/all_to_all | solution.py:318
  19.9 1.3 copy.20.m2l_ref
  21.7 1.0 copy.21
  22.7 1.3 reshape.39.slots_ref
  24.0 6.2 %fusion.1 = f32[80,8,296]{2,0,1:T(8,128)S(1)} fusion(f32[8,296,296]{2,1,0:T(8,128)} %param.17, f32[64,296]{1,0:T(8,128)S(1)} %copy-done.9, f32[16,296]{1,0:T(8,128)S(1)} %collective-permute-done), kind=kOutput, calls=%fused_computation.4 | convolution fusion | flops 672914560 | bytes 3656192 | tf_op jit(solution)/shard_map/pr,oqr->opq/dot_general | solution.py:323
  30.3 3.8 %route_leaves.1 = (f32[512,296]{1,0:T(8,128)S(1)}, f32[1024,384]{1,0:T(8,128)S(1)}) custom-call(s32[512]{0:T(512)S(1)} %get-tuple-element.27.index_ref, s32[512]{0:T(512)S(1)} %get-tuple-element.26.dest_ref, f32[512,296]{1,0:T(8,128)S(1)} %copy.20.m2l_ref, f32[640,296]{1,0:T(8,128)S(1)} %bitcast.14), custom_call_target="tpu_custom_call" | custom-call | tf_op jit(solution)/shard_map/route_leaves/pallas_call | solution.py:325
  34.0 1.1 copy-done
  35.2 0.9 copy-done.2
  36.1 35.4 %all-to-all-done.1 = f32[32,136,128]{2,1,0:T(8,128)S(1)} async-done(((f32[32,136,128]{2,1,0:T(8,128)}), f32[32,136,128]{2,1,0:T(8,128)S(1)}, u32[]{:S(2)}, u32[]{:S(2)}) %all-to-all-start.1) | async-done | bytes 2228256 | tf_op jit(solution)/shard_map/all_to_all | solution.py:318
  71.5 4.3 %all-to-all-start = ((f32[32,32,384]{2,1,0:T(8,128)}), f32[32,32,384]{2,1,0:T(8,128)}, u32[]{:S(2)}, u32[]{:S(2)}) async-start(f32[32,32,384]{2,1,0:T(8,128)} %bitcast.16), calls=%async_computation | async-start | bytes 3145728 | tf_op jit(solution)/shard_map/all_to_all | solution.py:337
  75.8 1.1 copy.22
  76.9 1.4 copy-done.5
  78.3 0.9 copy-done.8
  79.3 84.1 %near_field.1.near_ref = f32[1024,128]{1,0:T(8,128)S(1)} custom-call(s32[8192]{0:T(1024)S(1)} %reshape.39.slots_ref, f32[4352,128]{1,0:T(8,128)S(1)} %bitcast.15, f32[3,1024,128]{2,1,0:T(8,128)S(1)} %bitcast.18, bf16[512,208]{1,0:T(8,128)(2,1)S(1)} %copy-done.8, bf16[512,208]{1,0:T(8,128)(2,1)S(1)} %copy-done.7), custom_call_target="tpu_custom_call" | custom-call | flops 9395240960 | bytes 5000000 | tf_op jit(solution)/shard_map/near_field/pallas_call | solution.py:343
  163.4 1.4 copy-done.6
  164.8 27.4 %far_field.1 = f32[1024,128]{1,0:T(8,128)} custom-call(f32[1024,384]{1,0:T(8,128)} %bitcast.6.dens_ref, f32[3,1024,128]{2,1,0:T(8,128)S(1)} %bitcast.19, f32[1024,128]{1,0:T(8,128)S(1)} %near_field.1.near_ref, s32[8,128]{1,0:T(8,128)S(1)} %compare_convert_fusion.1.live_ref), custom_call_target="tpu_custom_call" | custom-call | flops 10000000000 | bytes 5000000 | tf_op jit(solution)/shard_map/far_field/pallas_call | solution.py:367
  (33 shorter events, 0.6 us)
Async XLA Ops:
  1.4 11.2 %collective-permute-start = (f32[16,296]{1,0:T(8,128)S(1)}, f32[16,296]{1,0:T(8,128)S(1)}, u32[]{:S(2)}, u32[]{:S(2)}) collective-permute-start(f32[16,296]{1,0:T(8,128)S(1)} %slice.3), channel_id=1, source_target_pairs={{0,1},{1,2},{2,3},{3,4},{4,5},{5,6},{6,7},{7,8},{8,9},{9,10},{10,1... | collective-permute-start | bytes 56840 | tf_op jit(solution)/shard_map/ppermute | solution.py:30
  5.5 1.1 copy-start.1
  6.6 0.9 copy-start.4
  12.6 8.6 %copy-start.10 = (s32[16384]{0:T(1024)S(1)}, s32[16384]{0:T(1024)}, u32[]{:S(2)}) copy-start(s32[16384]{0:T(1024)} %param.21) | copy-start | bytes 196612
  12.6 8.6 %copy-start.12 = (s32[512]{0:T(512)S(1)}, s32[512]{0:T(512)}, u32[]{:S(2)}) copy-start(s32[512]{0:T(512)} %param.14) | copy-start | bytes 6148
  12.6 8.6 %copy-start.13 = (s32[512]{0:T(512)S(1)}, s32[512]{0:T(512)}, u32[]{:S(2)}) copy-start(s32[512]{0:T(512)} %param.15) | copy-start | bytes 6148
  12.6 9.1 %copy-start.11 = (s32[1024,8]{0,1:T(8,128)S(1)}, s32[1024,8]{0,1:T(8,128)}, u32[]{:S(2)}) copy-start(s32[1024,8]{0,1:T(8,128)} %param.23) | copy-start | bytes 98308
  12.6 58.9 %all-to-all-start.1 = ((f32[32,136,128]{2,1,0:T(8,128)}), f32[32,136,128]{2,1,0:T(8,128)S(1)}, u32[]{:S(2)}, u32[]{:S(2)}) async-start(f32[32,136,128]{2,1,0:T(8,128)} %bitcast.8), calls=%async_computation.1 | async-start | bytes 4456448 | tf_op jit(solution)/shard_map/all_to_all | solution.py:318
  19.8 4.2 %copy-start.9 = (f32[64,296]{1,0:T(8,128)S(1)}, f32[64,296]{1,0:T(8,128)}, u32[]{:S(2)}) copy-start(f32[64,296]{1,0:T(8,128)} %param.13) | copy-start | bytes 227332
  34.0 1.1 copy-start
  35.2 0.9 copy-start.2
  36.1 39.7 %copy-start.3 = (f32[512,296]{1,0:T(8,128)S(1)}, f32[512,296]{1,0:T(8,128)}, u32[]{:S(2)}) copy-start(f32[512,296]{1,0:T(8,128)} %copy-done.2) | copy-start | bytes 1818628
  71.5 5.4 %copy-start.7 = (bf16[512,208]{1,0:T(8,128)(2,1)S(1)}, bf16[512,208]{1,0:T(8,128)(2,1)}, u32[]{:S(2)}) copy-start(bf16[512,208]{1,0:T(8,128)(2,1)} %constant.25.clone.target_matrix_ref) | copy-start | bytes 638980
  71.5 91.8 %all-to-all-start = ((f32[32,32,384]{2,1,0:T(8,128)}), f32[32,32,384]{2,1,0:T(8,128)}, u32[]{:S(2)}, u32[]{:S(2)}) async-start(f32[32,32,384]{2,1,0:T(8,128)} %bitcast.16), calls=%async_computation | async-start | bytes 3145728 | tf_op jit(solution)/shard_map/all_to_all | solution.py:337
  76.9 1.4 copy-start.5
  78.3 0.9 copy-start.8
  163.4 1.4 copy-start.6
